TPU v7x, 512 devices: a whole 4x8x8 slice. The times are simulated.
512 devices in a mesh: dp: 16 (over y, core), expert: 32 (over x, z).
Axes of the slice: x: 4, y: 8, z: 8, core: 2. Of those that a mesh axis runs over, the one named last changes fastest.
Arguments:
- tokens: bfloat16 [65536, 2048], P(('dp', 'expert')), may hold values from -6 to 6
- grad_out: bfloat16 [65536, 2048], P(('dp', 'expert')), may hold values from -3 to 3
- route_ids: int32 [65536, 2], P(('dp', 'expert')), may hold values from 0 to 31, all different within a row; in each aligned block of 128 rows (0 to 127, 128 to 255, ...) at most 10 rows name the same one
- route_probs: float32 [65536, 2], P(('dp', 'expert')), may hold values from 0.1 to 1
- gate_up: bfloat16 [32, 2, 2048, 768], P('expert', None, 'dp'), may hold values from -0.125 to 0.125
- w_down: bfloat16 [32, 768, 2048], P('expert', None, 'dp'), may hold values from -0.21875 to 0.21875
Outputs:
- input_grad: bfloat16 [65536, 2048], P(('dp', 'expert'))
- prob_grad: bfloat16 [65536, 2], P(('dp', 'expert'))
Inputs may be any that keep to these rules, and one draw needn't show every extreme that they name: `route_ids`: within the rows of one device, no expert is named by more than 10 rows, and in every draw some device names some expert exactly 10 times; the 2 experts of a token differ.
All inputs are finite; a program needn't handle non-finite values.
Results may differ from a plain program's by a relative error of at most 0.0057.
Values may be sent and summed in bfloat16 or wider, within the bound.
No kernel may reach another device: no remote copies, remote signals or barrier semaphores. Data moves between devices by JAX's collectives and lax.ppermute only.
A program may use at most 64 MiB of HBM per device.

v0:
```python
import jax
import jax.numpy as jnp
from jax import lax
from jax.sharding import PartitionSpec as P


def expert_block(rows_in, rows_grad, gate_up, w_down):
    gate_pre = jnp.dot(rows_in, gate_up[0], preferred_element_type=jnp.float32)
    up_value = jnp.dot(rows_in, gate_up[1], preferred_element_type=jnp.float32)
    sigmoid_gate = jax.nn.sigmoid(gate_pre)
    activated = gate_pre * sigmoid_gate
    hidden = (activated * up_value).astype(jnp.bfloat16)
    expert_out = jnp.dot(hidden, w_down, preferred_element_type=jnp.float32)
    prob_grad = jnp.sum(rows_grad.astype(jnp.float32) * expert_out, axis=-1).astype(jnp.bfloat16)
    last_dims = (((1,), (1,)), ((), ()))
    hidden_grad = lax.dot_general(rows_grad, w_down, last_dims, preferred_element_type=jnp.float32)
    gate_grad = (
        hidden_grad * up_value * sigmoid_gate * (1.0 + gate_pre * (1.0 - sigmoid_gate))
    ).astype(jnp.bfloat16)
    up_grad = (hidden_grad * activated).astype(jnp.bfloat16)
    row_grad = lax.dot_general(gate_grad, gate_up[0], last_dims, preferred_element_type=jnp.float32)
    row_grad = row_grad + lax.dot_general(
        up_grad, gate_up[1], last_dims, preferred_element_type=jnp.float32
    )
    return (row_grad.astype(jnp.bfloat16), prob_grad)


def rows_work(rows_in, rows_grad, rows_live, gate_up, w_down):
    keep_rows = rows_live > 0
    row_grad, prob_grad = expert_block(rows_in, rows_grad, gate_up, w_down)
    row_grad = jnp.where(keep_rows[:, None], row_grad, jnp.zeros_like(row_grad))
    prob_grad = jnp.where(keep_rows, prob_grad, jnp.zeros_like(prob_grad))
    return (row_grad, prob_grad)


def shards(tokens, grad_out, route_ids, route_probs, gate_up, w_down):
    tok_rows, features = tokens.shape
    top_count = route_ids.shape[1]
    experts = lax.axis_size("expert")
    capacity = 5 * tok_rows * top_count // (4 * experts)
    full_gate_up, full_down = (
        lax.all_gather(gate_up, "dp", axis=2, tiled=True),
        lax.all_gather(w_down, "dp", axis=2, tiled=True),
    )
    full_gate_up = full_gate_up[0]
    full_down = full_down[0]
    pair_count = tok_rows * top_count
    flat_ids = route_ids.reshape(-1)
    one_hot = (flat_ids[:, None] == jnp.arange(experts, dtype=jnp.int32)[None, :]).astype(jnp.int32)
    before = jnp.cumsum(one_hot, axis=0) - one_hot
    slot_rank = jnp.sum(before * one_hot, axis=1)
    slot_index = flat_ids * capacity + slot_rank
    filler = (
        jnp.full((experts * capacity,), pair_count, jnp.int32)
        .at[slot_index]
        .set(jnp.arange(pair_count, dtype=jnp.int32))
    )
    filled = filler < pair_count
    source = jnp.minimum(filler, pair_count - 1) // top_count
    zero_row = jnp.zeros((), jnp.bfloat16)
    send_rows = jnp.where(filled[:, None], jnp.take(tokens, source, axis=0), zero_row).reshape(
        experts, capacity, features
    )
    send_grads = jnp.where(filled[:, None], jnp.take(grad_out, source, axis=0), zero_row).reshape(
        experts, capacity, features
    )
    live_mark = filled.astype(jnp.bfloat16).reshape(experts, capacity)
    rows_in = lax.all_to_all(send_rows, "expert", split_axis=0, concat_axis=0, tiled=True)
    rows_grad = lax.all_to_all(send_grads, "expert", split_axis=0, concat_axis=0, tiled=True)
    rows_live = lax.all_to_all(live_mark, "expert", split_axis=0, concat_axis=0, tiled=True)
    source_count, item_count = rows_live.shape
    row_grad, prob_grad = rows_work(
        rows_in.reshape(-1, features),
        rows_grad.reshape(-1, features),
        rows_live.reshape(-1),
        full_gate_up,
        full_down,
    )
    row_grad = row_grad.reshape(source_count, item_count, features)
    prob_grad = prob_grad.reshape(source_count, item_count)
    row_back = lax.all_to_all(row_grad, "expert", split_axis=0, concat_axis=0, tiled=True)
    prob_back = lax.all_to_all(prob_grad, "expert", split_axis=0, concat_axis=0, tiled=True)
    pair_grads = jnp.take(row_back.reshape(experts * capacity, features), slot_index, axis=0)
    pair_probs = jnp.take(prob_back.reshape(-1), slot_index, axis=0)
    weighted = route_probs.reshape(-1)[:, None] * pair_grads.astype(jnp.float32)
    input_grad = jnp.sum(weighted.reshape(tok_rows, top_count, features), axis=1).astype(
        jnp.bfloat16
    )
    return (input_grad, pair_probs.reshape(tok_rows, top_count))


def solution(mesh):
    return jax.shard_map(
        shards,
        mesh=mesh,
        in_specs=(
            P(("dp", "expert"), None),
            P(("dp", "expert"), None),
            P(("dp", "expert"), None),
            P(("dp", "expert"), None),
            P("expert", None, "dp", None),
            P("expert", None, "dp"),
        ),
        out_specs=(P(("dp", "expert"), None), P(("dp", "expert"), None)),
        check_vma=False,
    )
```

profile of v0, /device:TPU:24, one launch (start us, length us, event | category | flops | bytes accessed | tf_op | source)
XLA Modules:
  0.0 256.5 jit_solution(14992742776180642031)
XLA Ops:
  7.2 0.7 all-gather.3.cloned.1.call-update
  8.0 0.7 all-gather.5.cloned.1.call-update
  8.7 0.8 copy.17
  9.4 0.1 eq.26
  9.6 0.1 reshape.136
  9.7 0.6 reduce-window.6
  10.3 0.2 slice_reduce_fusion
  10.6 0.1 mul.60
  10.8 1.4 scatter_custom_fusion
  12.3 2.4 gather_fusion.2
  14.8 3.0 %gather_fusion.3 = bf16[320,2048]{1,0:T(8,128)(2,1)} fusion(bf16[128,2048]{1,0:T(8,128)(2,1)S(1)} %copy-done.1, s32[1024]{0:T(1024)S(1)} %pad_clamp_fusion.1), kind=kCustom, calls=%fused_computation.1.clone | custom fusion | bytes 2622720 | tf_op jit(solution)/shard_map/jit(_take)/gather | solution.py:61
  17.8 2.8 %select_select_fusion.1 = (bf16[320,2048]{1,0:T(8,128)(2,1)}, bf16[320,2048]{1,0:T(8,128)(2,1)S(1)}) fusion(bf16[320,2048]{1,0:T(8,128)(2,1)S(1)} %gather_fusion.2, pred[320]{0:T(512)(128)(4,1)S(1)} %get-tuple-element.15, pred[320]{0:T(512)(128)(4,1)S(1)} %get-tuple-element.12, bf16[320,2048]{1,0:T(8,128)(2,1)} %gather_fusion.3), kind=kLoop, calls=%fused_computation.22 | loop fusion | flops 2621440 | bytes 5243520 | tf_op jit(solution)/shard_map/jit(_where)/select_n | solution.py:64
  20.6 1.6 reshape.140
  22.2 13.2 %all-to-all-start.2 = ((bf16[32,10,2048]{2,1,0:T(8,128)(2,1)}), bf16[32,10,2048]{2,1,0:T(8,128)(2,1)S(1)}, u32[]{:S(2)}, u32[]{:S(2)}) async-start(bf16[32,10,2048]{2,1,0:T(8,128)(2,1)} %reshape.140), calls=%async_computation.2 | async-start | bytes 4194304 | tf_op jit(solution)/shard_map/all_to_all | solution.py:68
  35.4 3.3 %reshape.138 = bf16[32,10,2048]{2,1,0:T(8,128)(2,1)} reshape(bf16[320,2048]{1,0:T(8,128)(2,1)} %get-tuple-element.17) | data formatting | bytes 2621440 | tf_op jit(solution)/shard_map/reshape | solution.py:64
  38.7 46.7 %all-to-all-done.2 = bf16[32,10,2048]{2,1,0:T(8,128)(2,1)S(1)} async-done(((bf16[32,10,2048]{2,1,0:T(8,128)(2,1)}), bf16[32,10,2048]{2,1,0:T(8,128)(2,1)S(1)}, u32[]{:S(2)}, u32[]{:S(2)}) %all-to-all-start.2) | async-done | bytes 1310752 | tf_op jit(solution)/shard_map/all_to_all | solution.py:68
  85.4 6.3 %all-to-all-start.1 = ((bf16[32,10,2048]{2,1,0:T(8,128)(2,1)}), bf16[32,10,2048]{2,1,0:T(8,128)(2,1)}, u32[]{:S(2)}, u32[]{:S(2)}) async-start(bf16[32,10,2048]{2,1,0:T(8,128)(2,1)} %reshape.138), calls=%async_computation.1 | async-start | bytes 4194304 | tf_op jit(solution)/shard_map/all_to_all | solution.py:69
  91.7 0.7 reshape.192
  92.4 1.3 reshape.141
  93.8 47.7 %all-to-all-done.1 = bf16[32,10,2048]{2,1,0:T(8,128)(2,1)} async-done(((bf16[32,10,2048]{2,1,0:T(8,128)(2,1)}), bf16[32,10,2048]{2,1,0:T(8,128)(2,1)}, u32[]{:S(2)}, u32[]{:S(2)}) %all-to-all-start.1) | async-done | bytes 1310752 | tf_op jit(solution)/shard_map/all_to_all | solution.py:69
  141.5 6.1 %all-to-all-start = ((bf16[32,1,10]{2,1,0:T(2,128)(2,1)}), bf16[32,1,10]{2,1,0:T(2,128)(2,1)S(1)}, u32[]{:S(2)}, u32[]{:S(2)}) async-start(bf16[32,1,10]{2,1,0:T(2,128)(2,1)} %reshape.192), calls=%async_computation | async-start | bytes 32768 | tf_op jit(solution)/shard_map/all_to_all | solution.py:70
  147.6 2.5 reshape.139
  150.2 4.1 %fusion.2 = f32[320,768]{1,0:T(8,128)} fusion(bf16[320,2048]{1,0:T(8,128)(2,1)S(1)} %reshape.139, bf16[1,768,2048]{2,1,0:T(8,128)(2,1)} %all-gather.3.cloned.1.call-done), kind=kOutput, calls=%fused_computation.9 | convolution fusion | flops 1006632960 | bytes 5439488 | tf_op jit(solution)/shard_map/dot_general | solution.py:16
  154.3 3.2 %fusion.7 = f32[320,768]{1,0:T(8,128)S(1)} fusion(bf16[320,2048]{1,0:T(8,128)(2,1)S(1)} %copy-done.2, bf16[1,2,2048,768]{3,2,1,0:T(8,128)(2,1)} %all-gather.5.cloned.1.call-done), kind=kOutput, calls=%fused_computation.13 | convolution fusion | flops 1006632960 | bytes 5439488 | tf_op jit(solution)/shard_map/dot_general | solution.py:9
  157.5 0.5 copy-done.4
  158.0 1.2 fusion.9
  159.3 0.9 copy-done.8
  160.2 0.2 copy-done.5
  160.4 1.4 fusion.12
  161.8 0.1 convert_element_type.54
  162.1 0.6 copy.23
  162.7 10.0 %all-to-all-start.4 = ((bf16[32,1,10]{2,1,0:T(2,128)(2,1)}), bf16[32,1,10]{2,1,0:T(2,128)(2,1)S(1)}, u32[]{:S(2)}, u32[]{:S(2)}) async-start(bf16[32,1,10]{2,1,0:T(2,128)(2,1)} %copy.23), calls=%async_computation.4 | async-start | bytes 32768 | tf_op jit(solution)/shard_map/all_to_all | solution.py:82
  172.7 4.0 %fusion.8 = f32[320,2048]{1,0:T(8,128)S(1)} fusion(bf16[1,2,2048,768]{3,2,1,0:T(8,128)(2,1)} %all-gather.5.cloned.1.call-done, f32[320,768]{1,0:T(8,128)} %copy-done.8, f32[320,768]{1,0:T(8,128)S(1)} %copy-done.6, f32[320,768]{1,0:T(8,128)} %copy-done.10), kind=kOutput, calls=%fused_computation.14 | convolution fusion | flops 1009090560 | bytes 8716288 | tf_op jit(solution)/shard_map/dot_general | solution.py:21
  176.7 3.1 %fusion.11 = bf16[320,2048]{1,0:T(8,128)(2,1)S(1)} fusion(f32[320,2048]{1,0:T(8,128)S(1)} %fusion.8, bf16[1,2,2048,768]{3,2,1,0:T(8,128)(2,1)} %all-gather.5.cloned.1.call-done, pred[320]{0:T(512)(128)(4,1)S(1)} %gt.13, f32[320,768]{1,0:T(8,128)S(1)} %copy-done.7, f32[320,768]{1,0:T(8,128)S(1)} %copy-done.9), kind=kOutput, calls=%fused_computation.17 | convolution fusion | flops 1010073600 | bytes 9044288 | tf_op jit(solution)/shard_map/dot_general | solution.py:22
  179.8 1.5 reshape.142
  181.3 0.8 all-to-all-done.4
  182.2 9.0 %all-to-all-start.3 = ((bf16[32,10,2048]{2,1,0:T(8,128)(2,1)}), bf16[32,10,2048]{2,1,0:T(8,128)(2,1)}, u32[]{:S(2)}, u32[]{:S(2)}) async-start(bf16[32,10,2048]{2,1,0:T(8,128)(2,1)} %reshape.142), calls=%async_computation.3 | async-start | bytes 4194304 | tf_op jit(solution)/shard_map/all_to_all | solution.py:81
  191.2 0.1 reduce_sum.32
  191.4 0.1 copy.16
  191.6 0.1 reshape.144
  191.7 1.9 gather_fusion.1
  193.6 0.2 gather.18
  193.8 0.6 copy.24
  194.4 45.7 %all-to-all-done.3 = bf16[32,10,2048]{2,1,0:T(8,128)(2,1)} async-done(((bf16[32,10,2048]{2,1,0:T(8,128)(2,1)}), bf16[32,10,2048]{2,1,0:T(8,128)(2,1)}, u32[]{:S(2)}, u32[]{:S(2)}) %all-to-all-start.3) | async-done | bytes 1310752 | tf_op jit(solution)/shard_map/all_to_all | solution.py:81
  240.1 2.5 reshape.143
  242.6 1.4 gather_fusion
  244.0 0.7 gather.16
  244.7 4.9 %multiply_reduce_fusion = bf16[128,2048]{1,0:T(8,128)(2,1)} fusion(bf16[128,2,2048]{2,1,0:T(2,128)(2,1)S(1)} %gather.16, pred[128,2]{1,0:T(8,128)(4,1)S(1)} %get-tuple-element.8, f32[128,2]{1,0:T(8,128)S(1)} %copy.16), kind=kLoop, calls=%fused_computation.18 | loop fusion | flops 1835008 | bytes 1574144 | tf_op jit(solution)/shard_map/reduce_sum | solution.py:86
  (38 shorter events, 0.5 us)
Async XLA Ops:
  7.2 5.1 %copy-start = (bf16[128,2048]{1,0:T(8,128)(2,1)S(1)}, bf16[128,2048]{1,0:T(8,128)(2,1)}, u32[]{:S(2)}) copy-start(bf16[128,2048]{1,0:T(8,128)(2,1)} %param.9) | copy-start | bytes 1572868
  7.2 143.0 %all-gather.3.cloned.1.call-start = ((), (), s32[]{:S(2)}) async-start(), calls=%async_computation.5 | async-start | bytes 3342336 | tf_op jit(solution)/shard_map/all_gather | solution.py:43
  7.9 146.4 %all-gather.5.cloned.1.call-start = ((), (), s32[]{:S(2)}) async-start(), calls=%async_computation.6 | async-start | bytes 6684672 | tf_op jit(solution)/shard_map/all_gather | solution.py:42
  12.3 2.5 copy-start.1
  22.2 63.2 %all-to-all-start.2 = ((bf16[32,10,2048]{2,1,0:T(8,128)(2,1)}), bf16[32,10,2048]{2,1,0:T(8,128)(2,1)S(1)}, u32[]{:S(2)}, u32[]{:S(2)}) async-start(bf16[32,10,2048]{2,1,0:T(8,128)(2,1)} %reshape.140), calls=%async_computation.2 | async-start | bytes 4194304 | tf_op jit(solution)/shard_map/all_to_all | solution.py:68
  85.4 56.0 %all-to-all-start.1 = ((bf16[32,10,2048]{2,1,0:T(8,128)(2,1)}), bf16[32,10,2048]{2,1,0:T(8,128)(2,1)}, u32[]{:S(2)}, u32[]{:S(2)}) async-start(bf16[32,10,2048]{2,1,0:T(8,128)(2,1)} %reshape.138), calls=%async_computation.1 | async-start | bytes 4194304 | tf_op jit(solution)/shard_map/all_to_all | solution.py:69
  141.5 20.5 %all-to-all-start = ((bf16[32,1,10]{2,1,0:T(2,128)(2,1)}), bf16[32,1,10]{2,1,0:T(2,128)(2,1)S(1)}, u32[]{:S(2)}, u32[]{:S(2)}) async-start(bf16[32,1,10]{2,1,0:T(2,128)(2,1)} %reshape.192), calls=%async_computation | async-start | bytes 32768 | tf_op jit(solution)/shard_map/all_to_all | solution.py:70
  150.1 4.2 %copy-start.2 = (bf16[320,2048]{1,0:T(8,128)(2,1)S(1)}, bf16[320,2048]{1,0:T(8,128)(2,1)}, u32[]{:S(2)}) copy-start(bf16[320,2048]{1,0:T(8,128)(2,1)} %reshape.141) | copy-start | bytes 3932164
  154.3 3.7 %copy-start.4 = (bf16[1,2,2048,768]{3,2,1,0:T(8,128)(2,1)S(1)}, bf16[1,2,2048,768]{3,2,1,0:T(8,128)(2,1)}, u32[]{:S(2)}) copy-start(bf16[1,2,2048,768]{3,2,1,0:T(8,128)(2,1)} %all-gather.5.cloned.1.call-done) | copy-start | bytes 18874372
  158.0 1.2 copy-start.10
  158.0 2.4 copy-start.5
  159.3 1.0 copy-start.8
  160.4 12.2 %copy-start.6 = (f32[320,768]{1,0:T(8,128)S(1)}, f32[320,768]{1,0:T(8,128)}, u32[]{:S(2)}) copy-start(f32[320,768]{1,0:T(8,128)} %fusion.2) | copy-start | bytes 2949124
  162.7 19.5 %all-to-all-start.4 = ((bf16[32,1,10]{2,1,0:T(2,128)(2,1)}), bf16[32,1,10]{2,1,0:T(2,128)(2,1)S(1)}, u32[]{:S(2)}, u32[]{:S(2)}) async-start(bf16[32,1,10]{2,1,0:T(2,128)(2,1)} %copy.23), calls=%async_computation.4 | async-start | bytes 32768 | tf_op jit(solution)/shard_map/all_to_all | solution.py:82
  172.7 4.0 %copy-start.7 = (f32[320,768]{1,0:T(8,128)S(1)}, f32[320,768]{1,0:T(8,128)}, u32[]{:S(2)}) copy-start(f32[320,768]{1,0:T(8,128)} %fusion.2) | copy-start | bytes 2949124
  172.7 4.0 %copy-start.9 = (f32[320,768]{1,0:T(8,128)S(1)}, f32[320,768]{1,0:T(8,128)}, u32[]{:S(2)}) copy-start(f32[320,768]{1,0:T(8,128)} %copy-done.8) | copy-start | bytes 2949124
  181.3 10.0 %copy-start.3 = (f32[128,2]{0,1:T(2,128)S(1)}, f32[128,2]{0,1:T(2,128)}, u32[]{:S(2)}) copy-start(f32[128,2]{0,1:T(2,128)} %param.11) | copy-start | bytes 3076
  182.2 57.9 %all-to-all-start.3 = ((bf16[32,10,2048]{2,1,0:T(8,128)(2,1)}), bf16[32,10,2048]{2,1,0:T(8,128)(2,1)}, u32[]{:S(2)}, u32[]{:S(2)}) async-start(bf16[32,10,2048]{2,1,0:T(8,128)(2,1)} %reshape.142), calls=%async_computation.3 | async-start | bytes 4194304 | tf_op jit(solution)/shard_map/all_to_all | solution.py:81
Sparse Core Ops, SparseCore 0:
  10.1 50.8 all-gather.2
  63.0 48.3 all-gather.4
where the time goes:
time: 257 us; the launch traced here: 256 us
  waiting for transfers between devices  142 us (55%)
  starting transfers between devices  44.6 us (17%)
  local copies, waits for them, and re-layouts  29.5 us (11%)
  matrix products  17 us (7%)
  between operations  14.4 us (6%)
  other arithmetic  8.58 us (3%)
    all_to_all x1, waiting for transfers between devices, shards(): lax.all_to_all(send_grads, 'expert', split_axis=0, concat_axis=0, tiled=T...  47.7 us
    all_to_all x1, waiting for transfers between devices, shards(): lax.all_to_all(send_rows, 'expert', split_axis=0, concat_axis=0, tiled=True)  46.7 us
    all_to_all x1, waiting for transfers between devices, shards(): lax.all_to_all(row_grad, 'expert', split_axis=0, concat_axis=0, tiled=True)  45.7 us
    all_to_all x1, starting transfers between devices, shards(): lax.all_to_all(send_rows, 'expert', split_axis=0, concat_axis=0, tiled=True)  13.2 us
    all_to_all x1, starting transfers between devices, shards(): lax.all_to_all(prob_grad, 'expert', split_axis=0, concat_axis=0, tiled=True)  9.96 us
    all_to_all x1, starting transfers between devices, shards(): lax.all_to_all(row_grad, 'expert', split_axis=0, concat_axis=0, tiled=True)  9.04 us
    all_to_all x1, starting transfers between devices, shards(): lax.all_to_all(send_grads, 'expert', split_axis=0, concat_axis=0, tiled=T...  6.26 us
    all_to_all x1, starting transfers between devices, shards(): lax.all_to_all(live_mark, 'expert', split_axis=0, concat_axis=0, tiled=True)  6.13 us
  transfers between devices with their start and end apart: 7, of which 4 were waited for; matrix products, arithmetic and copies ran while one was open for 17% of the time, Pallas kernels for 0%

commit v1 on v0

v1 whole, which is shorter than its diff:
```python
import functools

import jax
import jax.numpy as jnp
from jax import lax
from jax.experimental import pallas as pl
from jax.experimental.pallas import tpu as pltpu
from jax.sharding import PartitionSpec as P

BF = jnp.bfloat16
F32 = jnp.float32
I32 = jnp.int32


def iota(shape, dim):
    return lax.broadcasted_iota(I32, shape, dim)


def row_quarter(j):
    return jnp.where(j < 32, j >> 3, (j - 32) >> 1)


def row_slot(j):
    return jnp.where(j < 32, j & 7, 8 + (j & 1))


def dot(a, b):
    return jnp.dot(a, b, preferred_element_type=F32)


def dot_nt(a, b):
    return lax.dot_general(a, b, (((1,), (1,)), ((), ())), preferred_element_type=F32)


def onehot(cond):
    return jnp.where(cond, 1.0, 0.0).astype(BF)


def ranks(ids, experts):
    toks = ids.shape[1]
    e = iota((experts, toks), 0)
    m0, m1 = e == ids[0:1, :], e == ids[1:2, :]
    o0, o1 = jnp.where(m0, 1.0, 0.0), jnp.where(m1, 1.0, 0.0)
    earlier = onehot(iota((toks, toks), 0) < iota((toks, toks), 1))
    r0 = dot(o0.astype(BF), earlier)
    r1 = dot(o1.astype(BF), earlier) + jnp.sum(o0, axis=1, keepdims=True)
    return jnp.where(m0, r0, -1.0), jnp.where(m1, r1, -1.0)


def weights_kernel(gu_ref, wd_ref, out_ref):
    out_ref[0:2] = gu_ref[0]
    eye = onehot(iota((128, 128), 0) == iota((128, 128), 1))
    out_ref[2] = dot_nt(eye, wd_ref[0]).astype(BF)


def pack_kernel(ids_ref, tok_ref, grad_ref, out_ref):
    experts = out_ref.shape[0]
    k0, k1 = ranks(ids_ref[...], experts)
    slot = jnp.maximum(k0, k1).astype(BF)
    quarters = lambda ref: jnp.concatenate([ref[:, q * 512 : (q + 1) * 512] for q in range(4)], axis=0)
    toks, grads = quarters(tok_ref), quarters(grad_ref)
    step = 8
    rows = step * 40
    row = iota((rows, 128), 0)
    j = row % 40
    want_slot = row_slot(j).astype(F32)
    want_q = row_quarter(j)
    local = iota((rows, experts), 0) // 40
    for b in range(experts // step):
        spread = onehot(local + b * step == iota((rows, experts), 1))
        hit = jnp.where(dot(spread, slot) == want_slot, 1.0, 0.0)
        pick = jnp.concatenate([jnp.where(want_q == q, hit, 0.0).astype(BF) for q in range(4)], axis=1)
        t = dot(pick, toks).reshape(step, 40, 512)
        g = dot(pick, grads).reshape(step, 40, 512)
        both = jnp.concatenate([t[:, :32], g[:, :32], t[:, 32:], g[:, 32:]], axis=1)
        out_ref[b * step : (b + 1) * step] = both.astype(BF)


def expert_kernel(x_ref, w_ref, out_ref, prob_ref, w, xs, gs, gg, ug, sems):
    sources = x_ref.shape[0]
    main, extra = sources * 8, sources * 2
    copies = [
        [
            pltpu.make_async_copy(
                w_ref.at[:, i, :, pl.ds(n * 256, 256)], w.at[i, :, :, pl.ds(n * 256, 256)], sems.at[n, i]
            )
            for i in range(3)
        ]
        for n in range(3)
    ]
    for group in copies:
        for c in group:
            c.start()
    tail = x_ref[:, 64:80, :].reshape(sources * 16, 512)
    src = iota((sources * 16, sources * 16), 1)
    dst = iota((sources * 16, sources * 16), 0)
    part, rest = dst // extra, dst % extra
    perm = onehot(src == (rest >> 1) * 16 + part * 2 + (rest & 1))
    tail = dot(perm, tail).astype(BF)
    for p in range(8):
        to = xs if p < 4 else gs
        cols = slice((p % 4) * 512, (p % 4 + 1) * 512)
        body = x_ref[:, p * 8 : (p + 1) * 8, :].astype(F32).reshape(main, 512)
        to[0:main, cols] = body.astype(BF)
        to[main : main + extra, cols] = tail[p * extra : (p + 1) * extra]
    prob = jnp.zeros((main + extra, 1), F32)
    for n in range(3):
        for c in copies[n]:
            c.wait()
        cols = slice(n * 256, (n + 1) * 256)
        gate_pre = dot(xs[...], w[0, :, :, cols].reshape(2048, 256))
        up_value = dot(xs[...], w[1, :, :, cols].reshape(2048, 256))
        hidden_grad = dot(gs[...], w[2, :, :, cols].reshape(2048, 256))
        sig = jax.nn.sigmoid(gate_pre)
        act = gate_pre * sig
        hidden = (act * up_value).astype(BF).astype(F32)
        prob = prob + jnp.sum(hidden * hidden_grad, axis=1, keepdims=True)
        gg[:, cols] = (hidden_grad * up_value * sig * (1.0 + gate_pre * (1.0 - sig))).astype(BF)
        ug[:, cols] = (hidden_grad * act).astype(BF)
    rows = main + extra
    row = iota((rows, 128), 0)
    lane = iota((rows, 128), 1)
    source = jnp.where(row < main, row >> 3, (row - main) >> 1)
    slot = jnp.where(row < main, row & 7, 8 + (row & 1))
    placed = jnp.where(lane == (source & 7) * 16 + slot, jnp.broadcast_to(prob, (rows, 128)), 0.0).astype(BF)
    row8 = iota((8, rows), 1)
    group = jnp.where(row8 < main, row8 >> 6, (row8 - main) >> 4)
    prob_ref[...] = dot(onehot(group == iota((8, rows), 0)), placed).astype(BF)
    tails = []
    for q in range(4):
        feats = slice(q * 4, (q + 1) * 4)
        row_grad = dot_nt(gg[...], w[0, feats].reshape(512, 768)) + dot_nt(ug[...], w[1, feats].reshape(512, 768))
        row_grad = row_grad.astype(BF)
        tails.append(row_grad[main:])
        xs[0:main, q * 512 : (q + 1) * 512] = row_grad[:main]
    tail = jnp.concatenate(tails, axis=0)
    dst = iota((4 * extra, 4 * extra), 0)
    src = iota((4 * extra, 4 * extra), 1)
    perm = onehot(src == ((dst >> 1) & 3) * extra + (dst >> 3) * 2 + (dst & 1))
    tail = dot(perm, tail).reshape(sources, 8, 512)
    body = [xs[0:main, q * 512 : (q + 1) * 512].astype(F32).reshape(sources, 8, 512) for q in range(4)]
    out_ref[...] = jnp.concatenate(body + [tail], axis=1).astype(BF)


def combine_kernel(ids_ref, ids_t_ref, p_ref, back_ref, prob_ref, out_ref, prob_out_ref):
    experts, per, width = back_ref.shape
    toks = p_ref.shape[0]
    k0, k1 = ranks(ids_ref[...], experts)
    for k, slots in enumerate((k0, k1)):
        acc = jnp.zeros((experts, toks), F32)
        for r in range(10):
            acc = acc + jnp.where(slots == r, jnp.broadcast_to(prob_ref[:, r : r + 1].astype(F32), (experts, toks)), 0.0)
        prob_out_ref[k : k + 1, :] = jnp.sum(acc, axis=0, keepdims=True).astype(BF)
    ids_t = ids_t_ref[...]
    e = iota((toks, experts), 1)
    m0, m1 = e == ids_t[:, 0:1], e == ids_t[:, 1:2]
    o0, o1 = jnp.where(m0, 1.0, 0.0), jnp.where(m1, 1.0, 0.0)
    earlier = onehot(iota((toks, toks), 1) < iota((toks, toks), 0))
    r0 = dot(earlier, o0.astype(BF))
    r1 = dot(earlier, o1.astype(BF)) + jnp.sum(o0, axis=0, keepdims=True)
    slot = jnp.concatenate([jnp.where(m0, r0, -1.0), jnp.where(m1, r1, -1.0)], axis=0).astype(BF)
    lanes = experts * per
    spread = onehot(iota((experts, lanes), 1) // per == iota((experts, lanes), 0))
    j = iota((1, lanes), 1) % per
    hit = jnp.where(dot(slot, spread) == row_slot(j).astype(F32), 1.0, 0.0)
    want_q = row_quarter(j)
    back = back_ref[...].astype(F32).reshape(lanes, width).astype(BF)
    p0, p1 = p_ref[:, 0:1], p_ref[:, 1:2]
    for q in range(4):
        rows = dot(jnp.where(want_q == q, hit, 0.0).astype(BF), back)
        out_ref[:, q * width : (q + 1) * width] = (p0 * rows[:toks] + p1 * rows[toks:]).astype(BF)


def params():
    return pltpu.CompilerParams(vmem_limit_bytes=56 * 1024 * 1024)


def cost(flops, size):
    return pl.CostEstimate(flops=flops, bytes_accessed=size, transcendentals=0)


def shards(tokens, grad_out, route_ids, route_probs, gate_up, w_down):
    toks, features = tokens.shape
    experts = lax.axis_size("expert")
    n_dp = lax.axis_size("dp")
    ids = route_ids.T
    own_w = pl.pallas_call(
        weights_kernel,
        out_shape=jax.ShapeDtypeStruct((3, 128, 768), BF),
        compiler_params=params(),
        cost_estimate=cost(10**8, 1200000),
        name="join_weights",
    )(gate_up, w_down)
    full_w = lax.all_gather(own_w, "dp", axis=0, tiled=False)
    send = pl.pallas_call(
        pack_kernel,
        out_shape=jax.ShapeDtypeStruct((experts, 80, 512), BF),
        compiler_params=params(),
        cost_estimate=cost(3 * 10**9, 4000000),
        name="pack_rows",
    )(ids, tokens, grad_out)
    rows = lax.all_to_all(send, "expert", split_axis=0, concat_axis=0, tiled=True)
    back, prob = pl.pallas_call(
        expert_kernel,
        in_specs=[pl.BlockSpec(memory_space=pltpu.VMEM), pl.BlockSpec(memory_space=pl.ANY)],
        out_shape=(jax.ShapeDtypeStruct((experts, 40, 512), BF), jax.ShapeDtypeStruct((8, 128), BF)),
        scratch_shapes=[
            pltpu.VMEM((3, n_dp, 128, 768), BF),
            pltpu.VMEM((experts * 10, features), BF),
            pltpu.VMEM((experts * 10, features), BF),
            pltpu.VMEM((experts * 10, 768), BF),
            pltpu.VMEM((experts * 10, 768), BF),
            pltpu.SemaphoreType.DMA((3, 3)),
        ],
        compiler_params=params(),
        cost_estimate=cost(6 * 10**9, 14000000),
        name="expert_rows",
    )(rows, full_w)
    probs = lax.all_gather(prob, "expert", axis=0, tiled=False)
    back = lax.all_to_all(back, "expert", split_axis=0, concat_axis=0, tiled=True)
    own = lax.axis_index("expert")
    own_prob = lax.dynamic_slice(probs, (0, own // 8, (own % 8) * 16), (experts, 1, 16))[:, 0]
    input_grad, prob_grad = pl.pallas_call(
        combine_kernel,
        out_shape=(jax.ShapeDtypeStruct((toks, features), BF), jax.ShapeDtypeStruct((2, toks), BF)),
        compiler_params=params(),
        cost_estimate=cost(2 * 10**9, 2000000),
        name="combine_rows",
    )(ids, route_ids, route_probs, back, own_prob)
    return input_grad, prob_grad.T


def solution(mesh):
    return jax.shard_map(
        shards,
        mesh=mesh,
        in_specs=(
            P(("dp", "expert"), None),
            P(("dp", "expert"), None),
            P(("dp", "expert"), None),
            P(("dp", "expert"), None),
            P("expert", None, "dp", None),
            P("expert", None, "dp"),
        ),
        out_specs=(P(("dp", "expert"), None), P(("dp", "expert"), None)),
        check_vma=False,
    )
```

time: 257 us -> 193 us (0.75)
  the two profiles are of different devices: /device:TPU:24 before, /device:TPU:40 now
where the time goes in v1:
time: 193 us
  blocking collectives  146 us (76%)
  Pallas kernels  23.3 us (12%)
  between operations  14.1 us (7%)
  starting transfers between devices  5.79 us (3%)
  local copies, waits for them, and re-layouts  3.28 us (2%)
    all_to_all x1, blocking collectives, shards(): lax.all_to_all(send, 'expert', split_axis=0, concat_axis=0, tiled=True)  75.1 us
    all_gather x1, blocking collectives, shards(): probs = lax.all_gather(prob, 'expert', axis=0, tiled=False)  71.2 us
    pallas_call x1, Pallas kernels, shards(): pl.pallas_call(expert_kernel, in_specs=[pl.BlockSpec(memory_space=pltpu.V...  12.2 us
    all_to_all x1, starting transfers between devices, shards(): lax.all_to_all(back, 'expert', split_axis=0, concat_axis=0, tiled=True)  5.75 us
    pallas_call x1, Pallas kernels, shards(): pl.pallas_call(pack_kernel, out_shape=jax.ShapeDtypeStruct((experts, 80,...  4.98 us
    pallas_call x1, Pallas kernels, shards(): pl.pallas_call(combine_kernel, out_shape=(jax.ShapeDtypeStruct((toks, fea...  4.06 us
  transfers between devices with their start and end apart: 2, of which 0 were waited for; matrix products, arithmetic and copies ran while one was open for 1% of the time, Pallas kernels for 3%

profile of v1, /device:TPU:40, one launch (start us, length us, event | category | flops | bytes accessed | tf_op | source)
XLA Modules:
  0.0 192.7 jit_solution(11899544230312923916)
XLA Ops:
  7.2 0.0 all-gather.4.cloned.1.call-start
  7.2 2.1 %join_weights.1 = bf16[3,128,768]{2,1,0:T(8,128)(2,1)} custom-call(bf16[1,2,128,768]{3,2,1,0:T(8,128)(2,1)} %gu_ref.1, bf16[1,768,128]{2,1,0:T(8,128)(2,1)} %wd_ref.1), custom_call_target="tpu_custom_call" | custom-call | flops 100000000 | bytes 1200000 | tf_op jit(solution)/shard_map/join_weights/pallas_call | solution.py:187
  9.3 0.0 all-gather.4.cloned.1.call-update
  9.3 5.0 %pack_rows.1 = bf16[32,80,512]{2,1,0:T(8,128)(2,1)} custom-call(s32[2,128]{1,0:T(2,128)} %bitcast.9, bf16[128,2048]{1,0:T(8,128)(2,1)} %tok_ref.1, bf16[128,2048]{1,0:T(8,128)(2,1)} %grad_ref.1), custom_call_target="tpu_custom_call" | custom-call | flops 3000000000 | bytes 4000000 | tf_op jit(solution)/shard_map/pack_rows/pallas_call | solution.py:195
  14.3 75.1 %all_to_all.10.x_ref = bf16[32,80,512]{2,1,0:T(8,128)(2,1)} all-to-all(bf16[32,80,512]{2,1,0:T(8,128)(2,1)} %pack_rows.1), channel_id=1, replica_groups=mesh['dp'=16,'expert'=32] {'expert'}, dimensions={0} | all-to-all | bytes 5242880 | tf_op jit(solution)/shard_map/all_to_all | solution.py:202
  89.3 0.0 all-gather.4.cloned.1.call-done
  89.4 12.2 %expert_rows.1 = (bf16[32,40,512]{2,1,0:T(8,128)(2,1)}, bf16[8,128]{1,0:T(8,128)(2,1)}) custom-call(bf16[32,80,512]{2,1,0:T(8,128)(2,1)} %all_to_all.10.x_ref, bf16[16,3,128,768]{3,2,1,0:T(8,128)(2,1)} %bitcast.11), custom_call_target="tpu_custom_call" | custom-call | flops 6000000000 | bytes 14000000 | tf_op jit(solution)/shard_map/expert_rows/pallas_call | solution.py:203
  101.5 0.0 copy-start.3
  101.6 0.0 copy-start.2
  101.6 0.0 copy-start.1
  101.6 5.8 %all-to-all-start.1 = ((bf16[32,40,512]{2,1,0:T(8,128)(2,1)}), bf16[32,40,512]{2,1,0:T(8,128)(2,1)S(1)}, u32[]{:S(2)}, u32[]{:S(2)}) async-start(bf16[32,40,512]{2,1,0:T(8,128)(2,1)} %get-tuple-element.6), calls=%async_computation.1 | async-start | bytes 2621440 | tf_op jit(solution)/shard_map/all_to_all | solution.py:220
  107.4 0.0 copy-done.3
  107.4 0.7 copy.12.ids_t_ref
  108.1 0.0 copy-done.2
  108.1 0.7 copy.13.p_ref
  108.8 0.0 copy-done.1
  108.8 71.2 %all-gather.1 = bf16[256,128]{1,0:T(8,128)(2,1)S(1)} all-gather(bf16[8,128]{1,0:T(8,128)(2,1)S(1)} %copy-done.1), channel_id=3, replica_groups=mesh['dp'=16,'expert'=32] {'expert'}, dimensions={0}, use_global_device_ids=true | all-gather | bytes 67584 | tf_op jit(solution)/shard_map/all_gather | solution.py:219
  180.0 0.1 constant_dynamic-slice_fusion
  180.1 0.6 copy.16
  180.7 0.0 all-to-all-done.1.back_ref
  180.7 0.0 copy-start
  180.7 1.1 copy-done
  181.8 4.1 %combine_rows.1 = (bf16[128,2048]{1,0:T(8,128)(2,1)}, bf16[2,128]{1,0:T(2,128)(2,1)}) custom-call(s32[2,128]{1,0:T(2,128)} %bitcast.10, s32[128,2]{1,0:T(8,128)} %copy.12.ids_t_ref, f32[128,2]{1,0:T(8,128)} %copy.13.p_ref, bf16[32,40,512]{2,1,0:T(8,128)(2,1)} %copy-done, bf16[32,16]{1,0:T(8,128)(2,1)} %bitcast.8), custom_call_target="tpu_custom_call" | custom-call | flops 2000000000 | bytes 2000000 | tf_op jit(solution)/shard_map/combine_rows/pallas_call | solution.py:223
Async XLA Ops:
  7.2 82.2 %all-gather.4.cloned.1.call-start = ((), (), s32[]{:S(2)}) async-start(), calls=%async_computation.2 | async-start | bytes 10027008 | tf_op jit(solution)/shard_map/all_gather | solution.py:194
  101.5 5.8 %copy-start.3 = (s32[128,2]{0,1:T(2,128)S(1)}, s32[128,2]{0,1:T(2,128)}, u32[]{:S(2)}) copy-start(s32[128,2]{0,1:T(2,128)} %param.8) | copy-start | bytes 3076
  101.6 6.6 %copy-start.2 = (f32[128,2]{0,1:T(2,128)S(1)}, f32[128,2]{0,1:T(2,128)}, u32[]{:S(2)}) copy-start(f32[128,2]{0,1:T(2,128)} %param.9) | copy-start | bytes 3076
  101.6 7.3 %copy-start.1 = (bf16[8,128]{1,0:T(8,128)(2,1)S(1)}, bf16[8,128]{1,0:T(8,128)(2,1)}, u32[]{:S(2)}) copy-start(bf16[8,128]{1,0:T(8,128)(2,1)} %get-tuple-element.7) | copy-start | bytes 6148
  101.6 79.2 %all-to-all-start.1 = ((bf16[32,40,512]{2,1,0:T(8,128)(2,1)}), bf16[32,40,512]{2,1,0:T(8,128)(2,1)S(1)}, u32[]{:S(2)}, u32[]{:S(2)}) async-start(bf16[32,40,512]{2,1,0:T(8,128)(2,1)} %get-tuple-element.6), calls=%async_computation.1 | async-start | bytes 2621440 | tf_op jit(solution)/shard_map/all_to_all | solution.py:220
  180.7 1.1 copy-start
Sparse Core Ops, SparseCore 0:
  10.1 65.9 all-gather.3

commit v2 on v1

v2 whole, which is shorter than its diff:
```python
import jax
import jax.numpy as jnp
from jax import lax
from jax.experimental import pallas as pl
from jax.experimental.pallas import tpu as pltpu
from jax.sharding import PartitionSpec as P

BF = jnp.bfloat16
F32 = jnp.float32
I32 = jnp.int32


def iota(shape, dim):
    return lax.broadcasted_iota(I32, shape, dim)


def dot(a, b):
    return jnp.dot(a, b, preferred_element_type=F32)


def dot_nt(a, b):
    return lax.dot_general(a, b, (((1,), (1,)), ((), ())), preferred_element_type=F32)


def onehot(cond):
    return jnp.where(cond, 1.0, 0.0).astype(BF)


def ranks(ids, experts):
    toks = ids.shape[1]
    e = iota((experts, toks), 0)
    m0, m1 = e == ids[0:1, :], e == ids[1:2, :]
    o0, o1 = jnp.where(m0, 1.0, 0.0), jnp.where(m1, 1.0, 0.0)
    earlier = onehot(iota((toks, toks), 0) < iota((toks, toks), 1))
    r0 = dot(o0.astype(BF), earlier)
    r1 = dot(o1.astype(BF), earlier) + jnp.sum(o0, axis=1, keepdims=True)
    return jnp.where(m0, r0, -1.0), jnp.where(m1, r1, -1.0)


def weights_kernel(gu_ref, wd_ref, out_ref):
    out_ref[0:2] = gu_ref[0]
    eye = onehot(iota((128, 128), 0) == iota((128, 128), 1))
    out_ref[2] = dot_nt(eye, wd_ref[0]).astype(BF)


def quarters(x):
    return jnp.concatenate([x[:, q * 512 : (q + 1) * 512] for q in range(4)], axis=0)


def pack_kernel(ids_ref, tok_ref, grad_ref, out_ref):
    experts = out_ref.shape[0]
    toks = tok_ref.shape[0]
    k0, k1 = ranks(ids_ref[...], experts)
    slot = jnp.maximum(k0, k1).astype(BF)
    rows = experts * 8
    spread = onehot(iota((rows, experts), 0) >> 3 == iota((rows, experts), 1))
    ranked = dot(spread, slot)
    row = iota((rows, toks), 0)
    pick = onehot(ranked == (row & 7).astype(F32))
    late = jnp.where(ranked == (8 + (row & 1)).astype(F32), 1.0, 0.0)
    picks = jnp.concatenate([jnp.where((row & 7) >> 1 == q, late, 0.0).astype(BF) for q in range(4)], axis=1)
    refs = (tok_ref, grad_ref)
    for c in range(4):
        cols = slice(c * 512, (c + 1) * 512)
        parts = [dot(pick, ref[:, cols]).reshape(experts, 8, 512) for ref in refs]
        out_ref[:, :, cols] = jnp.concatenate(parts, axis=1).astype(BF)
    parts = [dot(picks, quarters(ref[...])).reshape(experts, 8, 512) for ref in refs]
    out_ref[:, :, 2048:2560] = jnp.concatenate(parts, axis=1).astype(BF)


def expert_kernel(x_ref, w_ref, out_ref, w, xs, gs, gg, ug, sems):
    sources = x_ref.shape[0]
    main, extra = sources * 8, sources * 2
    copies = [
        [
            pltpu.make_async_copy(
                w_ref.at[:, i, :, pl.ds(n * 256, 256)], w.at[i, :, :, pl.ds(n * 256, 256)], sems.at[n, i]
            )
            for i in range(3)
        ]
        for n in range(3)
    ]
    for group in copies:
        for c in group:
            c.start()
    for c in range(4):
        cols = slice(c * 512, (c + 1) * 512)
        both = x_ref[:, :, cols].astype(F32)
        xs[0:main, cols] = both[:, :8].reshape(main, 512).astype(BF)
        gs[0:main, cols] = both[:, 8:].reshape(main, 512).astype(BF)
    both = x_ref[:, :, 2048:2560].astype(F32)
    dst, src = iota((main, main), 0), iota((main, main), 1)
    gather = onehot(src == ((dst % extra) >> 1) * 8 + (dst // extra) * 2 + (dst & 1))
    for to, half in ((xs, both[:, :8]), (gs, both[:, 8:])):
        tail = dot(gather, half.reshape(main, 512).astype(BF)).astype(BF)
        for q in range(4):
            to[main : main + extra, q * 512 : (q + 1) * 512] = tail[q * extra : (q + 1) * extra]
    prob = jnp.zeros((main + extra, 1), F32)
    for n in range(3):
        for c in copies[n]:
            c.wait()
        cols = slice(n * 256, (n + 1) * 256)
        gate_pre = dot(xs[...], w[0, :, :, cols].reshape(2048, 256))
        up_value = dot(xs[...], w[1, :, :, cols].reshape(2048, 256))
        hidden_grad = dot(gs[...], w[2, :, :, cols].reshape(2048, 256))
        sig = jax.nn.sigmoid(gate_pre)
        act = gate_pre * sig
        hidden = (act * up_value).astype(BF).astype(F32)
        prob = prob + jnp.sum(hidden * hidden_grad, axis=1, keepdims=True)
        gg[:, cols] = (hidden_grad * up_value * sig * (1.0 + gate_pre * (1.0 - sig))).astype(BF)
        ug[:, cols] = (hidden_grad * act).astype(BF)
    rows = main + extra
    row, lane = iota((rows, 128), 0), iota((rows, 128), 1)
    slot = jnp.where(row < main, row & 7, 8 + (row & 1))
    placed = jnp.where(lane == slot, jnp.broadcast_to(prob, (rows, 128)), 0.0).astype(BF)
    at, row = iota((main, rows), 0), iota((main, rows), 1)
    source = jnp.where(row < main, row >> 3, (row - main) >> 1)
    placed = dot(onehot(at == source * 8), placed).reshape(sources, 8, 128)
    out_ref[:, :, 2560:2688] = placed.astype(BF)
    tails = []
    for q in range(4):
        feats = slice(q * 4, (q + 1) * 4)
        row_grad = dot_nt(gg[...], w[0, feats].reshape(512, 768)) + dot_nt(ug[...], w[1, feats].reshape(512, 768))
        tails.append(row_grad[main:].astype(BF))
        out_ref[:, :, q * 512 : (q + 1) * 512] = row_grad[:main].reshape(sources, 8, 512).astype(BF)
    tail = jnp.concatenate(tails, axis=0)
    scatter = onehot(src == ((dst >> 1) & 3) * extra + (dst >> 3) * 2 + (dst & 1))
    out_ref[:, :, 2048:2560] = dot(scatter, tail).reshape(sources, 8, 512).astype(BF)


def combine_kernel(ids_ref, ids_t_ref, p_ref, back_ref, out_ref, prob_out_ref):
    experts = back_ref.shape[0]
    toks = p_ref.shape[0]
    k0, k1 = ranks(ids_ref[...], experts)
    prob = back_ref[:, :, 2560:2688].astype(F32)[:, 0]
    for k, slots in enumerate((k0, k1)):
        acc = jnp.zeros((experts, toks), F32)
        for r in range(10):
            acc = acc + jnp.where(slots == r, jnp.broadcast_to(prob[:, r : r + 1], (experts, toks)), 0.0)
        prob_out_ref[k : k + 1, :] = jnp.sum(acc, axis=0, keepdims=True).astype(BF)
    ids_t = ids_t_ref[...]
    e = iota((toks, experts), 1)
    m0, m1 = e == ids_t[:, 0:1], e == ids_t[:, 1:2]
    o0, o1 = jnp.where(m0, 1.0, 0.0), jnp.where(m1, 1.0, 0.0)
    earlier = onehot(iota((toks, toks), 1) < iota((toks, toks), 0))
    r0 = dot(earlier, o0.astype(BF))
    r1 = dot(earlier, o1.astype(BF)) + jnp.sum(o0, axis=0, keepdims=True)
    slot = jnp.concatenate([jnp.where(m0, r0, -1.0), jnp.where(m1, r1, -1.0)], axis=0).astype(BF)
    lanes = experts * 8
    spread = onehot(iota((experts, lanes), 1) >> 3 == iota((experts, lanes), 0))
    ranked = dot(slot, spread)
    j = iota((2 * toks, lanes), 1) & 7
    pick = onehot(ranked == j.astype(F32))
    late = jnp.where(ranked == (8 + (j & 1)).astype(F32), 1.0, 0.0)
    tail = back_ref[:, :, 2048:2560].astype(F32).reshape(lanes, 512).astype(BF)
    p0, p1 = p_ref[:, 0:1], p_ref[:, 1:2]
    for q in range(4):
        cols = slice(q * 512, (q + 1) * 512)
        body = back_ref[:, :, cols].astype(F32).reshape(lanes, 512).astype(BF)
        rows = dot(pick, body) + dot(jnp.where(j >> 1 == q, late, 0.0).astype(BF), tail)
        out_ref[:, cols] = (p0 * rows[:toks] + p1 * rows[toks:]).astype(BF)


def params():
    return pltpu.CompilerParams(vmem_limit_bytes=56 * 1024 * 1024)


def cost(flops, size):
    return pl.CostEstimate(flops=flops, bytes_accessed=size, transcendentals=0)


def shards(tokens, grad_out, route_ids, route_probs, gate_up, w_down):
    toks, features = tokens.shape
    experts = lax.axis_size("expert")
    n_dp = lax.axis_size("dp")
    ids = route_ids.T
    own_w = pl.pallas_call(
        weights_kernel,
        out_shape=jax.ShapeDtypeStruct((3, 128, 768), BF),
        compiler_params=params(),
        cost_estimate=cost(10**8, 1200000),
        name="join_weights",
    )(gate_up, w_down)
    full_w = lax.all_gather(own_w, "dp", axis=0, tiled=False)
    send = pl.pallas_call(
        pack_kernel,
        out_shape=jax.ShapeDtypeStruct((experts, 16, 2560), BF),
        compiler_params=params(),
        cost_estimate=cost(3 * 10**9, 4000000),
        name="pack_rows",
    )(ids, tokens, grad_out)
    rows = lax.all_to_all(send, "expert", split_axis=0, concat_axis=0, tiled=True)
    back = pl.pallas_call(
        expert_kernel,
        in_specs=[pl.BlockSpec(memory_space=pltpu.VMEM), pl.BlockSpec(memory_space=pl.ANY)],
        out_shape=jax.ShapeDtypeStruct((experts, 8, 2688), BF),
        scratch_shapes=[
            pltpu.VMEM((3, n_dp, 128, 768), BF),
            pltpu.VMEM((experts * 10, features), BF),
            pltpu.VMEM((experts * 10, features), BF),
            pltpu.VMEM((experts * 10, 768), BF),
            pltpu.VMEM((experts * 10, 768), BF),
            pltpu.SemaphoreType.DMA((3, 3)),
        ],
        compiler_params=params(),
        cost_estimate=cost(6 * 10**9, 14000000),
        name="expert_rows",
    )(rows, full_w)
    back = lax.all_to_all(back, "expert", split_axis=0, concat_axis=0, tiled=True)
    input_grad, prob_grad = pl.pallas_call(
        combine_kernel,
        out_shape=(jax.ShapeDtypeStruct((toks, features), BF), jax.ShapeDtypeStruct((2, toks), BF)),
        compiler_params=params(),
        cost_estimate=cost(2 * 10**9, 2000000),
        name="combine_rows",
    )(ids, route_ids, route_probs, back)
    return input_grad, prob_grad.T


def solution(mesh):
    return jax.shard_map(
        shards,
        mesh=mesh,
        in_specs=(
            P(("dp", "expert"), None),
            P(("dp", "expert"), None),
            P(("dp", "expert"), None),
            P(("dp", "expert"), None),
            P("expert", None, "dp", None),
            P("expert", None, "dp"),
        ),
        out_specs=(P(("dp", "expert"), None), P(("dp", "expert"), None)),
        check_vma=False,
    )
```

time: 193 us -> 153 us (0.79)
  the two profiles are of different devices: /device:TPU:40 before, /device:TPU:24 now
where the time goes in v2:
time: 153 us
  blocking collectives  75.1 us (49%)
  waiting for transfers between devices  33.8 us (22%)
  Pallas kernels  21.4 us (14%)
  between operations  14.1 us (9%)
  starting transfers between devices  5.67 us (4%)
  local copies, waits for them, and re-layouts  2.59 us (2%)
    all_to_all x1, blocking collectives, shards(): lax.all_to_all(send, 'expert', split_axis=0, concat_axis=0, tiled=True)  75.1 us
    all_to_all x1, waiting for transfers between devices, shards(): lax.all_to_all(back, 'expert', split_axis=0, concat_axis=0, tiled=True)  33.7 us
    pallas_call x1, Pallas kernels, shards(): pl.pallas_call(expert_kernel, in_specs=[pl.BlockSpec(memory_space=pltpu.V...  12.1 us
    all_to_all x1, starting transfers between devices, shards(): lax.all_to_all(back, 'expert', split_axis=0, concat_axis=0, tiled=True)  5.64 us
    pallas_call x1, Pallas kernels, shards(): pl.pallas_call(pack_kernel, out_shape=jax.ShapeDtypeStruct((experts, 16,...  3.94 us
    pallas_call x1, Pallas kernels, shards(): pl.pallas_call(combine_kernel, out_shape=(jax.ShapeDtypeStruct((toks, fea...  3.26 us
  transfers between devices with their start and end apart: 2, of which 1 were waited for; matrix products, arithmetic and copies ran while one was open for 1% of the time, Pallas kernels for 3%

profile of v2, /device:TPU:24, one launch (start us, length us, event | category | flops | bytes accessed | tf_op | source)
XLA Modules:
  0.0 152.6 jit_solution(1218291917374588377)
XLA Ops:
  7.2 0.0 all-gather.3.cloned.1.call-start
  7.2 2.1 %join_weights.1 = bf16[3,128,768]{2,1,0:T(8,128)(2,1)} custom-call(bf16[1,2,128,768]{3,2,1,0:T(8,128)(2,1)} %gu_ref.1, bf16[1,768,128]{2,1,0:T(8,128)(2,1)} %wd_ref.1), custom_call_target="tpu_custom_call" | custom-call | flops 100000000 | bytes 1200000 | tf_op jit(solution)/shard_map/join_weights/pallas_call | solution.py:177
  9.3 0.0 all-gather.3.cloned.1.call-update
  9.3 3.9 %pack_rows.1 = bf16[32,16,2560]{2,1,0:T(8,128)(2,1)} custom-call(s32[2,128]{1,0:T(2,128)} %bitcast.3, bf16[128,2048]{1,0:T(8,128)(2,1)} %tok_ref.1, bf16[128,2048]{1,0:T(8,128)(2,1)} %grad_ref.1), custom_call_target="tpu_custom_call" | custom-call | flops 3000000000 | bytes 4000000 | tf_op jit(solution)/shard_map/pack_rows/pallas_call | solution.py:185
  13.2 75.1 %all_to_all.10.x_ref = bf16[32,16,2560]{2,1,0:T(8,128)(2,1)} all-to-all(bf16[32,16,2560]{2,1,0:T(8,128)(2,1)} %pack_rows.1), channel_id=1, replica_groups=mesh['dp'=16,'expert'=32] {'expert'}, dimensions={0} | all-to-all | bytes 5242880 | tf_op jit(solution)/shard_map/all_to_all | solution.py:192
  88.3 0.0 all-gather.3.cloned.1.call-done
  88.3 12.1 %expert_rows.1 = bf16[32,8,2688]{2,1,0:T(8,128)(2,1)} custom-call(bf16[32,16,2560]{2,1,0:T(8,128)(2,1)} %all_to_all.10.x_ref, bf16[16,3,128,768]{3,2,1,0:T(8,128)(2,1)} %bitcast.5), custom_call_target="tpu_custom_call" | custom-call | flops 6000000000 | bytes 14000000 | tf_op jit(solution)/shard_map/expert_rows/pallas_call | solution.py:193
  100.4 0.0 copy-start.2
  100.5 0.0 copy-start.1
  100.5 5.6 %all-to-all-start.1 = ((bf16[32,8,2688]{2,1,0:T(8,128)(2,1)}), bf16[32,8,2688]{2,1,0:T(8,128)(2,1)S(1)}, u32[]{:S(2)}, u32[]{:S(2)}) async-start(bf16[32,8,2688]{2,1,0:T(8,128)(2,1)} %expert_rows.1), calls=%async_computation.1 | async-start | bytes 2752512 | tf_op jit(solution)/shard_map/all_to_all | solution.py:209
  106.1 0.0 copy-done.2
  106.1 0.7 copy.10.ids_t_ref
  106.9 0.0 copy-done.1
  106.9 0.7 copy.11.p_ref
  107.6 33.7 %all-to-all-done.1.back_ref = bf16[32,8,2688]{2,1,0:T(8,128)(2,1)S(1)} async-done(((bf16[32,8,2688]{2,1,0:T(8,128)(2,1)}), bf16[32,8,2688]{2,1,0:T(8,128)(2,1)S(1)}, u32[]{:S(2)}, u32[]{:S(2)}) %all-to-all-start.1) | async-done | bytes 1376288 | tf_op jit(solution)/shard_map/all_to_all | solution.py:209
  141.4 0.0 copy-start
  141.4 1.1 copy-done
  142.5 3.3 %combine_rows.1 = (bf16[128,2048]{1,0:T(8,128)(2,1)}, bf16[2,128]{1,0:T(2,128)(2,1)}) custom-call(s32[2,128]{1,0:T(2,128)} %bitcast.4, s32[128,2]{1,0:T(8,128)} %copy.10.ids_t_ref, f32[128,2]{1,0:T(8,128)} %copy.11.p_ref, bf16[32,8,2688]{2,1,0:T(8,128)(2,1)} %copy-done), custom_call_target="tpu_custom_call" | custom-call | flops 2000000000 | bytes 2000000 | tf_op jit(solution)/shard_map/combine_rows/pallas_call | solution.py:210
Async XLA Ops:
  7.2 81.2 %all-gather.3.cloned.1.call-start = ((), (), s32[]{:S(2)}) async-start(), calls=%async_computation.2 | async-start | bytes 10027008 | tf_op jit(solution)/shard_map/all_gather | solution.py:184
  100.4 5.7 %copy-start.2 = (s32[128,2]{0,1:T(2,128)S(1)}, s32[128,2]{0,1:T(2,128)}, u32[]{:S(2)}) copy-start(s32[128,2]{0,1:T(2,128)} %param.8) | copy-start | bytes 3076
  100.5 6.4 %copy-start.1 = (f32[128,2]{0,1:T(2,128)S(1)}, f32[128,2]{0,1:T(2,128)}, u32[]{:S(2)}) copy-start(f32[128,2]{0,1:T(2,128)} %param.9) | copy-start | bytes 3076
  100.5 40.9 %all-to-all-start.1 = ((bf16[32,8,2688]{2,1,0:T(8,128)(2,1)}), bf16[32,8,2688]{2,1,0:T(8,128)(2,1)S(1)}, u32[]{:S(2)}, u32[]{:S(2)}) async-start(bf16[32,8,2688]{2,1,0:T(8,128)(2,1)} %expert_rows.1), calls=%async_computation.1 | async-start | bytes 2752512 | tf_op jit(solution)/shard_map/all_to_all | solution.py:209
  141.4 1.1 copy-start
Sparse Core Ops, SparseCore 0:
  10.1 67.3 all-gather.2

commit v3 on v2

--- a/solution.py
+++ b/solution.py
@@ -68,15 +68,25 @@
     out_ref[:, :, 2048:2560] = jnp.concatenate(parts, axis=1).astype(BF)
 
 
-def expert_kernel(x_ref, w_ref, out_ref, w, xs, gs, gg, ug, sems):
+def expert_kernel(x_ref, *refs):
+    pieces, (out_ref, w, xs, gs, gg, ug, sems) = refs[:-7], refs[-7:]
     sources = x_ref.shape[0]
     main, extra = sources * 8, sources * 2
+    me = lax.axis_index("dp")
+    chips = w.shape[0] // 2
+    chip, core = me // 2, me % 2
+    places = []
+    for hops in range(chips // 2 + 1):
+        up, down = (chip + hops) % chips, (chip + chips - hops) % chips
+        here = (down * (1 - core) + up * core) * 2
+        there = (up * (1 - core) + down * core) * 2
+        places += [here + core, here + 1 - core, there + 1 - core, there + core]
+    places = places[:2] + places[4:-4] + [places[-4], places[-2]]
+    blocks = list(zip(pieces, places, strict=True))
     copies = [
         [
-            pltpu.make_async_copy(
-                w_ref.at[:, i, :, pl.ds(n * 256, 256)], w.at[i, :, :, pl.ds(n * 256, 256)], sems.at[n, i]
-            )
-            for i in range(3)
+            pltpu.make_async_copy(src.at[:, :, pl.ds(n * 256, 256)], w.at[at, :, :, pl.ds(n * 256, 256)], sems.at[n, i])
+            for i, (src, at) in enumerate(blocks)
         ]
         for n in range(3)
     ]
@@ -100,9 +110,9 @@
         for c in copies[n]:
             c.wait()
         cols = slice(n * 256, (n + 1) * 256)
-        gate_pre = dot(xs[...], w[0, :, :, cols].reshape(2048, 256))
-        up_value = dot(xs[...], w[1, :, :, cols].reshape(2048, 256))
-        hidden_grad = dot(gs[...], w[2, :, :, cols].reshape(2048, 256))
+        gate_pre = dot(xs[...], w[:, 0, :, cols].reshape(2048, 256))
+        up_value = dot(xs[...], w[:, 1, :, cols].reshape(2048, 256))
+        hidden_grad = dot(gs[...], w[:, 2, :, cols].reshape(2048, 256))
         sig = jax.nn.sigmoid(gate_pre)
         act = gate_pre * sig
         hidden = (act * up_value).astype(BF).astype(F32)
@@ -120,7 +130,7 @@
     tails = []
     for q in range(4):
         feats = slice(q * 4, (q + 1) * 4)
-        row_grad = dot_nt(gg[...], w[0, feats].reshape(512, 768)) + dot_nt(ug[...], w[1, feats].reshape(512, 768))
+        row_grad = dot_nt(gg[...], w[feats, 0].reshape(512, 768)) + dot_nt(ug[...], w[feats, 1].reshape(512, 768))
         tails.append(row_grad[main:].astype(BF))
         out_ref[:, :, q * 512 : (q + 1) * 512] = row_grad[:main].reshape(sources, 8, 512).astype(BF)
     tail = jnp.concatenate(tails, axis=0)
@@ -169,11 +179,31 @@
     return pl.CostEstimate(flops=flops, bytes_accessed=size, transcendentals=0)
 
 
+def ring(own, n_dp):
+    swap = [(d, d ^ 1) for d in range(n_dp)]
+    on = [(d, (d + 2 if d % 2 == 0 else d - 2) % n_dp) for d in range(n_dp)]
+    pieces = [own, lax.ppermute(own, "dp", swap)]
+    first, second = pieces
+    for step in range(n_dp // 4 - 1):
+        first, second = lax.ppermute(first, "dp", on), lax.ppermute(second, "dp", on)
+        pieces += [first, second, lax.ppermute(first, "dp", swap), lax.ppermute(second, "dp", swap)]
+    first = lax.ppermute(first, "dp", on)
+    return pieces + [first, lax.ppermute(first, "dp", swap)]
+
+
 def shards(tokens, grad_out, route_ids, route_probs, gate_up, w_down):
     toks, features = tokens.shape
     experts = lax.axis_size("expert")
     n_dp = lax.axis_size("dp")
     ids = route_ids.T
+    send = pl.pallas_call(
+        pack_kernel,
+        out_shape=jax.ShapeDtypeStruct((experts, 16, 2560), BF),
+        compiler_params=params(),
+        cost_estimate=cost(10**9, 4000000),
+        name="pack_rows",
+    )(ids, tokens, grad_out)
+    rows = lax.all_to_all(send, "expert", split_axis=0, concat_axis=0, tiled=True)
     own_w = pl.pallas_call(
         weights_kernel,
         out_shape=jax.ShapeDtypeStruct((3, 128, 768), BF),
@@ -181,31 +211,23 @@
         cost_estimate=cost(10**8, 1200000),
         name="join_weights",
     )(gate_up, w_down)
-    full_w = lax.all_gather(own_w, "dp", axis=0, tiled=False)
-    send = pl.pallas_call(
-        pack_kernel,
-        out_shape=jax.ShapeDtypeStruct((experts, 16, 2560), BF),
-        compiler_params=params(),
-        cost_estimate=cost(3 * 10**9, 4000000),
-        name="pack_rows",
-    )(ids, tokens, grad_out)
-    rows = lax.all_to_all(send, "expert", split_axis=0, concat_axis=0, tiled=True)
+    pieces = ring(own_w, n_dp)
     back = pl.pallas_call(
         expert_kernel,
-        in_specs=[pl.BlockSpec(memory_space=pltpu.VMEM), pl.BlockSpec(memory_space=pl.ANY)],
+        in_specs=[pl.BlockSpec(memory_space=pltpu.VMEM)] + [pl.BlockSpec(memory_space=pl.ANY)] * len(pieces),
         out_shape=jax.ShapeDtypeStruct((experts, 8, 2688), BF),
         scratch_shapes=[
-            pltpu.VMEM((3, n_dp, 128, 768), BF),
+            pltpu.VMEM((n_dp, 3, 128, 768), BF),
             pltpu.VMEM((experts * 10, features), BF),
             pltpu.VMEM((experts * 10, features), BF),
             pltpu.VMEM((experts * 10, 768), BF),
             pltpu.VMEM((experts * 10, 768), BF),
-            pltpu.SemaphoreType.DMA((3, 3)),
+            pltpu.SemaphoreType.DMA((3, n_dp)),
         ],
         compiler_params=params(),
         cost_estimate=cost(6 * 10**9, 14000000),
         name="expert_rows",
-    )(rows, full_w)
+    )(rows, *pieces)
     back = lax.all_to_all(back, "expert", split_axis=0, concat_axis=0, tiled=True)
     input_grad, prob_grad = pl.pallas_call(
         combine_kernel,

time: 153 us -> 144 us (0.941)
  blocking collectives: 75.1 us -> 0 us
  starting transfers between devices: 5.67 us -> 71.3 us
  between operations: 14.1 us -> 1.03 us
  waiting for transfers between devices: 33.8 us -> 43.2 us
  local copies, waits for them, and re-layouts: 2.59 us -> 5.99 us
    all_to_all x1 -> x0, blocking collectives: 75.1 us -> none  [shards(): lax.all_to_all(send, 'expert', split_axis=0, concat_axis=0, tiled=True)]
    ppermute x0 -> x15, starting transfers between devices: none -> 48.6 us  [the longest x3 15.8 us: ring(): lax.ppermute(first, 'dp', on)]
    all_to_all x0 -> x1, starting transfers between devices: none -> 13.2 us  [shards(): lax.all_to_all(send, 'expert', split_axis=0, concat_axis=0, tiled=True)]
    ppermute x0 -> x15, waiting for transfers between devices: none -> 8.68 us  [the longest x3 7.2 us: ring(): lax.ppermute(first, 'dp', on)]
    all_to_all x1, starting transfers between devices: 5.64 us -> 9.5 us  [shards(): lax.all_to_all(back, 'expert', split_axis=0, concat_axis=0, tiled=True)]
    unnamed x8 -> x38, local copies, waits for them, and re-layouts: 2.59 us -> 5.99 us
  transfers between devices with their start and end apart: 2 -> 17, of which waited for: 1 -> 6; matrix products, arithmetic and copies ran while one was open for 1% -> 1% of each run, Pallas kernels for 3% -> 1%
where the time goes in v3:
time: 144 us; the launch traced here: 143 us
  starting transfers between devices  71.3 us (50%)
  waiting for transfers between devices  43.2 us (30%)
  Pallas kernels  21.8 us (15%)
  local copies, waits for them, and re-layouts  5.99 us (4%)
    all_to_all x1, waiting for transfers between devices, shards(): lax.all_to_all(back, 'expert', split_axis=0, concat_axis=0, tiled=True)  34.5 us
    ppermute x3, starting transfers between devices, ring(): lax.ppermute(first, 'dp', on)  15.8 us
    all_to_all x1, starting transfers between devices, shards(): lax.all_to_all(send, 'expert', split_axis=0, concat_axis=0, tiled=True)  13.2 us
    pallas_call x1, Pallas kernels, shards(): pl.pallas_call(expert_kernel, in_specs=[pl.BlockSpec(memory_space=pltpu.V...  12.5 us
    ppermute x3, starting transfers between devices, ring(): lax.ppermute(second, 'dp', on)  10.1 us
    all_to_all x1, starting transfers between devices, shards(): lax.all_to_all(back, 'expert', split_axis=0, concat_axis=0, tiled=True)  9.5 us
    ppermute x3, starting transfers between devices, ring(): lax.ppermute(second, 'dp', swap)  7.22 us
    ppermute x3, waiting for transfers between devices, ring(): lax.ppermute(first, 'dp', on)  7.2 us
  transfers between devices with their start and end apart: 17, of which 6 were waited for; matrix products, arithmetic and copies ran while one was open for 1% of the time, Pallas kernels for 1%

profile of v3, /device:TPU:24, one launch (start us, length us, event | category | flops | bytes accessed | tf_op | source)
XLA Modules:
  0.0 143.3 jit_solution(3611190945048142845)
XLA Ops:
  0.6 3.9 %pack_rows.1 = bf16[32,16,2560]{2,1,0:T(8,128)(2,1)} custom-call(s32[2,128]{1,0:T(2,128)} %bitcast.2, bf16[128,2048]{1,0:T(8,128)(2,1)} %tok_ref.1, bf16[128,2048]{1,0:T(8,128)(2,1)} %grad_ref.1), custom_call_target="tpu_custom_call" | custom-call | flops 1000000000 | bytes 4000000 | tf_op jit(solution)/shard_map/pack_rows/pallas_call | solution.py:199
  4.6 13.2 %all-to-all-start = ((bf16[32,16,2560]{2,1,0:T(8,128)(2,1)}), bf16[32,16,2560]{2,1,0:T(8,128)(2,1)S(1)}, u32[]{:S(2)}, u32[]{:S(2)}) async-start(bf16[32,16,2560]{2,1,0:T(8,128)(2,1)} %pack_rows.1), calls=%async_computation | async-start | bytes 5242880 | tf_op jit(solution)/shard_map/all_to_all | solution.py:206
  17.7 2.1 %join_weights.1.refs_0_ = bf16[3,128,768]{2,1,0:T(8,128)(2,1)} custom-call(bf16[1,2,128,768]{3,2,1,0:T(8,128)(2,1)} %gu_ref.1, bf16[1,768,128]{2,1,0:T(8,128)(2,1)} %wd_ref.1), custom_call_target="tpu_custom_call" | custom-call | flops 100000000 | bytes 1200000 | tf_op jit(solution)/shard_map/join_weights/pallas_call | solution.py:207
  19.8 1.9 %collective-permute-start = (bf16[3,128,768]{2,1,0:T(8,128)(2,1)}, bf16[3,128,768]{2,1,0:T(8,128)(2,1)S(1)}, u32[]{:S(2)}, u32[]{:S(2)}) collective-permute-start(bf16[3,128,768]{2,1,0:T(8,128)(2,1)} %join_weights.1.refs_0_), channel_id=1, source_target_pairs={{0,32},{32,0},{64,96},{96,64},{128,160},{160,128},{192,224},{224,1... | collective-permute-start | bytes 1769480 | tf_op jit(solution)/shard_map/ppermute | solution.py:185
  21.7 4.7 %collective-permute-start.1 = (bf16[3,128,768]{2,1,0:T(8,128)(2,1)}, bf16[3,128,768]{2,1,0:T(8,128)(2,1)S(1)}, u32[]{:S(2)}, u32[]{:S(2)}) collective-permute-start(bf16[3,128,768]{2,1,0:T(8,128)(2,1)} %join_weights.1.refs_0_), channel_id=1, source_target_pairs={{0,64},{32,480},{64,128},{96,32},{128,192},{160,96},{192,256},{224... | collective-permute-start | bytes 1769480 | tf_op jit(solution)/shard_map/ppermute | solution.py:188
  26.4 0.0 collective-permute-done.refs_1_
  26.4 2.6 %collective-permute-start.2 = (bf16[3,128,768]{2,1,0:T(8,128)(2,1)S(1)}, bf16[3,128,768]{2,1,0:T(8,128)(2,1)S(1)}, u32[]{:S(2)}, u32[]{:S(2)}) collective-permute-start(bf16[3,128,768]{2,1,0:T(8,128)(2,1)S(1)} %collective-permute-done.refs_1_), channel_id=1, source_target_pairs={{0,64},{32,480},{64,128},{96,32},{128,192},{160,96},{192,256},{224... | collective-permute-start | bytes 1769480 | tf_op jit(solution)/shard_map/ppermute | solution.py:188
  29.0 5.1 %collective-permute-done.1.refs_2_ = bf16[3,128,768]{2,1,0:T(8,128)(2,1)S(1)} collective-permute-done((bf16[3,128,768]{2,1,0:T(8,128)(2,1)}, bf16[3,128,768]{2,1,0:T(8,128)(2,1)S(1)}, u32[]{:S(2)}, u32[]{:S(2)}) %collective-permute-start.1) | collective-permute-done | bytes 589856 | tf_op jit(solution)/shard_map/ppermute | solution.py:188
  34.1 5.5 %collective-permute-start.5 = (bf16[3,128,768]{2,1,0:T(8,128)(2,1)S(1)}, bf16[3,128,768]{2,1,0:T(8,128)(2,1)S(1)}, u32[]{:S(2)}, u32[]{:S(2)}) collective-permute-start(bf16[3,128,768]{2,1,0:T(8,128)(2,1)S(1)} %collective-permute-done.1.refs_2_), channel_id=1, source_target_pairs={{0,64},{32,480},{64,128},{96,32},{128,192},{160,96},{192,256},{224... | collective-permute-start | bytes 1769480 | tf_op jit(solution)/shard_map/ppermute | solution.py:188
  39.6 0.7 collective-permute-done.2.refs_3_
  40.3 5.6 %collective-permute-start.6 = (bf16[3,128,768]{2,1,0:T(8,128)(2,1)S(1)}, bf16[3,128,768]{2,1,0:T(8,128)(2,1)S(1)}, u32[]{:S(2)}, u32[]{:S(2)}) collective-permute-start(bf16[3,128,768]{2,1,0:T(8,128)(2,1)S(1)} %collective-permute-done.2.refs_3_), channel_id=1, source_target_pairs={{0,64},{32,480},{64,128},{96,32},{128,192},{160,96},{192,256},{224... | collective-permute-start | bytes 1769480 | tf_op jit(solution)/shard_map/ppermute | solution.py:188
  45.9 1.1 collective-permute-done.5.refs_6_
  47.0 5.6 %collective-permute-start.9 = (bf16[3,128,768]{2,1,0:T(8,128)(2,1)S(1)}, bf16[3,128,768]{2,1,0:T(8,128)(2,1)S(1)}, u32[]{:S(2)}, u32[]{:S(2)}) collective-permute-start(bf16[3,128,768]{2,1,0:T(8,128)(2,1)S(1)} %collective-permute-done.5.refs_6_), channel_id=1, source_target_pairs={{0,64},{32,480},{64,128},{96,32},{128,192},{160,96},{192,256},{224... | collective-permute-start | bytes 1769480 | tf_op jit(solution)/shard_map/ppermute | solution.py:188
  52.6 1.9 %collective-permute-start.3 = (bf16[3,128,768]{2,1,0:T(8,128)(2,1)S(1)}, bf16[3,128,768]{2,1,0:T(8,128)(2,1)S(1)}, u32[]{:S(2)}, u32[]{:S(2)}) collective-permute-start(bf16[3,128,768]{2,1,0:T(8,128)(2,1)S(1)} %collective-permute-done.1.refs_2_), channel_id=1, source_target_pairs={{0,32},{32,0},{64,96},{96,64},{128,160},{160,128},{192,224},{224,1... | collective-permute-start | bytes 1769480 | tf_op jit(solution)/shard_map/ppermute | solution.py:189
  54.5 2.4 %collective-permute-start.4 = (bf16[3,128,768]{2,1,0:T(8,128)(2,1)S(1)}, bf16[3,128,768]{2,1,0:T(8,128)(2,1)S(1)}, u32[]{:S(2)}, u32[]{:S(2)}) collective-permute-start(bf16[3,128,768]{2,1,0:T(8,128)(2,1)S(1)} %collective-permute-done.2.refs_3_), channel_id=1, source_target_pairs={{0,32},{32,0},{64,96},{96,64},{128,160},{160,128},{192,224},{224,1... | collective-permute-start | bytes 1769480 | tf_op jit(solution)/shard_map/ppermute | solution.py:189
  56.9 0.0 collective-permute-done.6.refs_7_
  57.0 1.9 %collective-permute-start.10 = (bf16[3,128,768]{2,1,0:T(8,128)(2,1)S(1)}, bf16[3,128,768]{2,1,0:T(8,128)(2,1)S(1)}, u32[]{:S(2)}, u32[]{:S(2)}) collective-permute-start(bf16[3,128,768]{2,1,0:T(8,128)(2,1)S(1)} %collective-permute-done.6.refs_7_), channel_id=1, source_target_pairs={{0,64},{32,480},{64,128},{96,32},{128,192},{160,96},{192,256},{224... | collective-permute-start | bytes 1769480 | tf_op jit(solution)/shard_map/ppermute | solution.py:188
  58.9 1.1 collective-permute-done.9.refs_10_
  60.0 5.6 %collective-permute-start.13 = (bf16[3,128,768]{2,1,0:T(8,128)(2,1)S(1)}, bf16[3,128,768]{2,1,0:T(8,128)(2,1)S(1)}, u32[]{:S(2)}, u32[]{:S(2)}) collective-permute-start(bf16[3,128,768]{2,1,0:T(8,128)(2,1)S(1)} %collective-permute-done.9.refs_10_), channel_id=1, source_target_pairs={{0,64},{32,480},{64,128},{96,32},{128,192},{160,96},{192,256},{224... | collective-permute-start | bytes 1769480 | tf_op jit(solution)/shard_map/ppermute | solution.py:190
  65.6 1.9 %collective-permute-start.7 = (bf16[3,128,768]{2,1,0:T(8,128)(2,1)S(1)}, bf16[3,128,768]{2,1,0:T(8,128)(2,1)S(1)}, u32[]{:S(2)}, u32[]{:S(2)}) collective-permute-start(bf16[3,128,768]{2,1,0:T(8,128)(2,1)S(1)} %collective-permute-done.5.refs_6_), channel_id=1, source_target_pairs={{0,32},{32,0},{64,96},{96,64},{128,160},{160,128},{192,224},{224,1... | collective-permute-start | bytes 1769480 | tf_op jit(solution)/shard_map/ppermute | solution.py:189
  67.5 0.0 collective-permute-done.3.refs_4_
  67.5 2.4 %collective-permute-start.8 = (bf16[3,128,768]{2,1,0:T(8,128)(2,1)S(1)}, bf16[3,128,768]{2,1,0:T(8,128)(2,1)S(1)}, u32[]{:S(2)}, u32[]{:S(2)}) collective-permute-start(bf16[3,128,768]{2,1,0:T(8,128)(2,1)S(1)} %collective-permute-done.6.refs_7_), channel_id=1, source_target_pairs={{0,32},{32,0},{64,96},{96,64},{128,160},{160,128},{192,224},{224,1... | collective-permute-start | bytes 1769480 | tf_op jit(solution)/shard_map/ppermute | solution.py:189
  69.9 0.0 collective-permute-done.4.refs_5_
  70.0 1.9 %collective-permute-start.11 = (bf16[3,128,768]{2,1,0:T(8,128)(2,1)S(1)}, bf16[3,128,768]{2,1,0:T(8,128)(2,1)S(1)}, u32[]{:S(2)}, u32[]{:S(2)}) collective-permute-start(bf16[3,128,768]{2,1,0:T(8,128)(2,1)S(1)} %collective-permute-done.9.refs_10_), channel_id=1, source_target_pairs={{0,32},{32,0},{64,96},{96,64},{128,160},{160,128},{192,224},{224,1... | collective-permute-start | bytes 1769480 | tf_op jit(solution)/shard_map/ppermute | solution.py:189
  71.9 0.0 collective-permute-done.10.refs_11_
  71.9 2.4 %collective-permute-start.12 = (bf16[3,128,768]{2,1,0:T(8,128)(2,1)S(1)}, bf16[3,128,768]{2,1,0:T(8,128)(2,1)S(1)}, u32[]{:S(2)}, u32[]{:S(2)}) collective-permute-start(bf16[3,128,768]{2,1,0:T(8,128)(2,1)S(1)} %collective-permute-done.10.refs_11_), channel_id=1, source_target_pairs={{0,32},{32,0},{64,96},{96,64},{128,160},{160,128},{192,224},{224,1... | collective-permute-start | bytes 1769480 | tf_op jit(solution)/shard_map/ppermute | solution.py:189
  74.3 0.7 collective-permute-done.13.refs_14_
  75.1 2.3 %collective-permute-start.14 = (bf16[3,128,768]{2,1,0:T(8,128)(2,1)S(1)}, bf16[3,128,768]{2,1,0:T(8,128)(2,1)}, u32[]{:S(2)}, u32[]{:S(2)}) collective-permute-start(bf16[3,128,768]{2,1,0:T(8,128)(2,1)S(1)} %collective-permute-done.13.refs_14_), channel_id=1, source_target_pairs={{0,32},{32,0},{64,96},{96,64},{128,160},{160,128},{192,224},{224,1... | collective-permute-start | bytes 1769480 | tf_op jit(solution)/shard_map/ppermute | solution.py:191
  77.3 0.0 collective-permute-done.7.refs_8_
  77.4 0.0 collective-permute-done.8.refs_9_
  77.4 0.0 collective-permute-done.11.refs_12_
  77.4 0.0 collective-permute-done.12.refs_13_
  77.5 0.7 copy-done.14
  78.2 0.2 copy-done.15
  78.3 0.2 copy-done.16
  78.6 0.8 copy-done.17
  79.4 0.0 collective-permute-done.14.refs_15_
  79.4 0.0 all-to-all-done.x_ref
  79.4 1.5 %copy-done = bf16[32,16,2560]{2,1,0:T(8,128)(2,1)} copy-done((bf16[32,16,2560]{2,1,0:T(8,128)(2,1)}, bf16[32,16,2560]{2,1,0:T(8,128)(2,1)S(1)}, u32[]{:S(2)}) %copy-start) | copy-done | bytes 2621464
  80.9 12.5 %expert_rows.1 = bf16[32,8,2688]{2,1,0:T(8,128)(2,1)} custom-call(bf16[32,16,2560]{2,1,0:T(8,128)(2,1)} %copy-done, bf16[3,128,768]{2,1,0:T(8,128)(2,1)} %join_weights.1.refs_0_, bf16[3,128,768]{2,1,0:T(8,128)(2,1)} %copy-done.4, bf16[3,128,768]{2,1,0:T(8,128)(2,1)} %copy-done.5, bf16[3,128,768]{2,1,0:T(8,128)(2,1)} %copy-done.6, ...), custom_call_target="tpu_custom_call" | custom-call | flops 6000000000 | bytes 14000000 | tf_op jit(solution)/shard_map/expert_rows/pallas_call | solution.py:215
  93.4 0.0 copy-start.3
  93.4 0.0 copy-start.2
  93.5 9.5 %all-to-all-start.1 = ((bf16[32,8,2688]{2,1,0:T(8,128)(2,1)}), bf16[32,8,2688]{2,1,0:T(8,128)(2,1)S(1)}, u32[]{:S(2)}, u32[]{:S(2)}) async-start(bf16[32,8,2688]{2,1,0:T(8,128)(2,1)} %expert_rows.1), calls=%async_computation.1 | async-start | bytes 2752512 | tf_op jit(solution)/shard_map/all_to_all | solution.py:231
  103.0 0.7 copy.8.ids_t_ref
  103.7 0.7 copy.9.p_ref
  104.4 34.5 %all-to-all-done.1.back_ref = bf16[32,8,2688]{2,1,0:T(8,128)(2,1)S(1)} async-done(((bf16[32,8,2688]{2,1,0:T(8,128)(2,1)}), bf16[32,8,2688]{2,1,0:T(8,128)(2,1)S(1)}, u32[]{:S(2)}, u32[]{:S(2)}) %all-to-all-start.1) | async-done | bytes 1376288 | tf_op jit(solution)/shard_map/all_to_all | solution.py:231
  138.9 1.1 copy-done.1
  140.0 3.3 %combine_rows.1 = (bf16[128,2048]{1,0:T(8,128)(2,1)}, bf16[2,128]{1,0:T(2,128)(2,1)}) custom-call(s32[2,128]{1,0:T(2,128)} %bitcast.3, s32[128,2]{1,0:T(8,128)} %copy.8.ids_t_ref, f32[128,2]{1,0:T(8,128)} %copy.9.p_ref, bf16[32,8,2688]{2,1,0:T(8,128)(2,1)} %copy-done.1), custom_call_target="tpu_custom_call" | custom-call | flops 2000000000 | bytes 2000000 | tf_op jit(solution)/shard_map/combine_rows/pallas_call | solution.py:232
  (28 shorter events, 0.1 us)
Async XLA Ops:
  4.6 74.8 %all-to-all-start = ((bf16[32,16,2560]{2,1,0:T(8,128)(2,1)}), bf16[32,16,2560]{2,1,0:T(8,128)(2,1)S(1)}, u32[]{:S(2)}, u32[]{:S(2)}) async-start(bf16[32,16,2560]{2,1,0:T(8,128)(2,1)} %pack_rows.1), calls=%async_computation | async-start | bytes 5242880 | tf_op jit(solution)/shard_map/all_to_all | solution.py:206
  19.8 6.6 %collective-permute-start = (bf16[3,128,768]{2,1,0:T(8,128)(2,1)}, bf16[3,128,768]{2,1,0:T(8,128)(2,1)S(1)}, u32[]{:S(2)}, u32[]{:S(2)}) collective-permute-start(bf16[3,128,768]{2,1,0:T(8,128)(2,1)} %join_weights.1.refs_0_), channel_id=1, source_target_pairs={{0,32},{32,0},{64,96},{96,64},{128,160},{160,128},{192,224},{224,1... | collective-permute-start | bytes 1769480 | tf_op jit(solution)/shard_map/ppermute | solution.py:185
  21.7 12.4 %collective-permute-start.1 = (bf16[3,128,768]{2,1,0:T(8,128)(2,1)}, bf16[3,128,768]{2,1,0:T(8,128)(2,1)S(1)}, u32[]{:S(2)}, u32[]{:S(2)}) collective-permute-start(bf16[3,128,768]{2,1,0:T(8,128)(2,1)} %join_weights.1.refs_0_), channel_id=1, source_target_pairs={{0,64},{32,480},{64,128},{96,32},{128,192},{160,96},{192,256},{224... | collective-permute-start | bytes 1769480 | tf_op jit(solution)/shard_map/ppermute | solution.py:188
  26.4 52.9 %copy-start.4 = (bf16[3,128,768]{2,1,0:T(8,128)(2,1)}, bf16[3,128,768]{2,1,0:T(8,128)(2,1)S(1)}, u32[]{:S(2)}) copy-start(bf16[3,128,768]{2,1,0:T(8,128)(2,1)S(1)} %collective-permute-done.refs_1_) | copy-start | bytes 1769476
  26.4 13.9 %collective-permute-start.2 = (bf16[3,128,768]{2,1,0:T(8,128)(2,1)S(1)}, bf16[3,128,768]{2,1,0:T(8,128)(2,1)S(1)}, u32[]{:S(2)}, u32[]{:S(2)}) collective-permute-start(bf16[3,128,768]{2,1,0:T(8,128)(2,1)S(1)} %collective-permute-done.refs_1_), channel_id=1, source_target_pairs={{0,64},{32,480},{64,128},{96,32},{128,192},{160,96},{192,256},{224... | collective-permute-start | bytes 1769480 | tf_op jit(solution)/shard_map/ppermute | solution.py:188
  34.1 43.3 %copy-start.5 = (bf16[3,128,768]{2,1,0:T(8,128)(2,1)}, bf16[3,128,768]{2,1,0:T(8,128)(2,1)S(1)}, u32[]{:S(2)}) copy-start(bf16[3,128,768]{2,1,0:T(8,128)(2,1)S(1)} %collective-permute-done.1.refs_2_) | copy-start | bytes 1769476
  34.1 12.9 %collective-permute-start.5 = (bf16[3,128,768]{2,1,0:T(8,128)(2,1)S(1)}, bf16[3,128,768]{2,1,0:T(8,128)(2,1)S(1)}, u32[]{:S(2)}, u32[]{:S(2)}) collective-permute-start(bf16[3,128,768]{2,1,0:T(8,128)(2,1)S(1)} %collective-permute-done.1.refs_2_), channel_id=1, source_target_pairs={{0,64},{32,480},{64,128},{96,32},{128,192},{160,96},{192,256},{224... | collective-permute-start | bytes 1769480 | tf_op jit(solution)/shard_map/ppermute | solution.py:188
  40.3 37.1 %copy-start.6 = (bf16[3,128,768]{2,1,0:T(8,128)(2,1)}, bf16[3,128,768]{2,1,0:T(8,128)(2,1)S(1)}, u32[]{:S(2)}) copy-start(bf16[3,128,768]{2,1,0:T(8,128)(2,1)S(1)} %collective-permute-done.2.refs_3_) | copy-start | bytes 1769476
  40.3 16.6 %collective-permute-start.6 = (bf16[3,128,768]{2,1,0:T(8,128)(2,1)S(1)}, bf16[3,128,768]{2,1,0:T(8,128)(2,1)S(1)}, u32[]{:S(2)}, u32[]{:S(2)}) collective-permute-start(bf16[3,128,768]{2,1,0:T(8,128)(2,1)S(1)} %collective-permute-done.2.refs_3_), channel_id=1, source_target_pairs={{0,64},{32,480},{64,128},{96,32},{128,192},{160,96},{192,256},{224... | collective-permute-start | bytes 1769480 | tf_op jit(solution)/shard_map/ppermute | solution.py:188
  47.0 30.4 %copy-start.7 = (bf16[3,128,768]{2,1,0:T(8,128)(2,1)}, bf16[3,128,768]{2,1,0:T(8,128)(2,1)S(1)}, u32[]{:S(2)}) copy-start(bf16[3,128,768]{2,1,0:T(8,128)(2,1)S(1)} %collective-permute-done.5.refs_6_) | copy-start | bytes 1769476
  47.0 13.0 %collective-permute-start.9 = (bf16[3,128,768]{2,1,0:T(8,128)(2,1)S(1)}, bf16[3,128,768]{2,1,0:T(8,128)(2,1)S(1)}, u32[]{:S(2)}, u32[]{:S(2)}) collective-permute-start(bf16[3,128,768]{2,1,0:T(8,128)(2,1)S(1)} %collective-permute-done.5.refs_6_), channel_id=1, source_target_pairs={{0,64},{32,480},{64,128},{96,32},{128,192},{160,96},{192,256},{224... | collective-permute-start | bytes 1769480 | tf_op jit(solution)/shard_map/ppermute | solution.py:188
  52.6 14.9 %collective-permute-start.3 = (bf16[3,128,768]{2,1,0:T(8,128)(2,1)S(1)}, bf16[3,128,768]{2,1,0:T(8,128)(2,1)S(1)}, u32[]{:S(2)}, u32[]{:S(2)}) collective-permute-start(bf16[3,128,768]{2,1,0:T(8,128)(2,1)S(1)} %collective-permute-done.1.refs_2_), channel_id=1, source_target_pairs={{0,32},{32,0},{64,96},{96,64},{128,160},{160,128},{192,224},{224,1... | collective-permute-start | bytes 1769480 | tf_op jit(solution)/shard_map/ppermute | solution.py:189
  54.5 15.4 %collective-permute-start.4 = (bf16[3,128,768]{2,1,0:T(8,128)(2,1)S(1)}, bf16[3,128,768]{2,1,0:T(8,128)(2,1)S(1)}, u32[]{:S(2)}, u32[]{:S(2)}) collective-permute-start(bf16[3,128,768]{2,1,0:T(8,128)(2,1)S(1)} %collective-permute-done.2.refs_3_), channel_id=1, source_target_pairs={{0,32},{32,0},{64,96},{96,64},{128,160},{160,128},{192,224},{224,1... | collective-permute-start | bytes 1769480 | tf_op jit(solution)/shard_map/ppermute | solution.py:189
  56.9 20.5 %copy-start.8 = (bf16[3,128,768]{2,1,0:T(8,128)(2,1)}, bf16[3,128,768]{2,1,0:T(8,128)(2,1)S(1)}, u32[]{:S(2)}) copy-start(bf16[3,128,768]{2,1,0:T(8,128)(2,1)S(1)} %collective-permute-done.6.refs_7_) | copy-start | bytes 1769476
  57.0 14.9 %collective-permute-start.10 = (bf16[3,128,768]{2,1,0:T(8,128)(2,1)S(1)}, bf16[3,128,768]{2,1,0:T(8,128)(2,1)S(1)}, u32[]{:S(2)}, u32[]{:S(2)}) collective-permute-start(bf16[3,128,768]{2,1,0:T(8,128)(2,1)S(1)} %collective-permute-done.6.refs_7_), channel_id=1, source_target_pairs={{0,64},{32,480},{64,128},{96,32},{128,192},{160,96},{192,256},{224... | collective-permute-start | bytes 1769480 | tf_op jit(solution)/shard_map/ppermute | solution.py:188
  60.0 17.5 %copy-start.9 = (bf16[3,128,768]{2,1,0:T(8,128)(2,1)}, bf16[3,128,768]{2,1,0:T(8,128)(2,1)S(1)}, u32[]{:S(2)}) copy-start(bf16[3,128,768]{2,1,0:T(8,128)(2,1)S(1)} %collective-permute-done.9.refs_10_) | copy-start | bytes 1769476
  60.0 15.1 %collective-permute-start.13 = (bf16[3,128,768]{2,1,0:T(8,128)(2,1)S(1)}, bf16[3,128,768]{2,1,0:T(8,128)(2,1)S(1)}, u32[]{:S(2)}, u32[]{:S(2)}) collective-permute-start(bf16[3,128,768]{2,1,0:T(8,128)(2,1)S(1)} %collective-permute-done.9.refs_10_), channel_id=1, source_target_pairs={{0,64},{32,480},{64,128},{96,32},{128,192},{160,96},{192,256},{224... | collective-permute-start | bytes 1769480 | tf_op jit(solution)/shard_map/ppermute | solution.py:190
  65.6 11.8 %collective-permute-start.7 = (bf16[3,128,768]{2,1,0:T(8,128)(2,1)S(1)}, bf16[3,128,768]{2,1,0:T(8,128)(2,1)S(1)}, u32[]{:S(2)}, u32[]{:S(2)}) collective-permute-start(bf16[3,128,768]{2,1,0:T(8,128)(2,1)S(1)} %collective-permute-done.5.refs_6_), channel_id=1, source_target_pairs={{0,32},{32,0},{64,96},{96,64},{128,160},{160,128},{192,224},{224,1... | collective-permute-start | bytes 1769480 | tf_op jit(solution)/shard_map/ppermute | solution.py:189
  67.5 9.9 %copy-start.10 = (bf16[3,128,768]{2,1,0:T(8,128)(2,1)}, bf16[3,128,768]{2,1,0:T(8,128)(2,1)S(1)}, u32[]{:S(2)}) copy-start(bf16[3,128,768]{2,1,0:T(8,128)(2,1)S(1)} %collective-permute-done.3.refs_4_) | copy-start | bytes 1769476
  67.5 9.8 %collective-permute-start.8 = (bf16[3,128,768]{2,1,0:T(8,128)(2,1)S(1)}, bf16[3,128,768]{2,1,0:T(8,128)(2,1)S(1)}, u32[]{:S(2)}, u32[]{:S(2)}) collective-permute-start(bf16[3,128,768]{2,1,0:T(8,128)(2,1)S(1)} %collective-permute-done.6.refs_7_), channel_id=1, source_target_pairs={{0,32},{32,0},{64,96},{96,64},{128,160},{160,128},{192,224},{224,1... | collective-permute-start | bytes 1769480 | tf_op jit(solution)/shard_map/ppermute | solution.py:189
  69.9 7.5 %copy-start.11 = (bf16[3,128,768]{2,1,0:T(8,128)(2,1)}, bf16[3,128,768]{2,1,0:T(8,128)(2,1)S(1)}, u32[]{:S(2)}) copy-start(bf16[3,128,768]{2,1,0:T(8,128)(2,1)S(1)} %collective-permute-done.4.refs_5_) | copy-start | bytes 1769476
  70.0 7.4 %collective-permute-start.11 = (bf16[3,128,768]{2,1,0:T(8,128)(2,1)S(1)}, bf16[3,128,768]{2,1,0:T(8,128)(2,1)S(1)}, u32[]{:S(2)}, u32[]{:S(2)}) collective-permute-start(bf16[3,128,768]{2,1,0:T(8,128)(2,1)S(1)} %collective-permute-done.9.refs_10_), channel_id=1, source_target_pairs={{0,32},{32,0},{64,96},{96,64},{128,160},{160,128},{192,224},{224,1... | collective-permute-start | bytes 1769480 | tf_op jit(solution)/shard_map/ppermute | solution.py:189
  71.9 5.6 %copy-start.12 = (bf16[3,128,768]{2,1,0:T(8,128)(2,1)}, bf16[3,128,768]{2,1,0:T(8,128)(2,1)S(1)}, u32[]{:S(2)}) copy-start(bf16[3,128,768]{2,1,0:T(8,128)(2,1)S(1)} %collective-permute-done.10.refs_11_) | copy-start | bytes 1769476
  71.9 5.5 %collective-permute-start.12 = (bf16[3,128,768]{2,1,0:T(8,128)(2,1)S(1)}, bf16[3,128,768]{2,1,0:T(8,128)(2,1)S(1)}, u32[]{:S(2)}, u32[]{:S(2)}) collective-permute-start(bf16[3,128,768]{2,1,0:T(8,128)(2,1)S(1)} %collective-permute-done.10.refs_11_), channel_id=1, source_target_pairs={{0,32},{32,0},{64,96},{96,64},{128,160},{160,128},{192,224},{224,1... | collective-permute-start | bytes 1769480 | tf_op jit(solution)/shard_map/ppermute | solution.py:189
  75.1 2.4 %copy-start.13 = (bf16[3,128,768]{2,1,0:T(8,128)(2,1)}, bf16[3,128,768]{2,1,0:T(8,128)(2,1)S(1)}, u32[]{:S(2)}) copy-start(bf16[3,128,768]{2,1,0:T(8,128)(2,1)S(1)} %collective-permute-done.13.refs_14_) | copy-start | bytes 1769476
  75.1 4.3 %collective-permute-start.14 = (bf16[3,128,768]{2,1,0:T(8,128)(2,1)S(1)}, bf16[3,128,768]{2,1,0:T(8,128)(2,1)}, u32[]{:S(2)}, u32[]{:S(2)}) collective-permute-start(bf16[3,128,768]{2,1,0:T(8,128)(2,1)S(1)} %collective-permute-done.13.refs_14_), channel_id=1, source_target_pairs={{0,32},{32,0},{64,96},{96,64},{128,160},{160,128},{192,224},{224,1... | collective-permute-start | bytes 1769480 | tf_op jit(solution)/shard_map/ppermute | solution.py:191
  77.3 0.8 copy-start.14
  77.4 1.0 copy-start.15
  77.4 1.2 copy-start.16
  78.6 0.8 copy-start.17
  79.4 1.5 %copy-start = (bf16[32,16,2560]{2,1,0:T(8,128)(2,1)}, bf16[32,16,2560]{2,1,0:T(8,128)(2,1)S(1)}, u32[]{:S(2)}) copy-start(bf16[32,16,2560]{2,1,0:T(8,128)(2,1)S(1)} %all-to-all-done.x_ref) | copy-start | bytes 7864324
  93.4 9.5 %copy-start.3 = (s32[128,2]{0,1:T(2,128)S(1)}, s32[128,2]{0,1:T(2,128)}, u32[]{:S(2)}) copy-start(s32[128,2]{0,1:T(2,128)} %param.8) | copy-start | bytes 3076
  93.4 10.3 %copy-start.2 = (f32[128,2]{0,1:T(2,128)S(1)}, f32[128,2]{0,1:T(2,128)}, u32[]{:S(2)}) copy-start(f32[128,2]{0,1:T(2,128)} %param.9) | copy-start | bytes 3076
  93.5 45.5 %all-to-all-start.1 = ((bf16[32,8,2688]{2,1,0:T(8,128)(2,1)}), bf16[32,8,2688]{2,1,0:T(8,128)(2,1)S(1)}, u32[]{:S(2)}, u32[]{:S(2)}) async-start(bf16[32,8,2688]{2,1,0:T(8,128)(2,1)} %expert_rows.1), calls=%async_computation.1 | async-start | bytes 2752512 | tf_op jit(solution)/shard_map/all_to_all | solution.py:231
  138.9 1.1 copy-start.1

commit v4 on v3

--- a/solution.py
+++ b/solution.py
@@ -47,9 +47,23 @@
     return jnp.concatenate([x[:, q * 512 : (q + 1) * 512] for q in range(4)], axis=0)
 
 
-def pack_kernel(ids_ref, tok_ref, grad_ref, out_ref):
+def stream(src, dst, sems, columns):
+    return [
+        pltpu.make_async_copy(src.at[:, :, pl.ds(at, size)], dst.at[:, :, pl.ds(at, size)], sems.at[i])
+        for i, (at, size) in enumerate(columns)
+    ]
+
+
+def pack_kernel(ids_hbm, tok_hbm, grad_hbm, out_hbm, ids_ref, tok_ref, grad_ref, out_ref, sems, out_sems):
+    refs = (tok_ref, grad_ref)
+    ids_load = pltpu.make_async_copy(ids_hbm, ids_ref, sems.at[2])
+    ids_load.start()
+    loads = [pltpu.make_async_copy(src, to, sems.at[i]) for i, (src, to) in enumerate(zip((tok_hbm, grad_hbm), refs))]
+    for load in loads:
+        load.start()
     experts = out_ref.shape[0]
     toks = tok_ref.shape[0]
+    ids_load.wait()
     k0, k1 = ranks(ids_ref[...], experts)
     slot = jnp.maximum(k0, k1).astype(BF)
     rows = experts * 8
@@ -59,45 +73,61 @@
     pick = onehot(ranked == (row & 7).astype(F32))
     late = jnp.where(ranked == (8 + (row & 1)).astype(F32), 1.0, 0.0)
     picks = jnp.concatenate([jnp.where((row & 7) >> 1 == q, late, 0.0).astype(BF) for q in range(4)], axis=1)
-    refs = (tok_ref, grad_ref)
+    for load in loads:
+        load.wait()
+    stores = stream(out_ref, out_hbm, out_sems, [(c * 512, 512) for c in range(5)])
     for c in range(4):
         cols = slice(c * 512, (c + 1) * 512)
         parts = [dot(pick, ref[:, cols]).reshape(experts, 8, 512) for ref in refs]
         out_ref[:, :, cols] = jnp.concatenate(parts, axis=1).astype(BF)
+        stores[c].start()
     parts = [dot(picks, quarters(ref[...])).reshape(experts, 8, 512) for ref in refs]
     out_ref[:, :, 2048:2560] = jnp.concatenate(parts, axis=1).astype(BF)
-
-
-def expert_kernel(x_ref, *refs):
-    pieces, (out_ref, w, xs, gs, gg, ug, sems) = refs[:-7], refs[-7:]
-    sources = x_ref.shape[0]
-    main, extra = sources * 8, sources * 2
-    me = lax.axis_index("dp")
-    chips = w.shape[0] // 2
-    chip, core = me // 2, me % 2
-    places = []
+    stores[4].start()
+    for store in stores:
+        store.wait()
+
+
+def owners(dp, n_dp):
+    chips, chip, core = n_dp // 2, dp >> 1, dp & 1
+    out = []
     for hops in range(chips // 2 + 1):
         up, down = (chip + hops) % chips, (chip + chips - hops) % chips
         here = (down * (1 - core) + up * core) * 2
         there = (up * (1 - core) + down * core) * 2
-        places += [here + core, here + 1 - core, there + 1 - core, there + core]
-    places = places[:2] + places[4:-4] + [places[-4], places[-2]]
-    blocks = list(zip(pieces, places, strict=True))
-    copies = [
-        [
-            pltpu.make_async_copy(src.at[:, :, pl.ds(n * 256, 256)], w.at[at, :, :, pl.ds(n * 256, 256)], sems.at[n, i])
-            for i, (src, at) in enumerate(blocks)
-        ]
-        for n in range(3)
-    ]
-    for group in copies:
-        for c in group:
-            c.start()
+        out += [here + core, here + 1 - core, there + 1 - core, there + core]
+    return out[:2] + out[4:-4] + [out[-4], out[-2]]
+
+
+def expert_kernel(x_hbm, *refs):
+    pieces, (out_hbm, x_ref, w, xs, gs, gg, ug, out_ref, x_sems, sems, out_sems) = refs[:-11], refs[-11:]
+    sources = x_ref.shape[0]
+    main, extra = sources * 8, sources * 2
+    places = owners(lax.axis_index("dp"), len(pieces))
+    loads = stream(x_hbm, x_ref, x_sems, [(c * 512, 512) for c in range(5)])
+    for load in loads:
+        load.start()
+    copies = []
+    for n in range(3):
+        cols = pl.ds(n * 256, 256)
+        copies.append(
+            [
+                pltpu.make_async_copy(src.at[:, :, cols], w.at[at, :, :, cols], sems.at[n, i])
+                for i, (src, at) in enumerate(zip(pieces, places, strict=True))
+            ]
+        )
+    for c in copies[0]:
+        c.start()
+    stores = stream(out_ref, out_hbm, out_sems, [(q * 512, 512) for q in range(5)] + [(2560, 128)])
     for c in range(4):
+        loads[c].wait()
         cols = slice(c * 512, (c + 1) * 512)
         both = x_ref[:, :, cols].astype(F32)
         xs[0:main, cols] = both[:, :8].reshape(main, 512).astype(BF)
         gs[0:main, cols] = both[:, 8:].reshape(main, 512).astype(BF)
+    for c in copies[1]:
+        c.start()
+    loads[4].wait()
     both = x_ref[:, :, 2048:2560].astype(F32)
     dst, src = iota((main, main), 0), iota((main, main), 1)
     gather = onehot(src == ((dst % extra) >> 1) * 8 + (dst // extra) * 2 + (dst & 1))
@@ -109,6 +139,9 @@
     for n in range(3):
         for c in copies[n]:
             c.wait()
+        if n == 0:
+            for c in copies[2]:
+                c.start()
         cols = slice(n * 256, (n + 1) * 256)
         gate_pre = dot(xs[...], w[:, 0, :, cols].reshape(2048, 256))
         up_value = dot(xs[...], w[:, 1, :, cols].reshape(2048, 256))
@@ -127,15 +160,20 @@
     source = jnp.where(row < main, row >> 3, (row - main) >> 1)
     placed = dot(onehot(at == source * 8), placed).reshape(sources, 8, 128)
     out_ref[:, :, 2560:2688] = placed.astype(BF)
+    stores[5].start()
     tails = []
     for q in range(4):
         feats = slice(q * 4, (q + 1) * 4)
         row_grad = dot_nt(gg[...], w[feats, 0].reshape(512, 768)) + dot_nt(ug[...], w[feats, 1].reshape(512, 768))
         tails.append(row_grad[main:].astype(BF))
         out_ref[:, :, q * 512 : (q + 1) * 512] = row_grad[:main].reshape(sources, 8, 512).astype(BF)
+        stores[q].start()
     tail = jnp.concatenate(tails, axis=0)
     scatter = onehot(src == ((dst >> 1) & 3) * extra + (dst >> 3) * 2 + (dst & 1))
     out_ref[:, :, 2048:2560] = dot(scatter, tail).reshape(sources, 8, 512).astype(BF)
+    stores[4].start()
+    for store in stores:
+        store.wait()
 
 
 def combine_kernel(ids_ref, ids_t_ref, p_ref, back_ref, out_ref, prob_out_ref):
@@ -171,8 +209,8 @@
         out_ref[:, cols] = (p0 * rows[:toks] + p1 * rows[toks:]).astype(BF)
 
 
-def params():
-    return pltpu.CompilerParams(vmem_limit_bytes=56 * 1024 * 1024)
+def params(mib):
+    return pltpu.CompilerParams(vmem_limit_bytes=mib * 1024 * 1024)
 
 
 def cost(flops, size):
@@ -196,10 +234,21 @@
     experts = lax.axis_size("expert")
     n_dp = lax.axis_size("dp")
     ids = route_ids.T
+    vmem, hbm = pl.BlockSpec(memory_space=pltpu.VMEM), pl.BlockSpec(memory_space=pl.ANY)
     send = pl.pallas_call(
         pack_kernel,
+        in_specs=[hbm, hbm, hbm],
+        out_specs=hbm,
         out_shape=jax.ShapeDtypeStruct((experts, 16, 2560), BF),
-        compiler_params=params(),
+        scratch_shapes=[
+            pltpu.VMEM(ids.shape, I32),
+            pltpu.VMEM((toks, features), BF),
+            pltpu.VMEM((toks, features), BF),
+            pltpu.VMEM((experts, 16, 2560), BF),
+            pltpu.SemaphoreType.DMA((3,)),
+            pltpu.SemaphoreType.DMA((5,)),
+        ],
+        compiler_params=params(60),
         cost_estimate=cost(10**9, 4000000),
         name="pack_rows",
     )(ids, tokens, grad_out)
@@ -207,24 +256,29 @@
     own_w = pl.pallas_call(
         weights_kernel,
         out_shape=jax.ShapeDtypeStruct((3, 128, 768), BF),
-        compiler_params=params(),
+        compiler_params=params(20),
         cost_estimate=cost(10**8, 1200000),
         name="join_weights",
     )(gate_up, w_down)
     pieces = ring(own_w, n_dp)
     back = pl.pallas_call(
         expert_kernel,
-        in_specs=[pl.BlockSpec(memory_space=pltpu.VMEM)] + [pl.BlockSpec(memory_space=pl.ANY)] * len(pieces),
+        in_specs=[hbm] * (1 + len(pieces)),
+        out_specs=hbm,
         out_shape=jax.ShapeDtypeStruct((experts, 8, 2688), BF),
         scratch_shapes=[
+            pltpu.VMEM((experts, 16, 2560), BF),
             pltpu.VMEM((n_dp, 3, 128, 768), BF),
             pltpu.VMEM((experts * 10, features), BF),
             pltpu.VMEM((experts * 10, features), BF),
             pltpu.VMEM((experts * 10, 768), BF),
             pltpu.VMEM((experts * 10, 768), BF),
+            pltpu.VMEM((experts, 8, 2688), BF),
+            pltpu.SemaphoreType.DMA((5,)),
             pltpu.SemaphoreType.DMA((3, n_dp)),
+            pltpu.SemaphoreType.DMA((6,)),
         ],
-        compiler_params=params(),
+        compiler_params=params(60),
         cost_estimate=cost(6 * 10**9, 14000000),
         name="expert_rows",
     )(rows, *pieces)
@@ -232,7 +286,7 @@
     input_grad, prob_grad = pl.pallas_call(
         combine_kernel,
         out_shape=(jax.ShapeDtypeStruct((toks, features), BF), jax.ShapeDtypeStruct((2, toks), BF)),
-        compiler_params=params(),
+        compiler_params=params(20),
         cost_estimate=cost(2 * 10**9, 2000000),
         name="combine_rows",
     )(ids, route_ids, route_probs, back)

time: 144 us -> 136 us (0.944)
  Pallas kernels: 21.8 us -> 16.7 us
  waiting for transfers between devices: 43.2 us -> 47.3 us
  local copies, waits for them, and re-layouts: 5.99 us -> 2.26 us
  starting transfers between devices: 71.3 us -> 68.4 us
    unnamed x38 -> x40, local copies, waits for them, and re-layouts: 5.99 us -> 2.26 us
    all_to_all x1, waiting for transfers between devices: 0.01 us -> 3.61 us  [shards(): lax.all_to_all(send, 'expert', split_axis=0, concat_axis=0, tiled=True)]
    all_to_all x1, starting transfers between devices: 9.5 us -> 6.13 us  [shards(): lax.all_to_all(back, 'expert', split_axis=0, concat_axis=0, tiled=True)]
    pallas_call x1, Pallas kernels: 2.09 us -> 0.22 us  [shards(): pl.pallas_call(weights_kernel, out_shape=jax.ShapeDtypeStruct((3, 128, 76...]
    pallas_call x2, Pallas kernels: 16.5 us -> 14.7 us  [the longest x1 11.6 us: shards(): pl.pallas_call(expert_kernel, in_specs=[hbm] * (1 + len(pieces)), out_spe...]
  transfers between devices with their start and end apart: 17 -> 17, of which waited for: 6 -> 7; matrix products, arithmetic and copies ran while one was open for 1% -> 0% of each run, Pallas kernels for 1% -> 0%
where the time goes in v4:
time: 136 us
  starting transfers between devices  68.4 us (50%)
  waiting for transfers between devices  47.3 us (35%)
  Pallas kernels  16.7 us (12%)
  local copies, waits for them, and re-layouts  2.26 us (2%)
    all_to_all x1, waiting for transfers between devices, shards(): lax.all_to_all(back, 'expert', split_axis=0, concat_axis=0, tiled=True)  35.3 us
    ppermute x3, starting transfers between devices, ring(): lax.ppermute(first, 'dp', on)  15.9 us
    all_to_all x1, starting transfers between devices, shards(): lax.all_to_all(send, 'expert', split_axis=0, concat_axis=0, tiled=True)  13.4 us
    pallas_call x1, Pallas kernels, shards(): pl.pallas_call(expert_kernel, in_specs=[hbm] * (1 + len(pieces)), out_spe...  11.6 us
    ppermute x3, starting transfers between devices, ring(): lax.ppermute(second, 'dp', on)  10.1 us
    ppermute x3, starting transfers between devices, ring(): lax.ppermute(second, 'dp', swap)  7.22 us
    ppermute x3, waiting for transfers between devices, ring(): lax.ppermute(first, 'dp', on)  6.88 us
    all_to_all x1, starting transfers between devices, shards(): lax.all_to_all(back, 'expert', split_axis=0, concat_axis=0, tiled=True)  6.13 us
  transfers between devices with their start and end apart: 17, of which 7 were waited for; matrix products, arithmetic and copies ran while one was open for 0% of the time, Pallas kernels for 0%

profile of v4, /device:TPU:24, one launch (start us, length us, event | category | flops | bytes accessed | tf_op | source)
XLA Modules:
  0.0 135.7 jit_solution(1142227442405422444)
XLA Ops:
  0.6 3.1 %pack_rows.1 = bf16[32,16,2560]{2,1,0:T(8,128)(2,1)} custom-call(s32[2,128]{1,0:T(2,128)} %bitcast.2, bf16[128,2048]{1,0:T(8,128)(2,1)} %tok_hbm.1, bf16[128,2048]{1,0:T(8,128)(2,1)} %grad_hbm.1), custom_call_target="tpu_custom_call" | custom-call | flops 1000000000 | bytes 4000000 | tf_op jit(solution)/shard_map/pack_rows/pallas_call | solution.py:238
  3.7 0.0 copy-start.1
  3.8 0.0 copy-start.2
  3.8 13.4 %all-to-all-start = ((bf16[32,16,2560]{2,1,0:T(8,128)(2,1)}), bf16[32,16,2560]{2,1,0:T(8,128)(2,1)}, u32[]{:S(2)}, u32[]{:S(2)}) async-start(bf16[32,16,2560]{2,1,0:T(8,128)(2,1)} %pack_rows.1), calls=%async_computation | async-start | bytes 5242880 | tf_op jit(solution)/shard_map/all_to_all | solution.py:255
  17.2 0.2 join_weights.1.refs_0_
  17.5 1.9 %collective-permute-start = (bf16[3,128,768]{2,1,0:T(8,128)(2,1)S(1)}, bf16[3,128,768]{2,1,0:T(8,128)(2,1)S(1)}, u32[]{:S(2)}, u32[]{:S(2)}) collective-permute-start(bf16[3,128,768]{2,1,0:T(8,128)(2,1)S(1)} %join_weights.1.refs_0_), channel_id=1, source_target_pairs={{0,32},{32,0},{64,96},{96,64},{128,160},{160,128},{192,224},{224,1... | collective-permute-start | bytes 1769480 | tf_op jit(solution)/shard_map/ppermute | solution.py:223
  19.4 4.7 %collective-permute-start.1 = (bf16[3,128,768]{2,1,0:T(8,128)(2,1)S(1)}, bf16[3,128,768]{2,1,0:T(8,128)(2,1)S(1)}, u32[]{:S(2)}, u32[]{:S(2)}) collective-permute-start(bf16[3,128,768]{2,1,0:T(8,128)(2,1)S(1)} %join_weights.1.refs_0_), channel_id=1, source_target_pairs={{0,64},{32,480},{64,128},{96,32},{128,192},{160,96},{192,256},{224... | collective-permute-start | bytes 1769480 | tf_op jit(solution)/shard_map/ppermute | solution.py:226
  24.1 0.0 collective-permute-done.refs_1_
  24.1 2.6 %collective-permute-start.2 = (bf16[3,128,768]{2,1,0:T(8,128)(2,1)S(1)}, bf16[3,128,768]{2,1,0:T(8,128)(2,1)S(1)}, u32[]{:S(2)}, u32[]{:S(2)}) collective-permute-start(bf16[3,128,768]{2,1,0:T(8,128)(2,1)S(1)} %collective-permute-done.refs_1_), channel_id=1, source_target_pairs={{0,64},{32,480},{64,128},{96,32},{128,192},{160,96},{192,256},{224... | collective-permute-start | bytes 1769480 | tf_op jit(solution)/shard_map/ppermute | solution.py:226
  26.7 4.8 %collective-permute-done.1.refs_2_ = bf16[3,128,768]{2,1,0:T(8,128)(2,1)S(1)} collective-permute-done((bf16[3,128,768]{2,1,0:T(8,128)(2,1)S(1)}, bf16[3,128,768]{2,1,0:T(8,128)(2,1)S(1)}, u32[]{:S(2)}, u32[]{:S(2)}) %collective-permute-start.1) | collective-permute-done | bytes 589856 | tf_op jit(solution)/shard_map/ppermute | solution.py:226
  31.5 5.6 %collective-permute-start.5 = (bf16[3,128,768]{2,1,0:T(8,128)(2,1)S(1)}, bf16[3,128,768]{2,1,0:T(8,128)(2,1)S(1)}, u32[]{:S(2)}, u32[]{:S(2)}) collective-permute-start(bf16[3,128,768]{2,1,0:T(8,128)(2,1)S(1)} %collective-permute-done.1.refs_2_), channel_id=1, source_target_pairs={{0,64},{32,480},{64,128},{96,32},{128,192},{160,96},{192,256},{224... | collective-permute-start | bytes 1769480 | tf_op jit(solution)/shard_map/ppermute | solution.py:226
  37.1 0.7 collective-permute-done.2.refs_3_
  37.8 5.6 %collective-permute-start.6 = (bf16[3,128,768]{2,1,0:T(8,128)(2,1)S(1)}, bf16[3,128,768]{2,1,0:T(8,128)(2,1)S(1)}, u32[]{:S(2)}, u32[]{:S(2)}) collective-permute-start(bf16[3,128,768]{2,1,0:T(8,128)(2,1)S(1)} %collective-permute-done.2.refs_3_), channel_id=1, source_target_pairs={{0,64},{32,480},{64,128},{96,32},{128,192},{160,96},{192,256},{224... | collective-permute-start | bytes 1769480 | tf_op jit(solution)/shard_map/ppermute | solution.py:226
  43.4 1.1 collective-permute-done.5.refs_6_
  44.4 5.6 %collective-permute-start.9 = (bf16[3,128,768]{2,1,0:T(8,128)(2,1)S(1)}, bf16[3,128,768]{2,1,0:T(8,128)(2,1)S(1)}, u32[]{:S(2)}, u32[]{:S(2)}) collective-permute-start(bf16[3,128,768]{2,1,0:T(8,128)(2,1)S(1)} %collective-permute-done.5.refs_6_), channel_id=1, source_target_pairs={{0,64},{32,480},{64,128},{96,32},{128,192},{160,96},{192,256},{224... | collective-permute-start | bytes 1769480 | tf_op jit(solution)/shard_map/ppermute | solution.py:226
  50.0 1.9 %collective-permute-start.3 = (bf16[3,128,768]{2,1,0:T(8,128)(2,1)S(1)}, bf16[3,128,768]{2,1,0:T(8,128)(2,1)S(1)}, u32[]{:S(2)}, u32[]{:S(2)}) collective-permute-start(bf16[3,128,768]{2,1,0:T(8,128)(2,1)S(1)} %collective-permute-done.1.refs_2_), channel_id=1, source_target_pairs={{0,32},{32,0},{64,96},{96,64},{128,160},{160,128},{192,224},{224,1... | collective-permute-start | bytes 1769480 | tf_op jit(solution)/shard_map/ppermute | solution.py:227
  52.0 2.4 %collective-permute-start.4 = (bf16[3,128,768]{2,1,0:T(8,128)(2,1)S(1)}, bf16[3,128,768]{2,1,0:T(8,128)(2,1)S(1)}, u32[]{:S(2)}, u32[]{:S(2)}) collective-permute-start(bf16[3,128,768]{2,1,0:T(8,128)(2,1)S(1)} %collective-permute-done.2.refs_3_), channel_id=1, source_target_pairs={{0,32},{32,0},{64,96},{96,64},{128,160},{160,128},{192,224},{224,1... | collective-permute-start | bytes 1769480 | tf_op jit(solution)/shard_map/ppermute | solution.py:227
  54.4 0.0 collective-permute-done.6.refs_7_
  54.4 1.9 %collective-permute-start.10 = (bf16[3,128,768]{2,1,0:T(8,128)(2,1)S(1)}, bf16[3,128,768]{2,1,0:T(8,128)(2,1)S(1)}, u32[]{:S(2)}, u32[]{:S(2)}) collective-permute-start(bf16[3,128,768]{2,1,0:T(8,128)(2,1)S(1)} %collective-permute-done.6.refs_7_), channel_id=1, source_target_pairs={{0,64},{32,480},{64,128},{96,32},{128,192},{160,96},{192,256},{224... | collective-permute-start | bytes 1769480 | tf_op jit(solution)/shard_map/ppermute | solution.py:226
  56.4 1.1 collective-permute-done.9.refs_10_
  57.4 5.6 %collective-permute-start.13 = (bf16[3,128,768]{2,1,0:T(8,128)(2,1)S(1)}, bf16[3,128,768]{2,1,0:T(8,128)(2,1)S(1)}, u32[]{:S(2)}, u32[]{:S(2)}) collective-permute-start(bf16[3,128,768]{2,1,0:T(8,128)(2,1)S(1)} %collective-permute-done.9.refs_10_), channel_id=1, source_target_pairs={{0,64},{32,480},{64,128},{96,32},{128,192},{160,96},{192,256},{224... | collective-permute-start | bytes 1769480 | tf_op jit(solution)/shard_map/ppermute | solution.py:228
  63.0 1.9 %collective-permute-start.7 = (bf16[3,128,768]{2,1,0:T(8,128)(2,1)S(1)}, bf16[3,128,768]{2,1,0:T(8,128)(2,1)S(1)}, u32[]{:S(2)}, u32[]{:S(2)}) collective-permute-start(bf16[3,128,768]{2,1,0:T(8,128)(2,1)S(1)} %collective-permute-done.5.refs_6_), channel_id=1, source_target_pairs={{0,32},{32,0},{64,96},{96,64},{128,160},{160,128},{192,224},{224,1... | collective-permute-start | bytes 1769480 | tf_op jit(solution)/shard_map/ppermute | solution.py:227
  64.9 0.0 collective-permute-done.3.refs_4_
  65.0 2.4 %collective-permute-start.8 = (bf16[3,128,768]{2,1,0:T(8,128)(2,1)S(1)}, bf16[3,128,768]{2,1,0:T(8,128)(2,1)S(1)}, u32[]{:S(2)}, u32[]{:S(2)}) collective-permute-start(bf16[3,128,768]{2,1,0:T(8,128)(2,1)S(1)} %collective-permute-done.6.refs_7_), channel_id=1, source_target_pairs={{0,32},{32,0},{64,96},{96,64},{128,160},{160,128},{192,224},{224,1... | collective-permute-start | bytes 1769480 | tf_op jit(solution)/shard_map/ppermute | solution.py:227
  67.4 0.0 collective-permute-done.4.refs_5_
  67.4 1.9 %collective-permute-start.11 = (bf16[3,128,768]{2,1,0:T(8,128)(2,1)S(1)}, bf16[3,128,768]{2,1,0:T(8,128)(2,1)S(1)}, u32[]{:S(2)}, u32[]{:S(2)}) collective-permute-start(bf16[3,128,768]{2,1,0:T(8,128)(2,1)S(1)} %collective-permute-done.9.refs_10_), channel_id=1, source_target_pairs={{0,32},{32,0},{64,96},{96,64},{128,160},{160,128},{192,224},{224,1... | collective-permute-start | bytes 1769480 | tf_op jit(solution)/shard_map/ppermute | solution.py:227
  69.3 0.0 collective-permute-done.10.refs_11_
  69.3 2.4 %collective-permute-start.12 = (bf16[3,128,768]{2,1,0:T(8,128)(2,1)S(1)}, bf16[3,128,768]{2,1,0:T(8,128)(2,1)S(1)}, u32[]{:S(2)}, u32[]{:S(2)}) collective-permute-start(bf16[3,128,768]{2,1,0:T(8,128)(2,1)S(1)} %collective-permute-done.10.refs_11_), channel_id=1, source_target_pairs={{0,32},{32,0},{64,96},{96,64},{128,160},{160,128},{192,224},{224,1... | collective-permute-start | bytes 1769480 | tf_op jit(solution)/shard_map/ppermute | solution.py:227
  71.8 0.7 collective-permute-done.13.refs_14_
  72.5 2.4 %collective-permute-start.14 = (bf16[3,128,768]{2,1,0:T(8,128)(2,1)S(1)}, bf16[3,128,768]{2,1,0:T(8,128)(2,1)}, u32[]{:S(2)}, u32[]{:S(2)}) collective-permute-start(bf16[3,128,768]{2,1,0:T(8,128)(2,1)S(1)} %collective-permute-done.13.refs_14_), channel_id=1, source_target_pairs={{0,32},{32,0},{64,96},{96,64},{128,160},{160,128},{192,224},{224,1... | collective-permute-start | bytes 1769480 | tf_op jit(solution)/shard_map/ppermute | solution.py:229
  74.9 0.0 collective-permute-done.7.refs_8_
  74.9 0.0 collective-permute-done.8.refs_9_
  74.9 0.0 collective-permute-done.11.refs_12_
  75.0 0.0 collective-permute-done.12.refs_13_
  75.0 0.7 copy-done.15
  75.7 0.2 copy-done.16
  75.9 0.2 copy-done.17
  76.2 0.8 copy-done.18
  77.0 0.0 collective-permute-done.14.refs_15_
  77.0 3.6 %all-to-all-done.x_hbm = bf16[32,16,2560]{2,1,0:T(8,128)(2,1)} async-done(((bf16[32,16,2560]{2,1,0:T(8,128)(2,1)}), bf16[32,16,2560]{2,1,0:T(8,128)(2,1)}, u32[]{:S(2)}, u32[]{:S(2)}) %all-to-all-start) | async-done | bytes 2621472 | tf_op jit(solution)/shard_map/all_to_all | solution.py:255
  80.6 11.6 %expert_rows.1 = bf16[32,8,2688]{2,1,0:T(8,128)(2,1)} custom-call(bf16[32,16,2560]{2,1,0:T(8,128)(2,1)} %all-to-all-done.x_hbm, bf16[3,128,768]{2,1,0:T(8,128)(2,1)} %copy-done, bf16[3,128,768]{2,1,0:T(8,128)(2,1)} %copy-done.5, bf16[3,128,768]{2,1,0:T(8,128)(2,1)} %copy-done.6, bf16[3,128,768]{2,1,0:T(8,128)(2,1)} %copy-done.7, ...), custom_call_target="tpu_custom_call" | custom-call | flops 6000000000 | bytes 14000000 | tf_op jit(solution)/shard_map/expert_rows/pallas_call | solution.py:264
  92.2 0.0 copy-start.3
  92.2 0.0 copy-start.4
  92.2 6.1 %all-to-all-start.1 = ((bf16[32,8,2688]{2,1,0:T(8,128)(2,1)}), bf16[32,8,2688]{2,1,0:T(8,128)(2,1)S(1)}, u32[]{:S(2)}, u32[]{:S(2)}) async-start(bf16[32,8,2688]{2,1,0:T(8,128)(2,1)} %expert_rows.1), calls=%async_computation.1 | async-start | bytes 2752512 | tf_op jit(solution)/shard_map/all_to_all | solution.py:285
  98.4 0.1 copy.8.ids_t_ref
  98.5 0.1 copy.9.p_ref
  98.6 35.3 %all-to-all-done.1.back_ref = bf16[32,8,2688]{2,1,0:T(8,128)(2,1)S(1)} async-done(((bf16[32,8,2688]{2,1,0:T(8,128)(2,1)}), bf16[32,8,2688]{2,1,0:T(8,128)(2,1)S(1)}, u32[]{:S(2)}, u32[]{:S(2)}) %all-to-all-start.1) | async-done | bytes 1376288 | tf_op jit(solution)/shard_map/all_to_all | solution.py:285
  133.9 1.8 %combine_rows.1 = (bf16[128,2048]{1,0:T(8,128)(2,1)}, bf16[2,128]{1,0:T(2,128)(2,1)}) custom-call(s32[2,128]{1,0:T(2,128)S(1)} %bitcast.3, s32[128,2]{1,0:T(8,128)S(1)} %copy.8.ids_t_ref, f32[128,2]{1,0:T(8,128)S(1)} %copy.9.p_ref, bf16[32,8,2688]{2,1,0:T(8,128)(2,1)S(1)} %all-to-all-done.1.back_ref), custom_call_target="tpu_custom_call" | custom-call | flops 2000000000 | bytes 2000000 | tf_op jit(solution)/shard_map/combine_rows/pallas_call | solution.py:286
  (30 shorter events, 0.1 us)
Async XLA Ops:
  3.7 13.5 %copy-start.1 = (bf16[1,2,128,768]{3,2,1,0:T(8,128)(2,1)S(1)}, bf16[1,2,128,768]{3,2,1,0:T(8,128)(2,1)}, u32[]{:S(2)}) copy-start(bf16[1,2,128,768]{3,2,1,0:T(8,128)(2,1)} %gu_ref.1) | copy-start | bytes 1179652
  3.8 13.5 %copy-start.2 = (bf16[1,768,128]{2,1,0:T(8,128)(2,1)S(1)}, bf16[1,768,128]{2,1,0:T(8,128)(2,1)}, u32[]{:S(2)}) copy-start(bf16[1,768,128]{2,1,0:T(8,128)(2,1)} %wd_ref.1) | copy-start | bytes 589828
  3.8 76.8 %all-to-all-start = ((bf16[32,16,2560]{2,1,0:T(8,128)(2,1)}), bf16[32,16,2560]{2,1,0:T(8,128)(2,1)}, u32[]{:S(2)}, u32[]{:S(2)}) async-start(bf16[32,16,2560]{2,1,0:T(8,128)(2,1)} %pack_rows.1), calls=%async_computation | async-start | bytes 5242880 | tf_op jit(solution)/shard_map/all_to_all | solution.py:255
  17.4 63.1 %copy-start = (bf16[3,128,768]{2,1,0:T(8,128)(2,1)}, bf16[3,128,768]{2,1,0:T(8,128)(2,1)S(1)}, u32[]{:S(2)}) copy-start(bf16[3,128,768]{2,1,0:T(8,128)(2,1)S(1)} %join_weights.1.refs_0_) | copy-start | bytes 1769476
  17.5 6.6 %collective-permute-start = (bf16[3,128,768]{2,1,0:T(8,128)(2,1)S(1)}, bf16[3,128,768]{2,1,0:T(8,128)(2,1)S(1)}, u32[]{:S(2)}, u32[]{:S(2)}) collective-permute-start(bf16[3,128,768]{2,1,0:T(8,128)(2,1)S(1)} %join_weights.1.refs_0_), channel_id=1, source_target_pairs={{0,32},{32,0},{64,96},{96,64},{128,160},{160,128},{192,224},{224,1... | collective-permute-start | bytes 1769480 | tf_op jit(solution)/shard_map/ppermute | solution.py:223
  19.4 12.1 %collective-permute-start.1 = (bf16[3,128,768]{2,1,0:T(8,128)(2,1)S(1)}, bf16[3,128,768]{2,1,0:T(8,128)(2,1)S(1)}, u32[]{:S(2)}, u32[]{:S(2)}) collective-permute-start(bf16[3,128,768]{2,1,0:T(8,128)(2,1)S(1)} %join_weights.1.refs_0_), channel_id=1, source_target_pairs={{0,64},{32,480},{64,128},{96,32},{128,192},{160,96},{192,256},{224... | collective-permute-start | bytes 1769480 | tf_op jit(solution)/shard_map/ppermute | solution.py:226
  24.1 56.5 %copy-start.5 = (bf16[3,128,768]{2,1,0:T(8,128)(2,1)}, bf16[3,128,768]{2,1,0:T(8,128)(2,1)S(1)}, u32[]{:S(2)}) copy-start(bf16[3,128,768]{2,1,0:T(8,128)(2,1)S(1)} %collective-permute-done.refs_1_) | copy-start | bytes 1769476
  24.1 13.7 %collective-permute-start.2 = (bf16[3,128,768]{2,1,0:T(8,128)(2,1)S(1)}, bf16[3,128,768]{2,1,0:T(8,128)(2,1)S(1)}, u32[]{:S(2)}, u32[]{:S(2)}) collective-permute-start(bf16[3,128,768]{2,1,0:T(8,128)(2,1)S(1)} %collective-permute-done.refs_1_), channel_id=1, source_target_pairs={{0,64},{32,480},{64,128},{96,32},{128,192},{160,96},{192,256},{224... | collective-permute-start | bytes 1769480 | tf_op jit(solution)/shard_map/ppermute | solution.py:226
  31.5 49.1 %copy-start.6 = (bf16[3,128,768]{2,1,0:T(8,128)(2,1)}, bf16[3,128,768]{2,1,0:T(8,128)(2,1)S(1)}, u32[]{:S(2)}) copy-start(bf16[3,128,768]{2,1,0:T(8,128)(2,1)S(1)} %collective-permute-done.1.refs_2_) | copy-start | bytes 1769476
  31.5 13.0 %collective-permute-start.5 = (bf16[3,128,768]{2,1,0:T(8,128)(2,1)S(1)}, bf16[3,128,768]{2,1,0:T(8,128)(2,1)S(1)}, u32[]{:S(2)}, u32[]{:S(2)}) collective-permute-start(bf16[3,128,768]{2,1,0:T(8,128)(2,1)S(1)} %collective-permute-done.1.refs_2_), channel_id=1, source_target_pairs={{0,64},{32,480},{64,128},{96,32},{128,192},{160,96},{192,256},{224... | collective-permute-start | bytes 1769480 | tf_op jit(solution)/shard_map/ppermute | solution.py:226
  37.8 42.8 %copy-start.7 = (bf16[3,128,768]{2,1,0:T(8,128)(2,1)}, bf16[3,128,768]{2,1,0:T(8,128)(2,1)S(1)}, u32[]{:S(2)}) copy-start(bf16[3,128,768]{2,1,0:T(8,128)(2,1)S(1)} %collective-permute-done.2.refs_3_) | copy-start | bytes 1769476
  37.8 16.6 %collective-permute-start.6 = (bf16[3,128,768]{2,1,0:T(8,128)(2,1)S(1)}, bf16[3,128,768]{2,1,0:T(8,128)(2,1)S(1)}, u32[]{:S(2)}, u32[]{:S(2)}) collective-permute-start(bf16[3,128,768]{2,1,0:T(8,128)(2,1)S(1)} %collective-permute-done.2.refs_3_), channel_id=1, source_target_pairs={{0,64},{32,480},{64,128},{96,32},{128,192},{160,96},{192,256},{224... | collective-permute-start | bytes 1769480 | tf_op jit(solution)/shard_map/ppermute | solution.py:226
  44.4 36.2 %copy-start.8 = (bf16[3,128,768]{2,1,0:T(8,128)(2,1)}, bf16[3,128,768]{2,1,0:T(8,128)(2,1)S(1)}, u32[]{:S(2)}) copy-start(bf16[3,128,768]{2,1,0:T(8,128)(2,1)S(1)} %collective-permute-done.5.refs_6_) | copy-start | bytes 1769476
  44.4 13.0 %collective-permute-start.9 = (bf16[3,128,768]{2,1,0:T(8,128)(2,1)S(1)}, bf16[3,128,768]{2,1,0:T(8,128)(2,1)S(1)}, u32[]{:S(2)}, u32[]{:S(2)}) collective-permute-start(bf16[3,128,768]{2,1,0:T(8,128)(2,1)S(1)} %collective-permute-done.5.refs_6_), channel_id=1, source_target_pairs={{0,64},{32,480},{64,128},{96,32},{128,192},{160,96},{192,256},{224... | collective-permute-start | bytes 1769480 | tf_op jit(solution)/shard_map/ppermute | solution.py:226
  50.0 14.9 %collective-permute-start.3 = (bf16[3,128,768]{2,1,0:T(8,128)(2,1)S(1)}, bf16[3,128,768]{2,1,0:T(8,128)(2,1)S(1)}, u32[]{:S(2)}, u32[]{:S(2)}) collective-permute-start(bf16[3,128,768]{2,1,0:T(8,128)(2,1)S(1)} %collective-permute-done.1.refs_2_), channel_id=1, source_target_pairs={{0,32},{32,0},{64,96},{96,64},{128,160},{160,128},{192,224},{224,1... | collective-permute-start | bytes 1769480 | tf_op jit(solution)/shard_map/ppermute | solution.py:227
  52.0 15.4 %collective-permute-start.4 = (bf16[3,128,768]{2,1,0:T(8,128)(2,1)S(1)}, bf16[3,128,768]{2,1,0:T(8,128)(2,1)S(1)}, u32[]{:S(2)}, u32[]{:S(2)}) collective-permute-start(bf16[3,128,768]{2,1,0:T(8,128)(2,1)S(1)} %collective-permute-done.2.refs_3_), channel_id=1, source_target_pairs={{0,32},{32,0},{64,96},{96,64},{128,160},{160,128},{192,224},{224,1... | collective-permute-start | bytes 1769480 | tf_op jit(solution)/shard_map/ppermute | solution.py:227
  54.4 26.2 %copy-start.9 = (bf16[3,128,768]{2,1,0:T(8,128)(2,1)}, bf16[3,128,768]{2,1,0:T(8,128)(2,1)S(1)}, u32[]{:S(2)}) copy-start(bf16[3,128,768]{2,1,0:T(8,128)(2,1)S(1)} %collective-permute-done.6.refs_7_) | copy-start | bytes 1769476
  54.4 14.9 %collective-permute-start.10 = (bf16[3,128,768]{2,1,0:T(8,128)(2,1)S(1)}, bf16[3,128,768]{2,1,0:T(8,128)(2,1)S(1)}, u32[]{:S(2)}, u32[]{:S(2)}) collective-permute-start(bf16[3,128,768]{2,1,0:T(8,128)(2,1)S(1)} %collective-permute-done.6.refs_7_), channel_id=1, source_target_pairs={{0,64},{32,480},{64,128},{96,32},{128,192},{160,96},{192,256},{224... | collective-permute-start | bytes 1769480 | tf_op jit(solution)/shard_map/ppermute | solution.py:226
  57.4 17.5 %copy-start.10 = (bf16[3,128,768]{2,1,0:T(8,128)(2,1)}, bf16[3,128,768]{2,1,0:T(8,128)(2,1)S(1)}, u32[]{:S(2)}) copy-start(bf16[3,128,768]{2,1,0:T(8,128)(2,1)S(1)} %collective-permute-done.9.refs_10_) | copy-start | bytes 1769476
  57.4 15.1 %collective-permute-start.13 = (bf16[3,128,768]{2,1,0:T(8,128)(2,1)S(1)}, bf16[3,128,768]{2,1,0:T(8,128)(2,1)S(1)}, u32[]{:S(2)}, u32[]{:S(2)}) collective-permute-start(bf16[3,128,768]{2,1,0:T(8,128)(2,1)S(1)} %collective-permute-done.9.refs_10_), channel_id=1, source_target_pairs={{0,64},{32,480},{64,128},{96,32},{128,192},{160,96},{192,256},{224... | collective-permute-start | bytes 1769480 | tf_op jit(solution)/shard_map/ppermute | solution.py:228
  63.0 11.9 %collective-permute-start.7 = (bf16[3,128,768]{2,1,0:T(8,128)(2,1)S(1)}, bf16[3,128,768]{2,1,0:T(8,128)(2,1)S(1)}, u32[]{:S(2)}, u32[]{:S(2)}) collective-permute-start(bf16[3,128,768]{2,1,0:T(8,128)(2,1)S(1)} %collective-permute-done.5.refs_6_), channel_id=1, source_target_pairs={{0,32},{32,0},{64,96},{96,64},{128,160},{160,128},{192,224},{224,1... | collective-permute-start | bytes 1769480 | tf_op jit(solution)/shard_map/ppermute | solution.py:227
  65.0 10.0 %copy-start.11 = (bf16[3,128,768]{2,1,0:T(8,128)(2,1)}, bf16[3,128,768]{2,1,0:T(8,128)(2,1)S(1)}, u32[]{:S(2)}) copy-start(bf16[3,128,768]{2,1,0:T(8,128)(2,1)S(1)} %collective-permute-done.3.refs_4_) | copy-start | bytes 1769476
  65.0 9.9 %collective-permute-start.8 = (bf16[3,128,768]{2,1,0:T(8,128)(2,1)S(1)}, bf16[3,128,768]{2,1,0:T(8,128)(2,1)S(1)}, u32[]{:S(2)}, u32[]{:S(2)}) collective-permute-start(bf16[3,128,768]{2,1,0:T(8,128)(2,1)S(1)} %collective-permute-done.6.refs_7_), channel_id=1, source_target_pairs={{0,32},{32,0},{64,96},{96,64},{128,160},{160,128},{192,224},{224,1... | collective-permute-start | bytes 1769480 | tf_op jit(solution)/shard_map/ppermute | solution.py:227
  67.4 7.6 %copy-start.12 = (bf16[3,128,768]{2,1,0:T(8,128)(2,1)}, bf16[3,128,768]{2,1,0:T(8,128)(2,1)S(1)}, u32[]{:S(2)}) copy-start(bf16[3,128,768]{2,1,0:T(8,128)(2,1)S(1)} %collective-permute-done.4.refs_5_) | copy-start | bytes 1769476
  67.4 7.5 %collective-permute-start.11 = (bf16[3,128,768]{2,1,0:T(8,128)(2,1)S(1)}, bf16[3,128,768]{2,1,0:T(8,128)(2,1)S(1)}, u32[]{:S(2)}, u32[]{:S(2)}) collective-permute-start(bf16[3,128,768]{2,1,0:T(8,128)(2,1)S(1)} %collective-permute-done.9.refs_10_), channel_id=1, source_target_pairs={{0,32},{32,0},{64,96},{96,64},{128,160},{160,128},{192,224},{224,1... | collective-permute-start | bytes 1769480 | tf_op jit(solution)/shard_map/ppermute | solution.py:227
  69.3 5.6 %copy-start.13 = (bf16[3,128,768]{2,1,0:T(8,128)(2,1)}, bf16[3,128,768]{2,1,0:T(8,128)(2,1)S(1)}, u32[]{:S(2)}) copy-start(bf16[3,128,768]{2,1,0:T(8,128)(2,1)S(1)} %collective-permute-done.10.refs_11_) | copy-start | bytes 1769476
  69.3 5.6 %collective-permute-start.12 = (bf16[3,128,768]{2,1,0:T(8,128)(2,1)S(1)}, bf16[3,128,768]{2,1,0:T(8,128)(2,1)S(1)}, u32[]{:S(2)}, u32[]{:S(2)}) collective-permute-start(bf16[3,128,768]{2,1,0:T(8,128)(2,1)S(1)} %collective-permute-done.10.refs_11_), channel_id=1, source_target_pairs={{0,32},{32,0},{64,96},{96,64},{128,160},{160,128},{192,224},{224,1... | collective-permute-start | bytes 1769480 | tf_op jit(solution)/shard_map/ppermute | solution.py:227
  72.5 2.5 %copy-start.14 = (bf16[3,128,768]{2,1,0:T(8,128)(2,1)}, bf16[3,128,768]{2,1,0:T(8,128)(2,1)S(1)}, u32[]{:S(2)}) copy-start(bf16[3,128,768]{2,1,0:T(8,128)(2,1)S(1)} %collective-permute-done.13.refs_14_) | copy-start | bytes 1769476
  72.5 4.5 %collective-permute-start.14 = (bf16[3,128,768]{2,1,0:T(8,128)(2,1)S(1)}, bf16[3,128,768]{2,1,0:T(8,128)(2,1)}, u32[]{:S(2)}, u32[]{:S(2)}) collective-permute-start(bf16[3,128,768]{2,1,0:T(8,128)(2,1)S(1)} %collective-permute-done.13.refs_14_), channel_id=1, source_target_pairs={{0,32},{32,0},{64,96},{96,64},{128,160},{160,128},{192,224},{224,1... | collective-permute-start | bytes 1769480 | tf_op jit(solution)/shard_map/ppermute | solution.py:229
  74.9 0.8 copy-start.15
  74.9 1.0 copy-start.16
  74.9 1.2 copy-start.17
  76.1 0.8 copy-start.18
  92.2 6.2 %copy-start.3 = (s32[128,2]{0,1:T(2,128)S(1)}, s32[128,2]{0,1:T(2,128)}, u32[]{:S(2)}) copy-start(s32[128,2]{0,1:T(2,128)} %param.8) | copy-start | bytes 3076
  92.2 6.3 %copy-start.4 = (f32[128,2]{0,1:T(2,128)S(1)}, f32[128,2]{0,1:T(2,128)}, u32[]{:S(2)}) copy-start(f32[128,2]{0,1:T(2,128)} %param.9) | copy-start | bytes 3076
  92.2 41.7 %all-to-all-start.1 = ((bf16[32,8,2688]{2,1,0:T(8,128)(2,1)}), bf16[32,8,2688]{2,1,0:T(8,128)(2,1)S(1)}, u32[]{:S(2)}, u32[]{:S(2)}) async-start(bf16[32,8,2688]{2,1,0:T(8,128)(2,1)} %expert_rows.1), calls=%async_computation.1 | async-start | bytes 2752512 | tf_op jit(solution)/shard_map/all_to_all | solution.py:285

commit v5 on v4

--- a/solution.py
+++ b/solution.py
@@ -47,14 +47,14 @@
     return jnp.concatenate([x[:, q * 512 : (q + 1) * 512] for q in range(4)], axis=0)
 
 
-def stream(src, dst, sems, columns):
+def stream(src, dst, sem, columns):
     return [
-        pltpu.make_async_copy(src.at[:, :, pl.ds(at, size)], dst.at[:, :, pl.ds(at, size)], sems.at[i])
-        for i, (at, size) in enumerate(columns)
+        pltpu.make_async_copy(src.at[:, :, pl.ds(at, size)], dst.at[:, :, pl.ds(at, size)], sem)
+        for at, size in columns
     ]
 
 
-def pack_kernel(ids_hbm, tok_hbm, grad_hbm, out_hbm, ids_ref, tok_ref, grad_ref, out_ref, sems, out_sems):
+def pack_kernel(ids_hbm, tok_hbm, grad_hbm, out_hbm, ids_ref, tok_ref, grad_ref, out_ref, sems, out_sem):
     refs = (tok_ref, grad_ref)
     ids_load = pltpu.make_async_copy(ids_hbm, ids_ref, sems.at[2])
     ids_load.start()
@@ -75,7 +75,7 @@
     picks = jnp.concatenate([jnp.where((row & 7) >> 1 == q, late, 0.0).astype(BF) for q in range(4)], axis=1)
     for load in loads:
         load.wait()
-    stores = stream(out_ref, out_hbm, out_sems, [(c * 512, 512) for c in range(5)])
+    stores = stream(out_ref, out_hbm, out_sem, [(c * 512, 512) for c in range(5)])
     for c in range(4):
         cols = slice(c * 512, (c + 1) * 512)
         parts = [dot(pick, ref[:, cols]).reshape(experts, 8, 512) for ref in refs]
@@ -84,8 +84,7 @@
     parts = [dot(picks, quarters(ref[...])).reshape(experts, 8, 512) for ref in refs]
     out_ref[:, :, 2048:2560] = jnp.concatenate(parts, axis=1).astype(BF)
     stores[4].start()
-    for store in stores:
-        store.wait()
+    pltpu.make_async_copy(out_ref, out_hbm, out_sem).wait()
 
 
 def owners(dp, n_dp):
@@ -100,11 +99,11 @@
 
 
 def expert_kernel(x_hbm, *refs):
-    pieces, (out_hbm, x_ref, w, xs, gs, gg, ug, out_ref, x_sems, sems, out_sems) = refs[:-11], refs[-11:]
+    pieces, (out_hbm, x_ref, w, xs, gs, gg, ug, out_ref, x_sems, sems, out_sem) = refs[:-11], refs[-11:]
     sources = x_ref.shape[0]
     main, extra = sources * 8, sources * 2
     places = owners(lax.axis_index("dp"), len(pieces))
-    loads = stream(x_hbm, x_ref, x_sems, [(c * 512, 512) for c in range(5)])
+    loads = [pltpu.make_async_copy(x_hbm.at[:, :, pl.ds(c * 512, 512)], x_ref.at[:, :, pl.ds(c * 512, 512)], x_sems.at[c]) for c in range(5)]
     for load in loads:
         load.start()
     copies = []
@@ -112,13 +111,13 @@
         cols = pl.ds(n * 256, 256)
         copies.append(
             [
-                pltpu.make_async_copy(src.at[:, :, cols], w.at[at, :, :, cols], sems.at[n, i])
-                for i, (src, at) in enumerate(zip(pieces, places, strict=True))
+                pltpu.make_async_copy(src.at[:, :, cols], w.at[at, :, :, cols], sems.at[n])
+                for src, at in zip(pieces, places, strict=True)
             ]
         )
     for c in copies[0]:
         c.start()
-    stores = stream(out_ref, out_hbm, out_sems, [(q * 512, 512) for q in range(5)] + [(2560, 128)])
+    stores = stream(out_ref, out_hbm, out_sem, [(q * 512, 512) for q in range(5)] + [(2560, 128)])
     for c in range(4):
         loads[c].wait()
         cols = slice(c * 512, (c + 1) * 512)
@@ -137,8 +136,8 @@
             to[main : main + extra, q * 512 : (q + 1) * 512] = tail[q * extra : (q + 1) * extra]
     prob = jnp.zeros((main + extra, 1), F32)
     for n in range(3):
-        for c in copies[n]:
-            c.wait()
+        third = w.at[:, :, :, pl.ds(n * 256, 256)]
+        pltpu.make_async_copy(third, third, sems.at[n]).wait()
         if n == 0:
             for c in copies[2]:
                 c.start()
@@ -172,8 +171,7 @@
     scatter = onehot(src == ((dst >> 1) & 3) * extra + (dst >> 3) * 2 + (dst & 1))
     out_ref[:, :, 2048:2560] = dot(scatter, tail).reshape(sources, 8, 512).astype(BF)
     stores[4].start()
-    for store in stores:
-        store.wait()
+    pltpu.make_async_copy(out_ref, out_hbm, out_sem).wait()
 
 
 def combine_kernel(ids_ref, ids_t_ref, p_ref, back_ref, out_ref, prob_out_ref):
@@ -246,7 +244,7 @@
             pltpu.VMEM((toks, features), BF),
             pltpu.VMEM((experts, 16, 2560), BF),
             pltpu.SemaphoreType.DMA((3,)),
-            pltpu.SemaphoreType.DMA((5,)),
+            pltpu.SemaphoreType.DMA,
         ],
         compiler_params=params(60),
         cost_estimate=cost(10**9, 4000000),
@@ -275,8 +273,8 @@
             pltpu.VMEM((experts * 10, 768), BF),
             pltpu.VMEM((experts, 8, 2688), BF),
             pltpu.SemaphoreType.DMA((5,)),
-            pltpu.SemaphoreType.DMA((3, n_dp)),
-            pltpu.SemaphoreType.DMA((6,)),
+            pltpu.SemaphoreType.DMA((3,)),
+            pltpu.SemaphoreType.DMA,
         ],
         compiler_params=params(60),
         cost_estimate=cost(6 * 10**9, 14000000),

time: 136 us -> 136 us (level)
  no operation moved by 1% of the time
where the time goes in v5:
time: 136 us; the launch traced here: 135 us
  starting transfers between devices  68.4 us (50%)
  waiting for transfers between devices  47.3 us (35%)
  Pallas kernels  16.2 us (12%)
  local copies, waits for them, and re-layouts  2.26 us (2%)
    all_to_all x1, waiting for transfers between devices, shards(): lax.all_to_all(back, 'expert', split_axis=0, concat_axis=0, tiled=True)  35.3 us
    ppermute x3, starting transfers between devices, ring(): lax.ppermute(first, 'dp', on)  15.9 us
    all_to_all x1, starting transfers between devices, shards(): lax.all_to_all(send, 'expert', split_axis=0, concat_axis=0, tiled=True)  13.4 us
    pallas_call x1, Pallas kernels, shards(): pl.pallas_call(expert_kernel, in_specs=[hbm] * (1 + len(pieces)), out_spe...  11.1 us
    ppermute x3, starting transfers between devices, ring(): lax.ppermute(second, 'dp', on)  10.1 us
    ppermute x3, starting transfers between devices, ring(): lax.ppermute(second, 'dp', swap)  7.22 us
    ppermute x3, waiting for transfers between devices, ring(): lax.ppermute(first, 'dp', on)  6.88 us
    all_to_all x1, starting transfers between devices, shards(): lax.all_to_all(back, 'expert', split_axis=0, concat_axis=0, tiled=True)  6.13 us
  transfers between devices with their start and end apart: 17, of which 7 were waited for; matrix products, arithmetic and copies ran while one was open for 0% of the time, Pallas kernels for 0%

profile of v5, /device:TPU:24, one launch (start us, length us, event | category | flops | bytes accessed | tf_op | source)
XLA Modules:
  0.0 135.2 jit_solution(12913577497042736198)
XLA Ops:
  0.6 3.1 %pack_rows.1 = bf16[32,16,2560]{2,1,0:T(8,128)(2,1)} custom-call(s32[2,128]{1,0:T(2,128)} %bitcast.2, bf16[128,2048]{1,0:T(8,128)(2,1)} %tok_hbm.1, bf16[128,2048]{1,0:T(8,128)(2,1)} %grad_hbm.1), custom_call_target="tpu_custom_call" | custom-call | flops 1000000000 | bytes 4000000 | tf_op jit(solution)/shard_map/pack_rows/pallas_call | solution.py:236
  3.7 0.0 copy-start.1
  3.7 0.0 copy-start.2
  3.7 13.4 %all-to-all-start = ((bf16[32,16,2560]{2,1,0:T(8,128)(2,1)}), bf16[32,16,2560]{2,1,0:T(8,128)(2,1)}, u32[]{:S(2)}, u32[]{:S(2)}) async-start(bf16[32,16,2560]{2,1,0:T(8,128)(2,1)} %pack_rows.1), calls=%async_computation | async-start | bytes 5242880 | tf_op jit(solution)/shard_map/all_to_all | solution.py:253
  17.2 0.2 join_weights.1.refs_0_
  17.4 1.9 %collective-permute-start = (bf16[3,128,768]{2,1,0:T(8,128)(2,1)S(1)}, bf16[3,128,768]{2,1,0:T(8,128)(2,1)S(1)}, u32[]{:S(2)}, u32[]{:S(2)}) collective-permute-start(bf16[3,128,768]{2,1,0:T(8,128)(2,1)S(1)} %join_weights.1.refs_0_), channel_id=1, source_target_pairs={{0,32},{32,0},{64,96},{96,64},{128,160},{160,128},{192,224},{224,1... | collective-permute-start | bytes 1769480 | tf_op jit(solution)/shard_map/ppermute | solution.py:221
  19.3 4.7 %collective-permute-start.1 = (bf16[3,128,768]{2,1,0:T(8,128)(2,1)S(1)}, bf16[3,128,768]{2,1,0:T(8,128)(2,1)S(1)}, u32[]{:S(2)}, u32[]{:S(2)}) collective-permute-start(bf16[3,128,768]{2,1,0:T(8,128)(2,1)S(1)} %join_weights.1.refs_0_), channel_id=1, source_target_pairs={{0,64},{32,480},{64,128},{96,32},{128,192},{160,96},{192,256},{224... | collective-permute-start | bytes 1769480 | tf_op jit(solution)/shard_map/ppermute | solution.py:224
  24.0 0.0 collective-permute-done.refs_1_
  24.1 2.6 %collective-permute-start.2 = (bf16[3,128,768]{2,1,0:T(8,128)(2,1)S(1)}, bf16[3,128,768]{2,1,0:T(8,128)(2,1)S(1)}, u32[]{:S(2)}, u32[]{:S(2)}) collective-permute-start(bf16[3,128,768]{2,1,0:T(8,128)(2,1)S(1)} %collective-permute-done.refs_1_), channel_id=1, source_target_pairs={{0,64},{32,480},{64,128},{96,32},{128,192},{160,96},{192,256},{224... | collective-permute-start | bytes 1769480 | tf_op jit(solution)/shard_map/ppermute | solution.py:224
  26.7 4.8 %collective-permute-done.1.refs_2_ = bf16[3,128,768]{2,1,0:T(8,128)(2,1)S(1)} collective-permute-done((bf16[3,128,768]{2,1,0:T(8,128)(2,1)S(1)}, bf16[3,128,768]{2,1,0:T(8,128)(2,1)S(1)}, u32[]{:S(2)}, u32[]{:S(2)}) %collective-permute-start.1) | collective-permute-done | bytes 589856 | tf_op jit(solution)/shard_map/ppermute | solution.py:224
  31.4 5.6 %collective-permute-start.5 = (bf16[3,128,768]{2,1,0:T(8,128)(2,1)S(1)}, bf16[3,128,768]{2,1,0:T(8,128)(2,1)S(1)}, u32[]{:S(2)}, u32[]{:S(2)}) collective-permute-start(bf16[3,128,768]{2,1,0:T(8,128)(2,1)S(1)} %collective-permute-done.1.refs_2_), channel_id=1, source_target_pairs={{0,64},{32,480},{64,128},{96,32},{128,192},{160,96},{192,256},{224... | collective-permute-start | bytes 1769480 | tf_op jit(solution)/shard_map/ppermute | solution.py:224
  37.0 0.7 collective-permute-done.2.refs_3_
  37.7 5.6 %collective-permute-start.6 = (bf16[3,128,768]{2,1,0:T(8,128)(2,1)S(1)}, bf16[3,128,768]{2,1,0:T(8,128)(2,1)S(1)}, u32[]{:S(2)}, u32[]{:S(2)}) collective-permute-start(bf16[3,128,768]{2,1,0:T(8,128)(2,1)S(1)} %collective-permute-done.2.refs_3_), channel_id=1, source_target_pairs={{0,64},{32,480},{64,128},{96,32},{128,192},{160,96},{192,256},{224... | collective-permute-start | bytes 1769480 | tf_op jit(solution)/shard_map/ppermute | solution.py:224
  43.3 1.1 collective-permute-done.5.refs_6_
  44.4 5.6 %collective-permute-start.9 = (bf16[3,128,768]{2,1,0:T(8,128)(2,1)S(1)}, bf16[3,128,768]{2,1,0:T(8,128)(2,1)S(1)}, u32[]{:S(2)}, u32[]{:S(2)}) collective-permute-start(bf16[3,128,768]{2,1,0:T(8,128)(2,1)S(1)} %collective-permute-done.5.refs_6_), channel_id=1, source_target_pairs={{0,64},{32,480},{64,128},{96,32},{128,192},{160,96},{192,256},{224... | collective-permute-start | bytes 1769480 | tf_op jit(solution)/shard_map/ppermute | solution.py:224
  50.0 1.9 %collective-permute-start.3 = (bf16[3,128,768]{2,1,0:T(8,128)(2,1)S(1)}, bf16[3,128,768]{2,1,0:T(8,128)(2,1)S(1)}, u32[]{:S(2)}, u32[]{:S(2)}) collective-permute-start(bf16[3,128,768]{2,1,0:T(8,128)(2,1)S(1)} %collective-permute-done.1.refs_2_), channel_id=1, source_target_pairs={{0,32},{32,0},{64,96},{96,64},{128,160},{160,128},{192,224},{224,1... | collective-permute-start | bytes 1769480 | tf_op jit(solution)/shard_map/ppermute | solution.py:225
  51.9 2.4 %collective-permute-start.4 = (bf16[3,128,768]{2,1,0:T(8,128)(2,1)S(1)}, bf16[3,128,768]{2,1,0:T(8,128)(2,1)S(1)}, u32[]{:S(2)}, u32[]{:S(2)}) collective-permute-start(bf16[3,128,768]{2,1,0:T(8,128)(2,1)S(1)} %collective-permute-done.2.refs_3_), channel_id=1, source_target_pairs={{0,32},{32,0},{64,96},{96,64},{128,160},{160,128},{192,224},{224,1... | collective-permute-start | bytes 1769480 | tf_op jit(solution)/shard_map/ppermute | solution.py:225
  54.3 0.0 collective-permute-done.6.refs_7_
  54.4 1.9 %collective-permute-start.10 = (bf16[3,128,768]{2,1,0:T(8,128)(2,1)S(1)}, bf16[3,128,768]{2,1,0:T(8,128)(2,1)S(1)}, u32[]{:S(2)}, u32[]{:S(2)}) collective-permute-start(bf16[3,128,768]{2,1,0:T(8,128)(2,1)S(1)} %collective-permute-done.6.refs_7_), channel_id=1, source_target_pairs={{0,64},{32,480},{64,128},{96,32},{128,192},{160,96},{192,256},{224... | collective-permute-start | bytes 1769480 | tf_op jit(solution)/shard_map/ppermute | solution.py:224
  56.3 1.1 collective-permute-done.9.refs_10_
  57.4 5.6 %collective-permute-start.13 = (bf16[3,128,768]{2,1,0:T(8,128)(2,1)S(1)}, bf16[3,128,768]{2,1,0:T(8,128)(2,1)S(1)}, u32[]{:S(2)}, u32[]{:S(2)}) collective-permute-start(bf16[3,128,768]{2,1,0:T(8,128)(2,1)S(1)} %collective-permute-done.9.refs_10_), channel_id=1, source_target_pairs={{0,64},{32,480},{64,128},{96,32},{128,192},{160,96},{192,256},{224... | collective-permute-start | bytes 1769480 | tf_op jit(solution)/shard_map/ppermute | solution.py:226
  63.0 1.9 %collective-permute-start.7 = (bf16[3,128,768]{2,1,0:T(8,128)(2,1)S(1)}, bf16[3,128,768]{2,1,0:T(8,128)(2,1)S(1)}, u32[]{:S(2)}, u32[]{:S(2)}) collective-permute-start(bf16[3,128,768]{2,1,0:T(8,128)(2,1)S(1)} %collective-permute-done.5.refs_6_), channel_id=1, source_target_pairs={{0,32},{32,0},{64,96},{96,64},{128,160},{160,128},{192,224},{224,1... | collective-permute-start | bytes 1769480 | tf_op jit(solution)/shard_map/ppermute | solution.py:225
  64.9 0.0 collective-permute-done.3.refs_4_
  64.9 2.4 %collective-permute-start.8 = (bf16[3,128,768]{2,1,0:T(8,128)(2,1)S(1)}, bf16[3,128,768]{2,1,0:T(8,128)(2,1)S(1)}, u32[]{:S(2)}, u32[]{:S(2)}) collective-permute-start(bf16[3,128,768]{2,1,0:T(8,128)(2,1)S(1)} %collective-permute-done.6.refs_7_), channel_id=1, source_target_pairs={{0,32},{32,0},{64,96},{96,64},{128,160},{160,128},{192,224},{224,1... | collective-permute-start | bytes 1769480 | tf_op jit(solution)/shard_map/ppermute | solution.py:225
  67.3 0.0 collective-permute-done.4.refs_5_
  67.4 1.9 %collective-permute-start.11 = (bf16[3,128,768]{2,1,0:T(8,128)(2,1)S(1)}, bf16[3,128,768]{2,1,0:T(8,128)(2,1)S(1)}, u32[]{:S(2)}, u32[]{:S(2)}) collective-permute-start(bf16[3,128,768]{2,1,0:T(8,128)(2,1)S(1)} %collective-permute-done.9.refs_10_), channel_id=1, source_target_pairs={{0,32},{32,0},{64,96},{96,64},{128,160},{160,128},{192,224},{224,1... | collective-permute-start | bytes 1769480 | tf_op jit(solution)/shard_map/ppermute | solution.py:225
  69.3 0.0 collective-permute-done.10.refs_11_
  69.3 2.4 %collective-permute-start.12 = (bf16[3,128,768]{2,1,0:T(8,128)(2,1)S(1)}, bf16[3,128,768]{2,1,0:T(8,128)(2,1)S(1)}, u32[]{:S(2)}, u32[]{:S(2)}) collective-permute-start(bf16[3,128,768]{2,1,0:T(8,128)(2,1)S(1)} %collective-permute-done.10.refs_11_), channel_id=1, source_target_pairs={{0,32},{32,0},{64,96},{96,64},{128,160},{160,128},{192,224},{224,1... | collective-permute-start | bytes 1769480 | tf_op jit(solution)/shard_map/ppermute | solution.py:225
  71.7 0.7 collective-permute-done.13.refs_14_
  72.5 2.4 %collective-permute-start.14 = (bf16[3,128,768]{2,1,0:T(8,128)(2,1)S(1)}, bf16[3,128,768]{2,1,0:T(8,128)(2,1)}, u32[]{:S(2)}, u32[]{:S(2)}) collective-permute-start(bf16[3,128,768]{2,1,0:T(8,128)(2,1)S(1)} %collective-permute-done.13.refs_14_), channel_id=1, source_target_pairs={{0,32},{32,0},{64,96},{96,64},{128,160},{160,128},{192,224},{224,1... | collective-permute-start | bytes 1769480 | tf_op jit(solution)/shard_map/ppermute | solution.py:227
  74.8 0.0 collective-permute-done.7.refs_8_
  74.9 0.0 collective-permute-done.8.refs_9_
  74.9 0.0 collective-permute-done.11.refs_12_
  74.9 0.0 collective-permute-done.12.refs_13_
  75.0 0.7 copy-done.15
  75.7 0.2 copy-done.16
  75.9 0.2 copy-done.17
  76.1 0.8 copy-done.18
  76.9 0.0 collective-permute-done.14.refs_15_
  76.9 3.6 %all-to-all-done.x_hbm = bf16[32,16,2560]{2,1,0:T(8,128)(2,1)} async-done(((bf16[32,16,2560]{2,1,0:T(8,128)(2,1)}), bf16[32,16,2560]{2,1,0:T(8,128)(2,1)}, u32[]{:S(2)}, u32[]{:S(2)}) %all-to-all-start) | async-done | bytes 2621472 | tf_op jit(solution)/shard_map/all_to_all | solution.py:253
  80.6 11.1 %expert_rows.1 = bf16[32,8,2688]{2,1,0:T(8,128)(2,1)} custom-call(bf16[32,16,2560]{2,1,0:T(8,128)(2,1)} %all-to-all-done.x_hbm, bf16[3,128,768]{2,1,0:T(8,128)(2,1)} %copy-done, bf16[3,128,768]{2,1,0:T(8,128)(2,1)} %copy-done.5, bf16[3,128,768]{2,1,0:T(8,128)(2,1)} %copy-done.6, bf16[3,128,768]{2,1,0:T(8,128)(2,1)} %copy-done.7, ...), custom_call_target="tpu_custom_call" | custom-call | flops 6000000000 | bytes 14000000 | tf_op jit(solution)/shard_map/expert_rows/pallas_call | solution.py:262
  91.6 0.0 copy-start.3
  91.7 0.0 copy-start.4
  91.7 6.1 %all-to-all-start.1 = ((bf16[32,8,2688]{2,1,0:T(8,128)(2,1)}), bf16[32,8,2688]{2,1,0:T(8,128)(2,1)S(1)}, u32[]{:S(2)}, u32[]{:S(2)}) async-start(bf16[32,8,2688]{2,1,0:T(8,128)(2,1)} %expert_rows.1), calls=%async_computation.1 | async-start | bytes 2752512 | tf_op jit(solution)/shard_map/all_to_all | solution.py:283
  97.8 0.1 copy.8.ids_t_ref
  97.9 0.1 copy.9.p_ref
  98.0 35.3 %all-to-all-done.1.back_ref = bf16[32,8,2688]{2,1,0:T(8,128)(2,1)S(1)} async-done(((bf16[32,8,2688]{2,1,0:T(8,128)(2,1)}), bf16[32,8,2688]{2,1,0:T(8,128)(2,1)S(1)}, u32[]{:S(2)}, u32[]{:S(2)}) %all-to-all-start.1) | async-done | bytes 1376288 | tf_op jit(solution)/shard_map/all_to_all | solution.py:283
  133.3 1.8 %combine_rows.1 = (bf16[128,2048]{1,0:T(8,128)(2,1)}, bf16[2,128]{1,0:T(2,128)(2,1)}) custom-call(s32[2,128]{1,0:T(2,128)S(1)} %bitcast.3, s32[128,2]{1,0:T(8,128)S(1)} %copy.8.ids_t_ref, f32[128,2]{1,0:T(8,128)S(1)} %copy.9.p_ref, bf16[32,8,2688]{2,1,0:T(8,128)(2,1)S(1)} %all-to-all-done.1.back_ref), custom_call_target="tpu_custom_call" | custom-call | flops 2000000000 | bytes 2000000 | tf_op jit(solution)/shard_map/combine_rows/pallas_call | solution.py:284
  (30 shorter events, 0.1 us)
Async XLA Ops:
  3.7 13.5 %copy-start.1 = (bf16[1,2,128,768]{3,2,1,0:T(8,128)(2,1)S(1)}, bf16[1,2,128,768]{3,2,1,0:T(8,128)(2,1)}, u32[]{:S(2)}) copy-start(bf16[1,2,128,768]{3,2,1,0:T(8,128)(2,1)} %gu_ref.1) | copy-start | bytes 1179652
  3.7 13.5 %copy-start.2 = (bf16[1,768,128]{2,1,0:T(8,128)(2,1)S(1)}, bf16[1,768,128]{2,1,0:T(8,128)(2,1)}, u32[]{:S(2)}) copy-start(bf16[1,768,128]{2,1,0:T(8,128)(2,1)} %wd_ref.1) | copy-start | bytes 589828
  3.7 76.8 %all-to-all-start = ((bf16[32,16,2560]{2,1,0:T(8,128)(2,1)}), bf16[32,16,2560]{2,1,0:T(8,128)(2,1)}, u32[]{:S(2)}, u32[]{:S(2)}) async-start(bf16[32,16,2560]{2,1,0:T(8,128)(2,1)} %pack_rows.1), calls=%async_computation | async-start | bytes 5242880 | tf_op jit(solution)/shard_map/all_to_all | solution.py:253
  17.4 63.1 %copy-start = (bf16[3,128,768]{2,1,0:T(8,128)(2,1)}, bf16[3,128,768]{2,1,0:T(8,128)(2,1)S(1)}, u32[]{:S(2)}) copy-start(bf16[3,128,768]{2,1,0:T(8,128)(2,1)S(1)} %join_weights.1.refs_0_) | copy-start | bytes 1769476
  17.4 6.6 %collective-permute-start = (bf16[3,128,768]{2,1,0:T(8,128)(2,1)S(1)}, bf16[3,128,768]{2,1,0:T(8,128)(2,1)S(1)}, u32[]{:S(2)}, u32[]{:S(2)}) collective-permute-start(bf16[3,128,768]{2,1,0:T(8,128)(2,1)S(1)} %join_weights.1.refs_0_), channel_id=1, source_target_pairs={{0,32},{32,0},{64,96},{96,64},{128,160},{160,128},{192,224},{224,1... | collective-permute-start | bytes 1769480 | tf_op jit(solution)/shard_map/ppermute | solution.py:221
  19.3 12.1 %collective-permute-start.1 = (bf16[3,128,768]{2,1,0:T(8,128)(2,1)S(1)}, bf16[3,128,768]{2,1,0:T(8,128)(2,1)S(1)}, u32[]{:S(2)}, u32[]{:S(2)}) collective-permute-start(bf16[3,128,768]{2,1,0:T(8,128)(2,1)S(1)} %join_weights.1.refs_0_), channel_id=1, source_target_pairs={{0,64},{32,480},{64,128},{96,32},{128,192},{160,96},{192,256},{224... | collective-permute-start | bytes 1769480 | tf_op jit(solution)/shard_map/ppermute | solution.py:224
  24.0 56.5 %copy-start.5 = (bf16[3,128,768]{2,1,0:T(8,128)(2,1)}, bf16[3,128,768]{2,1,0:T(8,128)(2,1)S(1)}, u32[]{:S(2)}) copy-start(bf16[3,128,768]{2,1,0:T(8,128)(2,1)S(1)} %collective-permute-done.refs_1_) | copy-start | bytes 1769476
  24.1 13.7 %collective-permute-start.2 = (bf16[3,128,768]{2,1,0:T(8,128)(2,1)S(1)}, bf16[3,128,768]{2,1,0:T(8,128)(2,1)S(1)}, u32[]{:S(2)}, u32[]{:S(2)}) collective-permute-start(bf16[3,128,768]{2,1,0:T(8,128)(2,1)S(1)} %collective-permute-done.refs_1_), channel_id=1, source_target_pairs={{0,64},{32,480},{64,128},{96,32},{128,192},{160,96},{192,256},{224... | collective-permute-start | bytes 1769480 | tf_op jit(solution)/shard_map/ppermute | solution.py:224
  31.4 49.1 %copy-start.6 = (bf16[3,128,768]{2,1,0:T(8,128)(2,1)}, bf16[3,128,768]{2,1,0:T(8,128)(2,1)S(1)}, u32[]{:S(2)}) copy-start(bf16[3,128,768]{2,1,0:T(8,128)(2,1)S(1)} %collective-permute-done.1.refs_2_) | copy-start | bytes 1769476
  31.4 13.0 %collective-permute-start.5 = (bf16[3,128,768]{2,1,0:T(8,128)(2,1)S(1)}, bf16[3,128,768]{2,1,0:T(8,128)(2,1)S(1)}, u32[]{:S(2)}, u32[]{:S(2)}) collective-permute-start(bf16[3,128,768]{2,1,0:T(8,128)(2,1)S(1)} %collective-permute-done.1.refs_2_), channel_id=1, source_target_pairs={{0,64},{32,480},{64,128},{96,32},{128,192},{160,96},{192,256},{224... | collective-permute-start | bytes 1769480 | tf_op jit(solution)/shard_map/ppermute | solution.py:224
  37.7 42.8 %copy-start.7 = (bf16[3,128,768]{2,1,0:T(8,128)(2,1)}, bf16[3,128,768]{2,1,0:T(8,128)(2,1)S(1)}, u32[]{:S(2)}) copy-start(bf16[3,128,768]{2,1,0:T(8,128)(2,1)S(1)} %collective-permute-done.2.refs_3_) | copy-start | bytes 1769476
  37.7 16.6 %collective-permute-start.6 = (bf16[3,128,768]{2,1,0:T(8,128)(2,1)S(1)}, bf16[3,128,768]{2,1,0:T(8,128)(2,1)S(1)}, u32[]{:S(2)}, u32[]{:S(2)}) collective-permute-start(bf16[3,128,768]{2,1,0:T(8,128)(2,1)S(1)} %collective-permute-done.2.refs_3_), channel_id=1, source_target_pairs={{0,64},{32,480},{64,128},{96,32},{128,192},{160,96},{192,256},{224... | collective-permute-start | bytes 1769480 | tf_op jit(solution)/shard_map/ppermute | solution.py:224
  44.4 36.2 %copy-start.8 = (bf16[3,128,768]{2,1,0:T(8,128)(2,1)}, bf16[3,128,768]{2,1,0:T(8,128)(2,1)S(1)}, u32[]{:S(2)}) copy-start(bf16[3,128,768]{2,1,0:T(8,128)(2,1)S(1)} %collective-permute-done.5.refs_6_) | copy-start | bytes 1769476
  44.4 13.0 %collective-permute-start.9 = (bf16[3,128,768]{2,1,0:T(8,128)(2,1)S(1)}, bf16[3,128,768]{2,1,0:T(8,128)(2,1)S(1)}, u32[]{:S(2)}, u32[]{:S(2)}) collective-permute-start(bf16[3,128,768]{2,1,0:T(8,128)(2,1)S(1)} %collective-permute-done.5.refs_6_), channel_id=1, source_target_pairs={{0,64},{32,480},{64,128},{96,32},{128,192},{160,96},{192,256},{224... | collective-permute-start | bytes 1769480 | tf_op jit(solution)/shard_map/ppermute | solution.py:224
  50.0 14.9 %collective-permute-start.3 = (bf16[3,128,768]{2,1,0:T(8,128)(2,1)S(1)}, bf16[3,128,768]{2,1,0:T(8,128)(2,1)S(1)}, u32[]{:S(2)}, u32[]{:S(2)}) collective-permute-start(bf16[3,128,768]{2,1,0:T(8,128)(2,1)S(1)} %collective-permute-done.1.refs_2_), channel_id=1, source_target_pairs={{0,32},{32,0},{64,96},{96,64},{128,160},{160,128},{192,224},{224,1... | collective-permute-start | bytes 1769480 | tf_op jit(solution)/shard_map/ppermute | solution.py:225
  51.9 15.4 %collective-permute-start.4 = (bf16[3,128,768]{2,1,0:T(8,128)(2,1)S(1)}, bf16[3,128,768]{2,1,0:T(8,128)(2,1)S(1)}, u32[]{:S(2)}, u32[]{:S(2)}) collective-permute-start(bf16[3,128,768]{2,1,0:T(8,128)(2,1)S(1)} %collective-permute-done.2.refs_3_), channel_id=1, source_target_pairs={{0,32},{32,0},{64,96},{96,64},{128,160},{160,128},{192,224},{224,1... | collective-permute-start | bytes 1769480 | tf_op jit(solution)/shard_map/ppermute | solution.py:225
  54.3 26.2 %copy-start.9 = (bf16[3,128,768]{2,1,0:T(8,128)(2,1)}, bf16[3,128,768]{2,1,0:T(8,128)(2,1)S(1)}, u32[]{:S(2)}) copy-start(bf16[3,128,768]{2,1,0:T(8,128)(2,1)S(1)} %collective-permute-done.6.refs_7_) | copy-start | bytes 1769476
  54.4 14.9 %collective-permute-start.10 = (bf16[3,128,768]{2,1,0:T(8,128)(2,1)S(1)}, bf16[3,128,768]{2,1,0:T(8,128)(2,1)S(1)}, u32[]{:S(2)}, u32[]{:S(2)}) collective-permute-start(bf16[3,128,768]{2,1,0:T(8,128)(2,1)S(1)} %collective-permute-done.6.refs_7_), channel_id=1, source_target_pairs={{0,64},{32,480},{64,128},{96,32},{128,192},{160,96},{192,256},{224... | collective-permute-start | bytes 1769480 | tf_op jit(solution)/shard_map/ppermute | solution.py:224
  57.4 17.5 %copy-start.10 = (bf16[3,128,768]{2,1,0:T(8,128)(2,1)}, bf16[3,128,768]{2,1,0:T(8,128)(2,1)S(1)}, u32[]{:S(2)}) copy-start(bf16[3,128,768]{2,1,0:T(8,128)(2,1)S(1)} %collective-permute-done.9.refs_10_) | copy-start | bytes 1769476
  57.4 15.1 %collective-permute-start.13 = (bf16[3,128,768]{2,1,0:T(8,128)(2,1)S(1)}, bf16[3,128,768]{2,1,0:T(8,128)(2,1)S(1)}, u32[]{:S(2)}, u32[]{:S(2)}) collective-permute-start(bf16[3,128,768]{2,1,0:T(8,128)(2,1)S(1)} %collective-permute-done.9.refs_10_), channel_id=1, source_target_pairs={{0,64},{32,480},{64,128},{96,32},{128,192},{160,96},{192,256},{224... | collective-permute-start | bytes 1769480 | tf_op jit(solution)/shard_map/ppermute | solution.py:226
  63.0 11.9 %collective-permute-start.7 = (bf16[3,128,768]{2,1,0:T(8,128)(2,1)S(1)}, bf16[3,128,768]{2,1,0:T(8,128)(2,1)S(1)}, u32[]{:S(2)}, u32[]{:S(2)}) collective-permute-start(bf16[3,128,768]{2,1,0:T(8,128)(2,1)S(1)} %collective-permute-done.5.refs_6_), channel_id=1, source_target_pairs={{0,32},{32,0},{64,96},{96,64},{128,160},{160,128},{192,224},{224,1... | collective-permute-start | bytes 1769480 | tf_op jit(solution)/shard_map/ppermute | solution.py:225
  64.9 10.0 %copy-start.11 = (bf16[3,128,768]{2,1,0:T(8,128)(2,1)}, bf16[3,128,768]{2,1,0:T(8,128)(2,1)S(1)}, u32[]{:S(2)}) copy-start(bf16[3,128,768]{2,1,0:T(8,128)(2,1)S(1)} %collective-permute-done.3.refs_4_) | copy-start | bytes 1769476
  64.9 9.9 %collective-permute-start.8 = (bf16[3,128,768]{2,1,0:T(8,128)(2,1)S(1)}, bf16[3,128,768]{2,1,0:T(8,128)(2,1)S(1)}, u32[]{:S(2)}, u32[]{:S(2)}) collective-permute-start(bf16[3,128,768]{2,1,0:T(8,128)(2,1)S(1)} %collective-permute-done.6.refs_7_), channel_id=1, source_target_pairs={{0,32},{32,0},{64,96},{96,64},{128,160},{160,128},{192,224},{224,1... | collective-permute-start | bytes 1769480 | tf_op jit(solution)/shard_map/ppermute | solution.py:225
  67.3 7.6 %copy-start.12 = (bf16[3,128,768]{2,1,0:T(8,128)(2,1)}, bf16[3,128,768]{2,1,0:T(8,128)(2,1)S(1)}, u32[]{:S(2)}) copy-start(bf16[3,128,768]{2,1,0:T(8,128)(2,1)S(1)} %collective-permute-done.4.refs_5_) | copy-start | bytes 1769476
  67.4 7.5 %collective-permute-start.11 = (bf16[3,128,768]{2,1,0:T(8,128)(2,1)S(1)}, bf16[3,128,768]{2,1,0:T(8,128)(2,1)S(1)}, u32[]{:S(2)}, u32[]{:S(2)}) collective-permute-start(bf16[3,128,768]{2,1,0:T(8,128)(2,1)S(1)} %collective-permute-done.9.refs_10_), channel_id=1, source_target_pairs={{0,32},{32,0},{64,96},{96,64},{128,160},{160,128},{192,224},{224,1... | collective-permute-start | bytes 1769480 | tf_op jit(solution)/shard_map/ppermute | solution.py:225
  69.3 5.6 %copy-start.13 = (bf16[3,128,768]{2,1,0:T(8,128)(2,1)}, bf16[3,128,768]{2,1,0:T(8,128)(2,1)S(1)}, u32[]{:S(2)}) copy-start(bf16[3,128,768]{2,1,0:T(8,128)(2,1)S(1)} %collective-permute-done.10.refs_11_) | copy-start | bytes 1769476
  69.3 5.6 %collective-permute-start.12 = (bf16[3,128,768]{2,1,0:T(8,128)(2,1)S(1)}, bf16[3,128,768]{2,1,0:T(8,128)(2,1)S(1)}, u32[]{:S(2)}, u32[]{:S(2)}) collective-permute-start(bf16[3,128,768]{2,1,0:T(8,128)(2,1)S(1)} %collective-permute-done.10.refs_11_), channel_id=1, source_target_pairs={{0,32},{32,0},{64,96},{96,64},{128,160},{160,128},{192,224},{224,1... | collective-permute-start | bytes 1769480 | tf_op jit(solution)/shard_map/ppermute | solution.py:225
  72.5 2.5 %copy-start.14 = (bf16[3,128,768]{2,1,0:T(8,128)(2,1)}, bf16[3,128,768]{2,1,0:T(8,128)(2,1)S(1)}, u32[]{:S(2)}) copy-start(bf16[3,128,768]{2,1,0:T(8,128)(2,1)S(1)} %collective-permute-done.13.refs_14_) | copy-start | bytes 1769476
  72.5 4.5 %collective-permute-start.14 = (bf16[3,128,768]{2,1,0:T(8,128)(2,1)S(1)}, bf16[3,128,768]{2,1,0:T(8,128)(2,1)}, u32[]{:S(2)}, u32[]{:S(2)}) collective-permute-start(bf16[3,128,768]{2,1,0:T(8,128)(2,1)S(1)} %collective-permute-done.13.refs_14_), channel_id=1, source_target_pairs={{0,32},{32,0},{64,96},{96,64},{128,160},{160,128},{192,224},{224,1... | collective-permute-start | bytes 1769480 | tf_op jit(solution)/shard_map/ppermute | solution.py:227
  74.8 0.8 copy-start.15
  74.9 1.0 copy-start.16
  74.9 1.2 copy-start.17
  76.1 0.8 copy-start.18
  91.6 6.2 %copy-start.3 = (s32[128,2]{0,1:T(2,128)S(1)}, s32[128,2]{0,1:T(2,128)}, u32[]{:S(2)}) copy-start(s32[128,2]{0,1:T(2,128)} %param.8) | copy-start | bytes 3076
  91.7 6.3 %copy-start.4 = (f32[128,2]{0,1:T(2,128)S(1)}, f32[128,2]{0,1:T(2,128)}, u32[]{:S(2)}) copy-start(f32[128,2]{0,1:T(2,128)} %param.9) | copy-start | bytes 3076
  91.7 41.7 %all-to-all-start.1 = ((bf16[32,8,2688]{2,1,0:T(8,128)(2,1)}), bf16[32,8,2688]{2,1,0:T(8,128)(2,1)S(1)}, u32[]{:S(2)}, u32[]{:S(2)}) async-start(bf16[32,8,2688]{2,1,0:T(8,128)(2,1)} %expert_rows.1), calls=%async_computation.1 | async-start | bytes 2752512 | tf_op jit(solution)/shard_map/all_to_all | solution.py:283

commit v6 on v5

--- a/solution.py
+++ b/solution.py
@@ -174,7 +174,7 @@
     pltpu.make_async_copy(out_ref, out_hbm, out_sem).wait()
 
 
-def combine_kernel(ids_ref, ids_t_ref, p_ref, back_ref, out_ref, prob_out_ref):
+def combine_kernel(ids_ref, ids_t_ref, p_ref, back_ref, out_hbm, prob_out_ref, out_ref, out_sem):
     experts = back_ref.shape[0]
     toks = p_ref.shape[0]
     k0, k1 = ranks(ids_ref[...], experts)
@@ -205,6 +205,9 @@
         body = back_ref[:, :, cols].astype(F32).reshape(lanes, 512).astype(BF)
         rows = dot(pick, body) + dot(jnp.where(j >> 1 == q, late, 0.0).astype(BF), tail)
         out_ref[:, cols] = (p0 * rows[:toks] + p1 * rows[toks:]).astype(BF)
+        part = pl.ds(q * 512, 512)
+        pltpu.make_async_copy(out_ref.at[:, part], out_hbm.at[:, part], out_sem).start()
+    pltpu.make_async_copy(out_ref, out_hbm, out_sem).wait()
 
 
 def params(mib):
@@ -283,7 +286,9 @@
     back = lax.all_to_all(back, "expert", split_axis=0, concat_axis=0, tiled=True)
     input_grad, prob_grad = pl.pallas_call(
         combine_kernel,
+        out_specs=(hbm, vmem),
         out_shape=(jax.ShapeDtypeStruct((toks, features), BF), jax.ShapeDtypeStruct((2, toks), BF)),
+        scratch_shapes=[pltpu.VMEM((toks, features), BF), pltpu.SemaphoreType.DMA],
         compiler_params=params(20),
         cost_estimate=cost(2 * 10**9, 2000000),
         name="combine_rows",

time: 136 us -> 136 us (level)
  no operation moved by 1% of the time
where the time goes in v6:
time: 136 us
  starting transfers between devices  68.4 us (50%)
  waiting for transfers between devices  47.3 us (35%)
  Pallas kernels  16.5 us (12%)
  local copies, waits for them, and re-layouts  2.26 us (2%)
    all_to_all x1, waiting for transfers between devices, shards(): lax.all_to_all(back, 'expert', split_axis=0, concat_axis=0, tiled=True)  35.3 us
    ppermute x3, starting transfers between devices, ring(): lax.ppermute(first, 'dp', on)  15.9 us
    all_to_all x1, starting transfers between devices, shards(): lax.all_to_all(send, 'expert', split_axis=0, concat_axis=0, tiled=True)  13.4 us
    pallas_call x1, Pallas kernels, shards(): pl.pallas_call(expert_kernel, in_specs=[hbm] * (1 + len(pieces)), out_spe...  11.1 us
    ppermute x3, starting transfers between devices, ring(): lax.ppermute(second, 'dp', on)  10.1 us
    ppermute x3, starting transfers between devices, ring(): lax.ppermute(second, 'dp', swap)  7.22 us
    ppermute x3, waiting for transfers between devices, ring(): lax.ppermute(first, 'dp', on)  6.88 us
    all_to_all x1, starting transfers between devices, shards(): lax.all_to_all(back, 'expert', split_axis=0, concat_axis=0, tiled=True)  6.13 us
  transfers between devices with their start and end apart: 17, of which 7 were waited for; matrix products, arithmetic and copies ran while one was open for 0% of the time, Pallas kernels for 0%

profile of v6, /device:TPU:24, one launch (start us, length us, event | category | flops | bytes accessed | tf_op | source)
XLA Modules:
  0.0 135.5 jit_solution(10099558933228590388)
XLA Ops:
  0.6 3.1 %pack_rows.1 = bf16[32,16,2560]{2,1,0:T(8,128)(2,1)} custom-call(s32[2,128]{1,0:T(2,128)} %bitcast.2, bf16[128,2048]{1,0:T(8,128)(2,1)} %tok_hbm.1, bf16[128,2048]{1,0:T(8,128)(2,1)} %grad_hbm.1), custom_call_target="tpu_custom_call" | custom-call | flops 1000000000 | bytes 4000000 | tf_op jit(solution)/shard_map/pack_rows/pallas_call | solution.py:239
  3.7 0.0 copy-start.1
  3.7 0.0 copy-start.2
  3.7 13.4 %all-to-all-start = ((bf16[32,16,2560]{2,1,0:T(8,128)(2,1)}), bf16[32,16,2560]{2,1,0:T(8,128)(2,1)}, u32[]{:S(2)}, u32[]{:S(2)}) async-start(bf16[32,16,2560]{2,1,0:T(8,128)(2,1)} %pack_rows.1), calls=%async_computation | async-start | bytes 5242880 | tf_op jit(solution)/shard_map/all_to_all | solution.py:256
  17.2 0.2 join_weights.1.refs_0_
  17.4 1.9 %collective-permute-start = (bf16[3,128,768]{2,1,0:T(8,128)(2,1)S(1)}, bf16[3,128,768]{2,1,0:T(8,128)(2,1)S(1)}, u32[]{:S(2)}, u32[]{:S(2)}) collective-permute-start(bf16[3,128,768]{2,1,0:T(8,128)(2,1)S(1)} %join_weights.1.refs_0_), channel_id=1, source_target_pairs={{0,32},{32,0},{64,96},{96,64},{128,160},{160,128},{192,224},{224,1... | collective-permute-start | bytes 1769480 | tf_op jit(solution)/shard_map/ppermute | solution.py:224
  19.3 4.7 %collective-permute-start.1 = (bf16[3,128,768]{2,1,0:T(8,128)(2,1)S(1)}, bf16[3,128,768]{2,1,0:T(8,128)(2,1)S(1)}, u32[]{:S(2)}, u32[]{:S(2)}) collective-permute-start(bf16[3,128,768]{2,1,0:T(8,128)(2,1)S(1)} %join_weights.1.refs_0_), channel_id=1, source_target_pairs={{0,64},{32,480},{64,128},{96,32},{128,192},{160,96},{192,256},{224... | collective-permute-start | bytes 1769480 | tf_op jit(solution)/shard_map/ppermute | solution.py:227
  24.0 0.0 collective-permute-done.refs_1_
  24.1 2.6 %collective-permute-start.2 = (bf16[3,128,768]{2,1,0:T(8,128)(2,1)S(1)}, bf16[3,128,768]{2,1,0:T(8,128)(2,1)S(1)}, u32[]{:S(2)}, u32[]{:S(2)}) collective-permute-start(bf16[3,128,768]{2,1,0:T(8,128)(2,1)S(1)} %collective-permute-done.refs_1_), channel_id=1, source_target_pairs={{0,64},{32,480},{64,128},{96,32},{128,192},{160,96},{192,256},{224... | collective-permute-start | bytes 1769480 | tf_op jit(solution)/shard_map/ppermute | solution.py:227
  26.7 4.8 %collective-permute-done.1.refs_2_ = bf16[3,128,768]{2,1,0:T(8,128)(2,1)S(1)} collective-permute-done((bf16[3,128,768]{2,1,0:T(8,128)(2,1)S(1)}, bf16[3,128,768]{2,1,0:T(8,128)(2,1)S(1)}, u32[]{:S(2)}, u32[]{:S(2)}) %collective-permute-start.1) | collective-permute-done | bytes 589856 | tf_op jit(solution)/shard_map/ppermute | solution.py:227
  31.4 5.6 %collective-permute-start.5 = (bf16[3,128,768]{2,1,0:T(8,128)(2,1)S(1)}, bf16[3,128,768]{2,1,0:T(8,128)(2,1)S(1)}, u32[]{:S(2)}, u32[]{:S(2)}) collective-permute-start(bf16[3,128,768]{2,1,0:T(8,128)(2,1)S(1)} %collective-permute-done.1.refs_2_), channel_id=1, source_target_pairs={{0,64},{32,480},{64,128},{96,32},{128,192},{160,96},{192,256},{224... | collective-permute-start | bytes 1769480 | tf_op jit(solution)/shard_map/ppermute | solution.py:227
  37.0 0.7 collective-permute-done.2.refs_3_
  37.7 5.6 %collective-permute-start.6 = (bf16[3,128,768]{2,1,0:T(8,128)(2,1)S(1)}, bf16[3,128,768]{2,1,0:T(8,128)(2,1)S(1)}, u32[]{:S(2)}, u32[]{:S(2)}) collective-permute-start(bf16[3,128,768]{2,1,0:T(8,128)(2,1)S(1)} %collective-permute-done.2.refs_3_), channel_id=1, source_target_pairs={{0,64},{32,480},{64,128},{96,32},{128,192},{160,96},{192,256},{224... | collective-permute-start | bytes 1769480 | tf_op jit(solution)/shard_map/ppermute | solution.py:227
  43.3 1.1 collective-permute-done.5.refs_6_
  44.4 5.6 %collective-permute-start.9 = (bf16[3,128,768]{2,1,0:T(8,128)(2,1)S(1)}, bf16[3,128,768]{2,1,0:T(8,128)(2,1)S(1)}, u32[]{:S(2)}, u32[]{:S(2)}) collective-permute-start(bf16[3,128,768]{2,1,0:T(8,128)(2,1)S(1)} %collective-permute-done.5.refs_6_), channel_id=1, source_target_pairs={{0,64},{32,480},{64,128},{96,32},{128,192},{160,96},{192,256},{224... | collective-permute-start | bytes 1769480 | tf_op jit(solution)/shard_map/ppermute | solution.py:227
  50.0 1.9 %collective-permute-start.3 = (bf16[3,128,768]{2,1,0:T(8,128)(2,1)S(1)}, bf16[3,128,768]{2,1,0:T(8,128)(2,1)S(1)}, u32[]{:S(2)}, u32[]{:S(2)}) collective-permute-start(bf16[3,128,768]{2,1,0:T(8,128)(2,1)S(1)} %collective-permute-done.1.refs_2_), channel_id=1, source_target_pairs={{0,32},{32,0},{64,96},{96,64},{128,160},{160,128},{192,224},{224,1... | collective-permute-start | bytes 1769480 | tf_op jit(solution)/shard_map/ppermute | solution.py:228
  51.9 2.4 %collective-permute-start.4 = (bf16[3,128,768]{2,1,0:T(8,128)(2,1)S(1)}, bf16[3,128,768]{2,1,0:T(8,128)(2,1)S(1)}, u32[]{:S(2)}, u32[]{:S(2)}) collective-permute-start(bf16[3,128,768]{2,1,0:T(8,128)(2,1)S(1)} %collective-permute-done.2.refs_3_), channel_id=1, source_target_pairs={{0,32},{32,0},{64,96},{96,64},{128,160},{160,128},{192,224},{224,1... | collective-permute-start | bytes 1769480 | tf_op jit(solution)/shard_map/ppermute | solution.py:228
  54.3 0.0 collective-permute-done.6.refs_7_
  54.4 1.9 %collective-permute-start.10 = (bf16[3,128,768]{2,1,0:T(8,128)(2,1)S(1)}, bf16[3,128,768]{2,1,0:T(8,128)(2,1)S(1)}, u32[]{:S(2)}, u32[]{:S(2)}) collective-permute-start(bf16[3,128,768]{2,1,0:T(8,128)(2,1)S(1)} %collective-permute-done.6.refs_7_), channel_id=1, source_target_pairs={{0,64},{32,480},{64,128},{96,32},{128,192},{160,96},{192,256},{224... | collective-permute-start | bytes 1769480 | tf_op jit(solution)/shard_map/ppermute | solution.py:227
  56.3 1.1 collective-permute-done.9.refs_10_
  57.4 5.6 %collective-permute-start.13 = (bf16[3,128,768]{2,1,0:T(8,128)(2,1)S(1)}, bf16[3,128,768]{2,1,0:T(8,128)(2,1)S(1)}, u32[]{:S(2)}, u32[]{:S(2)}) collective-permute-start(bf16[3,128,768]{2,1,0:T(8,128)(2,1)S(1)} %collective-permute-done.9.refs_10_), channel_id=1, source_target_pairs={{0,64},{32,480},{64,128},{96,32},{128,192},{160,96},{192,256},{224... | collective-permute-start | bytes 1769480 | tf_op jit(solution)/shard_map/ppermute | solution.py:229
  63.0 1.9 %collective-permute-start.7 = (bf16[3,128,768]{2,1,0:T(8,128)(2,1)S(1)}, bf16[3,128,768]{2,1,0:T(8,128)(2,1)S(1)}, u32[]{:S(2)}, u32[]{:S(2)}) collective-permute-start(bf16[3,128,768]{2,1,0:T(8,128)(2,1)S(1)} %collective-permute-done.5.refs_6_), channel_id=1, source_target_pairs={{0,32},{32,0},{64,96},{96,64},{128,160},{160,128},{192,224},{224,1... | collective-permute-start | bytes 1769480 | tf_op jit(solution)/shard_map/ppermute | solution.py:228
  64.9 0.0 collective-permute-done.3.refs_4_
  64.9 2.4 %collective-permute-start.8 = (bf16[3,128,768]{2,1,0:T(8,128)(2,1)S(1)}, bf16[3,128,768]{2,1,0:T(8,128)(2,1)S(1)}, u32[]{:S(2)}, u32[]{:S(2)}) collective-permute-start(bf16[3,128,768]{2,1,0:T(8,128)(2,1)S(1)} %collective-permute-done.6.refs_7_), channel_id=1, source_target_pairs={{0,32},{32,0},{64,96},{96,64},{128,160},{160,128},{192,224},{224,1... | collective-permute-start | bytes 1769480 | tf_op jit(solution)/shard_map/ppermute | solution.py:228
  67.3 0.0 collective-permute-done.4.refs_5_
  67.4 1.9 %collective-permute-start.11 = (bf16[3,128,768]{2,1,0:T(8,128)(2,1)S(1)}, bf16[3,128,768]{2,1,0:T(8,128)(2,1)S(1)}, u32[]{:S(2)}, u32[]{:S(2)}) collective-permute-start(bf16[3,128,768]{2,1,0:T(8,128)(2,1)S(1)} %collective-permute-done.9.refs_10_), channel_id=1, source_target_pairs={{0,32},{32,0},{64,96},{96,64},{128,160},{160,128},{192,224},{224,1... | collective-permute-start | bytes 1769480 | tf_op jit(solution)/shard_map/ppermute | solution.py:228
  69.3 0.0 collective-permute-done.10.refs_11_
  69.3 2.4 %collective-permute-start.12 = (bf16[3,128,768]{2,1,0:T(8,128)(2,1)S(1)}, bf16[3,128,768]{2,1,0:T(8,128)(2,1)S(1)}, u32[]{:S(2)}, u32[]{:S(2)}) collective-permute-start(bf16[3,128,768]{2,1,0:T(8,128)(2,1)S(1)} %collective-permute-done.10.refs_11_), channel_id=1, source_target_pairs={{0,32},{32,0},{64,96},{96,64},{128,160},{160,128},{192,224},{224,1... | collective-permute-start | bytes 1769480 | tf_op jit(solution)/shard_map/ppermute | solution.py:228
  71.7 0.7 collective-permute-done.13.refs_14_
  72.5 2.4 %collective-permute-start.14 = (bf16[3,128,768]{2,1,0:T(8,128)(2,1)S(1)}, bf16[3,128,768]{2,1,0:T(8,128)(2,1)}, u32[]{:S(2)}, u32[]{:S(2)}) collective-permute-start(bf16[3,128,768]{2,1,0:T(8,128)(2,1)S(1)} %collective-permute-done.13.refs_14_), channel_id=1, source_target_pairs={{0,32},{32,0},{64,96},{96,64},{128,160},{160,128},{192,224},{224,1... | collective-permute-start | bytes 1769480 | tf_op jit(solution)/shard_map/ppermute | solution.py:230
  74.8 0.0 collective-permute-done.7.refs_8_
  74.9 0.0 collective-permute-done.8.refs_9_
  74.9 0.0 collective-permute-done.11.refs_12_
  74.9 0.0 collective-permute-done.12.refs_13_
  75.0 0.7 copy-done.15
  75.7 0.2 copy-done.16
  75.9 0.2 copy-done.17
  76.1 0.8 copy-done.18
  76.9 0.0 collective-permute-done.14.refs_15_
  76.9 3.6 %all-to-all-done.x_hbm = bf16[32,16,2560]{2,1,0:T(8,128)(2,1)} async-done(((bf16[32,16,2560]{2,1,0:T(8,128)(2,1)}), bf16[32,16,2560]{2,1,0:T(8,128)(2,1)}, u32[]{:S(2)}, u32[]{:S(2)}) %all-to-all-start) | async-done | bytes 2621472 | tf_op jit(solution)/shard_map/all_to_all | solution.py:256
  80.6 11.1 %expert_rows.1 = bf16[32,8,2688]{2,1,0:T(8,128)(2,1)} custom-call(bf16[32,16,2560]{2,1,0:T(8,128)(2,1)} %all-to-all-done.x_hbm, bf16[3,128,768]{2,1,0:T(8,128)(2,1)} %copy-done, bf16[3,128,768]{2,1,0:T(8,128)(2,1)} %copy-done.5, bf16[3,128,768]{2,1,0:T(8,128)(2,1)} %copy-done.6, bf16[3,128,768]{2,1,0:T(8,128)(2,1)} %copy-done.7, ...), custom_call_target="tpu_custom_call" | custom-call | flops 6000000000 | bytes 14000000 | tf_op jit(solution)/shard_map/expert_rows/pallas_call | solution.py:265
  91.6 0.0 copy-start.3
  91.7 0.0 copy-start.4
  91.7 6.1 %all-to-all-start.1 = ((bf16[32,8,2688]{2,1,0:T(8,128)(2,1)}), bf16[32,8,2688]{2,1,0:T(8,128)(2,1)S(1)}, u32[]{:S(2)}, u32[]{:S(2)}) async-start(bf16[32,8,2688]{2,1,0:T(8,128)(2,1)} %expert_rows.1), calls=%async_computation.1 | async-start | bytes 2752512 | tf_op jit(solution)/shard_map/all_to_all | solution.py:286
  97.8 0.1 copy.8.ids_t_ref
  97.9 0.1 copy.9.p_ref
  98.0 35.3 %all-to-all-done.1.back_ref = bf16[32,8,2688]{2,1,0:T(8,128)(2,1)S(1)} async-done(((bf16[32,8,2688]{2,1,0:T(8,128)(2,1)}), bf16[32,8,2688]{2,1,0:T(8,128)(2,1)S(1)}, u32[]{:S(2)}, u32[]{:S(2)}) %all-to-all-start.1) | async-done | bytes 1376288 | tf_op jit(solution)/shard_map/all_to_all | solution.py:286
  133.3 2.2 %combine_rows.1 = (bf16[128,2048]{1,0:T(8,128)(2,1)}, bf16[2,128]{1,0:T(2,128)(2,1)}) custom-call(s32[2,128]{1,0:T(2,128)S(1)} %bitcast.3, s32[128,2]{1,0:T(8,128)S(1)} %copy.8.ids_t_ref, f32[128,2]{1,0:T(8,128)S(1)} %copy.9.p_ref, bf16[32,8,2688]{2,1,0:T(8,128)(2,1)S(1)} %all-to-all-done.1.back_ref), custom_call_target="tpu_custom_call" | custom-call | flops 2000000000 | bytes 2000000 | tf_op jit(solution)/shard_map/combine_rows/pallas_call | solution.py:287
  (30 shorter events, 0.1 us)
Async XLA Ops:
  3.7 13.5 %copy-start.1 = (bf16[1,2,128,768]{3,2,1,0:T(8,128)(2,1)S(1)}, bf16[1,2,128,768]{3,2,1,0:T(8,128)(2,1)}, u32[]{:S(2)}) copy-start(bf16[1,2,128,768]{3,2,1,0:T(8,128)(2,1)} %gu_ref.1) | copy-start | bytes 1179652
  3.7 13.5 %copy-start.2 = (bf16[1,768,128]{2,1,0:T(8,128)(2,1)S(1)}, bf16[1,768,128]{2,1,0:T(8,128)(2,1)}, u32[]{:S(2)}) copy-start(bf16[1,768,128]{2,1,0:T(8,128)(2,1)} %wd_ref.1) | copy-start | bytes 589828
  3.7 76.8 %all-to-all-start = ((bf16[32,16,2560]{2,1,0:T(8,128)(2,1)}), bf16[32,16,2560]{2,1,0:T(8,128)(2,1)}, u32[]{:S(2)}, u32[]{:S(2)}) async-start(bf16[32,16,2560]{2,1,0:T(8,128)(2,1)} %pack_rows.1), calls=%async_computation | async-start | bytes 5242880 | tf_op jit(solution)/shard_map/all_to_all | solution.py:256
  17.4 63.1 %copy-start = (bf16[3,128,768]{2,1,0:T(8,128)(2,1)}, bf16[3,128,768]{2,1,0:T(8,128)(2,1)S(1)}, u32[]{:S(2)}) copy-start(bf16[3,128,768]{2,1,0:T(8,128)(2,1)S(1)} %join_weights.1.refs_0_) | copy-start | bytes 1769476
  17.4 6.6 %collective-permute-start = (bf16[3,128,768]{2,1,0:T(8,128)(2,1)S(1)}, bf16[3,128,768]{2,1,0:T(8,128)(2,1)S(1)}, u32[]{:S(2)}, u32[]{:S(2)}) collective-permute-start(bf16[3,128,768]{2,1,0:T(8,128)(2,1)S(1)} %join_weights.1.refs_0_), channel_id=1, source_target_pairs={{0,32},{32,0},{64,96},{96,64},{128,160},{160,128},{192,224},{224,1... | collective-permute-start | bytes 1769480 | tf_op jit(solution)/shard_map/ppermute | solution.py:224
  19.3 12.1 %collective-permute-start.1 = (bf16[3,128,768]{2,1,0:T(8,128)(2,1)S(1)}, bf16[3,128,768]{2,1,0:T(8,128)(2,1)S(1)}, u32[]{:S(2)}, u32[]{:S(2)}) collective-permute-start(bf16[3,128,768]{2,1,0:T(8,128)(2,1)S(1)} %join_weights.1.refs_0_), channel_id=1, source_target_pairs={{0,64},{32,480},{64,128},{96,32},{128,192},{160,96},{192,256},{224... | collective-permute-start | bytes 1769480 | tf_op jit(solution)/shard_map/ppermute | solution.py:227
  24.0 56.5 %copy-start.5 = (bf16[3,128,768]{2,1,0:T(8,128)(2,1)}, bf16[3,128,768]{2,1,0:T(8,128)(2,1)S(1)}, u32[]{:S(2)}) copy-start(bf16[3,128,768]{2,1,0:T(8,128)(2,1)S(1)} %collective-permute-done.refs_1_) | copy-start | bytes 1769476
  24.1 13.7 %collective-permute-start.2 = (bf16[3,128,768]{2,1,0:T(8,128)(2,1)S(1)}, bf16[3,128,768]{2,1,0:T(8,128)(2,1)S(1)}, u32[]{:S(2)}, u32[]{:S(2)}) collective-permute-start(bf16[3,128,768]{2,1,0:T(8,128)(2,1)S(1)} %collective-permute-done.refs_1_), channel_id=1, source_target_pairs={{0,64},{32,480},{64,128},{96,32},{128,192},{160,96},{192,256},{224... | collective-permute-start | bytes 1769480 | tf_op jit(solution)/shard_map/ppermute | solution.py:227
  31.4 49.1 %copy-start.6 = (bf16[3,128,768]{2,1,0:T(8,128)(2,1)}, bf16[3,128,768]{2,1,0:T(8,128)(2,1)S(1)}, u32[]{:S(2)}) copy-start(bf16[3,128,768]{2,1,0:T(8,128)(2,1)S(1)} %collective-permute-done.1.refs_2_) | copy-start | bytes 1769476
  31.4 13.0 %collective-permute-start.5 = (bf16[3,128,768]{2,1,0:T(8,128)(2,1)S(1)}, bf16[3,128,768]{2,1,0:T(8,128)(2,1)S(1)}, u32[]{:S(2)}, u32[]{:S(2)}) collective-permute-start(bf16[3,128,768]{2,1,0:T(8,128)(2,1)S(1)} %collective-permute-done.1.refs_2_), channel_id=1, source_target_pairs={{0,64},{32,480},{64,128},{96,32},{128,192},{160,96},{192,256},{224... | collective-permute-start | bytes 1769480 | tf_op jit(solution)/shard_map/ppermute | solution.py:227
  37.7 42.8 %copy-start.7 = (bf16[3,128,768]{2,1,0:T(8,128)(2,1)}, bf16[3,128,768]{2,1,0:T(8,128)(2,1)S(1)}, u32[]{:S(2)}) copy-start(bf16[3,128,768]{2,1,0:T(8,128)(2,1)S(1)} %collective-permute-done.2.refs_3_) | copy-start | bytes 1769476
  37.7 16.6 %collective-permute-start.6 = (bf16[3,128,768]{2,1,0:T(8,128)(2,1)S(1)}, bf16[3,128,768]{2,1,0:T(8,128)(2,1)S(1)}, u32[]{:S(2)}, u32[]{:S(2)}) collective-permute-start(bf16[3,128,768]{2,1,0:T(8,128)(2,1)S(1)} %collective-permute-done.2.refs_3_), channel_id=1, source_target_pairs={{0,64},{32,480},{64,128},{96,32},{128,192},{160,96},{192,256},{224... | collective-permute-start | bytes 1769480 | tf_op jit(solution)/shard_map/ppermute | solution.py:227
  44.4 36.2 %copy-start.8 = (bf16[3,128,768]{2,1,0:T(8,128)(2,1)}, bf16[3,128,768]{2,1,0:T(8,128)(2,1)S(1)}, u32[]{:S(2)}) copy-start(bf16[3,128,768]{2,1,0:T(8,128)(2,1)S(1)} %collective-permute-done.5.refs_6_) | copy-start | bytes 1769476
  44.4 13.0 %collective-permute-start.9 = (bf16[3,128,768]{2,1,0:T(8,128)(2,1)S(1)}, bf16[3,128,768]{2,1,0:T(8,128)(2,1)S(1)}, u32[]{:S(2)}, u32[]{:S(2)}) collective-permute-start(bf16[3,128,768]{2,1,0:T(8,128)(2,1)S(1)} %collective-permute-done.5.refs_6_), channel_id=1, source_target_pairs={{0,64},{32,480},{64,128},{96,32},{128,192},{160,96},{192,256},{224... | collective-permute-start | bytes 1769480 | tf_op jit(solution)/shard_map/ppermute | solution.py:227
  50.0 14.9 %collective-permute-start.3 = (bf16[3,128,768]{2,1,0:T(8,128)(2,1)S(1)}, bf16[3,128,768]{2,1,0:T(8,128)(2,1)S(1)}, u32[]{:S(2)}, u32[]{:S(2)}) collective-permute-start(bf16[3,128,768]{2,1,0:T(8,128)(2,1)S(1)} %collective-permute-done.1.refs_2_), channel_id=1, source_target_pairs={{0,32},{32,0},{64,96},{96,64},{128,160},{160,128},{192,224},{224,1... | collective-permute-start | bytes 1769480 | tf_op jit(solution)/shard_map/ppermute | solution.py:228
  51.9 15.4 %collective-permute-start.4 = (bf16[3,128,768]{2,1,0:T(8,128)(2,1)S(1)}, bf16[3,128,768]{2,1,0:T(8,128)(2,1)S(1)}, u32[]{:S(2)}, u32[]{:S(2)}) collective-permute-start(bf16[3,128,768]{2,1,0:T(8,128)(2,1)S(1)} %collective-permute-done.2.refs_3_), channel_id=1, source_target_pairs={{0,32},{32,0},{64,96},{96,64},{128,160},{160,128},{192,224},{224,1... | collective-permute-start | bytes 1769480 | tf_op jit(solution)/shard_map/ppermute | solution.py:228
  54.3 26.2 %copy-start.9 = (bf16[3,128,768]{2,1,0:T(8,128)(2,1)}, bf16[3,128,768]{2,1,0:T(8,128)(2,1)S(1)}, u32[]{:S(2)}) copy-start(bf16[3,128,768]{2,1,0:T(8,128)(2,1)S(1)} %collective-permute-done.6.refs_7_) | copy-start | bytes 1769476
  54.4 14.9 %collective-permute-start.10 = (bf16[3,128,768]{2,1,0:T(8,128)(2,1)S(1)}, bf16[3,128,768]{2,1,0:T(8,128)(2,1)S(1)}, u32[]{:S(2)}, u32[]{:S(2)}) collective-permute-start(bf16[3,128,768]{2,1,0:T(8,128)(2,1)S(1)} %collective-permute-done.6.refs_7_), channel_id=1, source_target_pairs={{0,64},{32,480},{64,128},{96,32},{128,192},{160,96},{192,256},{224... | collective-permute-start | bytes 1769480 | tf_op jit(solution)/shard_map/ppermute | solution.py:227
  57.4 17.5 %copy-start.10 = (bf16[3,128,768]{2,1,0:T(8,128)(2,1)}, bf16[3,128,768]{2,1,0:T(8,128)(2,1)S(1)}, u32[]{:S(2)}) copy-start(bf16[3,128,768]{2,1,0:T(8,128)(2,1)S(1)} %collective-permute-done.9.refs_10_) | copy-start | bytes 1769476
  57.4 15.1 %collective-permute-start.13 = (bf16[3,128,768]{2,1,0:T(8,128)(2,1)S(1)}, bf16[3,128,768]{2,1,0:T(8,128)(2,1)S(1)}, u32[]{:S(2)}, u32[]{:S(2)}) collective-permute-start(bf16[3,128,768]{2,1,0:T(8,128)(2,1)S(1)} %collective-permute-done.9.refs_10_), channel_id=1, source_target_pairs={{0,64},{32,480},{64,128},{96,32},{128,192},{160,96},{192,256},{224... | collective-permute-start | bytes 1769480 | tf_op jit(solution)/shard_map/ppermute | solution.py:229
  63.0 11.9 %collective-permute-start.7 = (bf16[3,128,768]{2,1,0:T(8,128)(2,1)S(1)}, bf16[3,128,768]{2,1,0:T(8,128)(2,1)S(1)}, u32[]{:S(2)}, u32[]{:S(2)}) collective-permute-start(bf16[3,128,768]{2,1,0:T(8,128)(2,1)S(1)} %collective-permute-done.5.refs_6_), channel_id=1, source_target_pairs={{0,32},{32,0},{64,96},{96,64},{128,160},{160,128},{192,224},{224,1... | collective-permute-start | bytes 1769480 | tf_op jit(solution)/shard_map/ppermute | solution.py:228
  64.9 10.0 %copy-start.11 = (bf16[3,128,768]{2,1,0:T(8,128)(2,1)}, bf16[3,128,768]{2,1,0:T(8,128)(2,1)S(1)}, u32[]{:S(2)}) copy-start(bf16[3,128,768]{2,1,0:T(8,128)(2,1)S(1)} %collective-permute-done.3.refs_4_) | copy-start | bytes 1769476
  64.9 9.9 %collective-permute-start.8 = (bf16[3,128,768]{2,1,0:T(8,128)(2,1)S(1)}, bf16[3,128,768]{2,1,0:T(8,128)(2,1)S(1)}, u32[]{:S(2)}, u32[]{:S(2)}) collective-permute-start(bf16[3,128,768]{2,1,0:T(8,128)(2,1)S(1)} %collective-permute-done.6.refs_7_), channel_id=1, source_target_pairs={{0,32},{32,0},{64,96},{96,64},{128,160},{160,128},{192,224},{224,1... | collective-permute-start | bytes 1769480 | tf_op jit(solution)/shard_map/ppermute | solution.py:228
  67.3 7.6 %copy-start.12 = (bf16[3,128,768]{2,1,0:T(8,128)(2,1)}, bf16[3,128,768]{2,1,0:T(8,128)(2,1)S(1)}, u32[]{:S(2)}) copy-start(bf16[3,128,768]{2,1,0:T(8,128)(2,1)S(1)} %collective-permute-done.4.refs_5_) | copy-start | bytes 1769476
  67.4 7.5 %collective-permute-start.11 = (bf16[3,128,768]{2,1,0:T(8,128)(2,1)S(1)}, bf16[3,128,768]{2,1,0:T(8,128)(2,1)S(1)}, u32[]{:S(2)}, u32[]{:S(2)}) collective-permute-start(bf16[3,128,768]{2,1,0:T(8,128)(2,1)S(1)} %collective-permute-done.9.refs_10_), channel_id=1, source_target_pairs={{0,32},{32,0},{64,96},{96,64},{128,160},{160,128},{192,224},{224,1... | collective-permute-start | bytes 1769480 | tf_op jit(solution)/shard_map/ppermute | solution.py:228
  69.3 5.6 %copy-start.13 = (bf16[3,128,768]{2,1,0:T(8,128)(2,1)}, bf16[3,128,768]{2,1,0:T(8,128)(2,1)S(1)}, u32[]{:S(2)}) copy-start(bf16[3,128,768]{2,1,0:T(8,128)(2,1)S(1)} %collective-permute-done.10.refs_11_) | copy-start | bytes 1769476
  69.3 5.6 %collective-permute-start.12 = (bf16[3,128,768]{2,1,0:T(8,128)(2,1)S(1)}, bf16[3,128,768]{2,1,0:T(8,128)(2,1)S(1)}, u32[]{:S(2)}, u32[]{:S(2)}) collective-permute-start(bf16[3,128,768]{2,1,0:T(8,128)(2,1)S(1)} %collective-permute-done.10.refs_11_), channel_id=1, source_target_pairs={{0,32},{32,0},{64,96},{96,64},{128,160},{160,128},{192,224},{224,1... | collective-permute-start | bytes 1769480 | tf_op jit(solution)/shard_map/ppermute | solution.py:228
  72.5 2.5 %copy-start.14 = (bf16[3,128,768]{2,1,0:T(8,128)(2,1)}, bf16[3,128,768]{2,1,0:T(8,128)(2,1)S(1)}, u32[]{:S(2)}) copy-start(bf16[3,128,768]{2,1,0:T(8,128)(2,1)S(1)} %collective-permute-done.13.refs_14_) | copy-start | bytes 1769476
  72.5 4.5 %collective-permute-start.14 = (bf16[3,128,768]{2,1,0:T(8,128)(2,1)S(1)}, bf16[3,128,768]{2,1,0:T(8,128)(2,1)}, u32[]{:S(2)}, u32[]{:S(2)}) collective-permute-start(bf16[3,128,768]{2,1,0:T(8,128)(2,1)S(1)} %collective-permute-done.13.refs_14_), channel_id=1, source_target_pairs={{0,32},{32,0},{64,96},{96,64},{128,160},{160,128},{192,224},{224,1... | collective-permute-start | bytes 1769480 | tf_op jit(solution)/shard_map/ppermute | solution.py:230
  74.8 0.8 copy-start.15
  74.9 1.0 copy-start.16
  74.9 1.2 copy-start.17
  76.1 0.8 copy-start.18
  91.6 6.2 %copy-start.3 = (s32[128,2]{0,1:T(2,128)S(1)}, s32[128,2]{0,1:T(2,128)}, u32[]{:S(2)}) copy-start(s32[128,2]{0,1:T(2,128)} %param.8) | copy-start | bytes 3076
  91.7 6.3 %copy-start.4 = (f32[128,2]{0,1:T(2,128)S(1)}, f32[128,2]{0,1:T(2,128)}, u32[]{:S(2)}) copy-start(f32[128,2]{0,1:T(2,128)} %param.9) | copy-start | bytes 3076
  91.7 41.7 %all-to-all-start.1 = ((bf16[32,8,2688]{2,1,0:T(8,128)(2,1)}), bf16[32,8,2688]{2,1,0:T(8,128)(2,1)S(1)}, u32[]{:S(2)}, u32[]{:S(2)}) async-start(bf16[32,8,2688]{2,1,0:T(8,128)(2,1)} %expert_rows.1), calls=%async_computation.1 | async-start | bytes 2752512 | tf_op jit(solution)/shard_map/all_to_all | solution.py:286
